TPU v7x, 128 devices: a whole 4x4x4 slice. The times are simulated.
128 devices in a mesh: section: 8 (over z_lo, x), fsdp: 16 (over y, z_hi, core).
Axes of the slice: x: 4, y: 4, z: 4 (z_hi: 2, z_lo: 2; z = z_hi * 2 + z_lo), core: 2. Of those that a mesh axis runs over, the one named last changes fastest.
Arguments:
- in_base: bfloat16 [8, 5, 768, 9216], P('section', None, 'fsdp'), may hold values from -5 to 5
- out_base: bfloat16 [8, 5, 768, 9216], P('section', None, 'fsdp'), may hold values from -5 to 5, as said below
- sample_ids: int32 [4], replicated, may hold values from 0 to 4, as said below
- send_exponent: int32 [8, 4, 768, 72], P('section', None, 'fsdp'), may hold values from -9 to -4
- grad_exponent: int32 [8, 4, 768, 72], P('section', None, 'fsdp'), may hold values from -9 to -4
- loss_grad: bfloat16 [4, 768, 9216], P(None, 'fsdp'), may hold values from -6 to 6
- down_weight: bfloat16 [8, 9216, 256], P('section', 'fsdp'), may hold values from -0.0625 to 0.0625
- up_weight: bfloat16 [8, 9216, 256], P('section', 'fsdp'), may hold values from -0.0625 to 0.0625
- norm_gain: bfloat16 [8, 9216], P('section', 'fsdp'), may hold values from 0.5 to 2
Outputs:
- section_out: bfloat16 [8, 4, 768, 9216], P('section', None, 'fsdp')
- input_grad: bfloat16 [8, 4, 768, 9216], P('section', None, 'fsdp')
- down_grad: float32 [8, 9216, 256], P('section', 'fsdp')
- up_grad: float32 [8, 9216, 256], P('section', 'fsdp')
- gain_grad: float32 [8, 9216], P('section', 'fsdp')
Inputs may be any that keep to these rules, and one draw needn't show every extreme that they name: `sample_ids`: 4 different samples; 0 and 4 are among them. out_base[s] equals in_base[s + 1] for s < 7.
All inputs are finite; a program needn't handle non-finite values.
Results may differ from a plain program's by a relative error of at most 0.025.
Values may be sent and summed in bfloat16 or wider, within the bound.
No kernel may reach another device: no remote copies, remote signals or barrier semaphores. Data moves between devices by JAX's collectives and lax.ppermute only.
A program may use at most 128 MiB of HBM per device.

v0:
```python
import math

import jax
import jax.numpy as jnp
from jax import lax
from jax.sharding import PartitionSpec as P

SQRT_HALF = 0.7071067811865476
INV_ROOT_TAU = 0.3989422804014327
clip_level = 448.0
norm_epsilon = 1e-05
lowest_exponent = -9
highest_exponent = -3


def shifted(shard, axis, by):
    count = lax.axis_size(axis)
    pairs = [(i, i + by) for i in range(count) if 0 <= i + by < count]
    return lax.ppermute(shard, axis, pairs)


def gelu_value(values):
    return values * 0.5 * (1.0 + lax.erf(values * SQRT_HALF))


def gelu_slope(values):
    return 0.5 * (1.0 + lax.erf(values * SQRT_HALF)) + values * INV_ROOT_TAU * jnp.exp(
        -0.5 * values * values
    )


def block_powers(exponent):
    upward = jnp.zeros(exponent.shape, jnp.float32)
    downward = jnp.zeros(exponent.shape, jnp.float32)
    for exponent_value in range(lowest_exponent, highest_exponent):
        matches = exponent == exponent_value
        upward = jnp.where(matches, jnp.float32(2.0**exponent_value), upward)
        downward = jnp.where(matches, jnp.float32(2.0 ** (-exponent_value)), downward)
    return (upward, downward)


def encode(values, exponent):
    upward, downward = block_powers(exponent)
    full_shape = values.shape
    layer_groups = values.reshape(full_shape[:-1] + (full_shape[-1] // 128, 128))
    scaled = jnp.clip(layer_groups * downward[..., None], -clip_level, clip_level).astype(
        jnp.bfloat16
    )
    scaled = lax.optimization_barrier(scaled)
    return (scaled.astype(jnp.float32) * upward[..., None]).astype(jnp.bfloat16).reshape(full_shape)


def normalize(layer_in):
    values = layer_in.astype(jnp.float32)
    centred = values - jnp.mean(values, axis=-1, keepdims=True)
    inv_scale = lax.rsqrt(jnp.mean(centred * centred, axis=-1, keepdims=True) + norm_epsilon)
    return (centred * inv_scale, inv_scale)


def write_slot(piled_arrays, fresh_item, index, active):
    former = lax.dynamic_index_in_dim(piled_arrays, index, 0, False)
    return lax.dynamic_update_index_in_dim(
        piled_arrays, jnp.where(active, fresh_item, former), index, 0
    )


def shards(
    in_base,
    out_base,
    sample_ids,
    send_exponent,
    grad_exponent,
    loss_grad,
    down_weight,
    up_weight,
    norm_gain,
):
    sections = lax.axis_size("section")
    groups = lax.axis_size("fsdp")
    position = lax.axis_index("section")
    micro = sample_ids.shape[0]
    tokens = in_base.shape[2]
    width = in_base.shape[3]
    neck = down_weight.shape[2]
    down_full, up_full, gain_full = (
        lax.all_gather(down_weight, "fsdp", axis=1, tiled=True),
        lax.all_gather(up_weight, "fsdp", axis=1, tiled=True),
        lax.all_gather(norm_gain, "fsdp", axis=1, tiled=True),
    )
    down_mat = down_full[0]
    up_mat = up_full[0]
    gain_vector = gain_full[0].astype(jnp.float32)
    base_in = in_base[0]
    base_out = out_base[0]
    send_table = send_exponent[0]
    back_table = grad_exponent[0]
    is_last = position == sections - 1
    contract_last = (((1,), (1,)), ((), ()))
    contract_first = (((0,), (0,)), ((), ()))

    def forward_step(index, incoming):
        sample = sample_ids[index]
        stored_in = lax.dynamic_index_in_dim(base_in, sample, 0, False)
        layer_in = (stored_in.astype(jnp.float32) + incoming.astype(jnp.float32)).astype(
            jnp.bfloat16
        )
        centred, inv_scale = normalize(layer_in)
        normed = (centred * gain_vector).astype(jnp.bfloat16)
        bottleneck = jnp.dot(normed, down_mat, preferred_element_type=jnp.float32)
        activated = gelu_value(bottleneck).astype(jnp.bfloat16)
        branch = lax.dot_general(
            activated, up_mat, contract_last, preferred_element_type=jnp.float32
        )
        section_val = (layer_in.astype(jnp.float32) + branch).astype(jnp.bfloat16)
        stored_out = lax.dynamic_index_in_dim(base_out, sample, 0, False)
        delivered = encode(
            section_val.astype(jnp.float32) - stored_out.astype(jnp.float32),
            lax.dynamic_index_in_dim(send_table, index, 0, False),
        )
        return ((centred, inv_scale, normed, bottleneck, activated, section_val), delivered)

    def run_forward(index, incoming):
        return forward_step(index, incoming)

    def forward_tick(tick, carried):
        incoming, saved = carried
        index = tick - position
        active = (index >= 0) & (index < micro)
        index = jnp.clip(index, 0, micro - 1)
        fresh, delivered = run_forward(index, incoming)
        saved = tuple(
            (
                write_slot(piled_arrays, fresh_item, index, active)
                for piled_arrays, fresh_item in zip(saved, fresh)
            )
        )
        incoming = shifted(delivered, "section", 1)
        return (incoming, saved)

    def backward_step(index, incoming, saved):
        centred, inv_scale, normed, bottleneck, activated = [
            lax.dynamic_index_in_dim(piled_arrays, index, 0, False) for piled_arrays in saved[:5]
        ]
        out_cot = jnp.where(is_last, lax.dynamic_index_in_dim(loss_grad, index, 0, False), incoming)
        act_cot = jnp.dot(out_cot, up_mat, preferred_element_type=jnp.float32)
        neck_cot = (act_cot * gelu_slope(bottleneck)).astype(jnp.bfloat16)
        norm_cot = lax.dot_general(
            neck_cot, down_mat, contract_last, preferred_element_type=jnp.float32
        )
        scaled_cot = norm_cot * gain_vector
        in_cot = out_cot.astype(jnp.float32) + inv_scale * (
            scaled_cot
            - jnp.mean(scaled_cot, axis=-1, keepdims=True)
            - centred * jnp.mean(scaled_cot * centred, axis=-1, keepdims=True)
        )
        delivered = encode(in_cot, lax.dynamic_index_in_dim(back_table, index, 0, False))
        gain_addend = jnp.sum(norm_cot * centred, axis=0)
        return ((in_cot.astype(jnp.bfloat16), out_cot, neck_cot, gain_addend), delivered)

    def run_backward(index, incoming, saved):
        return backward_step(index, incoming, saved)

    def backward_tick(tick, carried, saved):
        incoming, cots = carried
        index = tick - (sections - 1 - position)
        active = (index >= 0) & (index < micro)
        index = jnp.clip(index, 0, micro - 1)
        fresh, delivered = run_backward(index, incoming, saved)
        cots = tuple(
            (
                write_slot(piled_arrays, fresh_item, index, active)
                for piled_arrays, fresh_item in zip(cots, fresh)
            )
        )
        incoming = shifted(delivered, "section", -1)
        return (incoming, cots)

    zero_rows = jnp.zeros((tokens, width), jnp.bfloat16)
    saved_start = (
        jnp.zeros((micro, tokens, width), jnp.float32),
        jnp.zeros((micro, tokens, 1), jnp.float32),
        jnp.zeros((micro, tokens, width), jnp.bfloat16),
        jnp.zeros((micro, tokens, neck), jnp.float32),
        jnp.zeros((micro, tokens, neck), jnp.bfloat16),
        jnp.zeros((micro, tokens, width), jnp.bfloat16),
    )
    cots_start = (
        jnp.zeros((micro, tokens, width), jnp.bfloat16),
        jnp.zeros((micro, tokens, width), jnp.bfloat16),
        jnp.zeros((micro, tokens, neck), jnp.bfloat16),
        jnp.zeros((micro, width), jnp.float32),
    )
    forward_state = lax.fori_loop(0, micro + sections - 1, forward_tick, (zero_rows, saved_start))

    def backward_only(tick, carried):
        return backward_tick(tick, carried, forward_state[1])

    backward_state = lax.fori_loop(0, micro + sections - 1, backward_only, (zero_rows, cots_start))
    saved = forward_state[1]
    cots = backward_state[1]
    factor = 1.0 / math.sqrt(micro * tokens * groups)
    gain_addend = jnp.sum(cots[3], axis=0) * factor
    normed_all = saved[2].reshape(micro * tokens, width)
    activated_all = saved[4].reshape(micro * tokens, neck)
    out_all = cots[1].reshape(micro * tokens, width)
    neck_all = cots[2].reshape(micro * tokens, neck)
    down_term = (
        lax.dot_general(normed_all, neck_all, contract_first, preferred_element_type=jnp.float32)
        * factor
    )
    up_term = (
        lax.dot_general(out_all, activated_all, contract_first, preferred_element_type=jnp.float32)
        * factor
    )
    down_part, up_part, gain_part = (
        lax.psum_scatter(
            down_term.astype(jnp.bfloat16), "fsdp", scatter_dimension=0, tiled=True
        ).astype(jnp.float32),
        lax.psum_scatter(
            up_term.astype(jnp.bfloat16), "fsdp", scatter_dimension=0, tiled=True
        ).astype(jnp.float32),
        lax.psum_scatter(
            gain_addend.astype(jnp.bfloat16), "fsdp", scatter_dimension=0, tiled=True
        ).astype(jnp.float32),
    )
    return (saved[5][None], cots[0][None], down_part[None], up_part[None], gain_part[None])


def solution(mesh):
    in_specs = (
        P("section", None, "fsdp", None),
        P("section", None, "fsdp", None),
        P(),
        P("section", None, "fsdp", None),
        P("section", None, "fsdp", None),
        P(None, "fsdp", None),
        P("section", "fsdp", None),
        P("section", "fsdp", None),
        P("section", "fsdp"),
    )
    out_specs = (
        P("section", None, "fsdp", None),
        P("section", None, "fsdp", None),
        P("section", "fsdp", None),
        P("section", "fsdp", None),
        P("section", "fsdp"),
    )
    return jax.shard_map(shards, mesh=mesh, in_specs=in_specs, out_specs=out_specs, check_vma=False)
```

profile of v0, /device:TPU:0, one launch (start us, length us, event | category | flops | bytes accessed | tf_op | source)
XLA Modules:
  0.0 1077.2 jit_solution(3485013684466422333)
XLA Ops:
  11.6 70.9 %all-reduce = bf16[9216]{0:T(1024)(128)(2,1)S(1)} all-reduce(bf16[9216]{0:T(1024)(128)(2,1)S(1)} %dynamic-update-slice), channel_id=1, replica_groups=mesh['section'=8,'fsdp'=16] {'fsdp'}, use_global_device_ids=true, to_apply=%add | all-reduce | flops 9216 | bytes 36864
  82.6 47.6 %all-gather.5.cloned.1.call-done = bf16[1,9216,256]{2,1,0:T(8,128)(2,1)} async-done(((bf16[1,576,256]{2,1,0:T(8,128)(2,1)}), bf16[1,9216,256]{2,1,0:T(8,128)(2,1)}) %all-gather.5.cloned.1.call-update) | async-done | bytes 4718608 | tf_op jit(solution)/shard_map/all_gather | solution.py:87
  130.2 3.7 broadcast_in_dim.265
  138.3 393.1 %while.48 = (s32[]{:T(128)}, bf16[48,9216]{1,0:T(8,128)(2,1)S(1)}, f32[4,48,9216]{2,1,0:T(8,128)}, f32[4,48,1]{1,2,0:T(1,128)S(1)}, bf16[4,48,9216]{2,1,0:T(8,12...) while((s32[]{:T(128)}, bf16[48,9216]{1,0:T(8,128)(2,1)S(1)}, ...), condition=%wide.region_3.4_spmd, body=%wide.region_0.3_spmd.sunk | while | flops 470004672 | bytes 67871720 | solution.py:193
  144.2 3.5 bitcast_dynamic-update-slice_fusion.14
  154.0 3.4 collective-permute-start
  163.2 13.5 %collective-permute-done = bf16[48,9216]{1,0:T(8,128)(2,1)S(1)} collective-permute-done((bf16[48,9216]{1,0:T(8,128)(2,1)S(1)}, bf16[48,9216]{1,0:T(8,128)(2,1)S(1)}, u32[]{:S(2)}, u32[]{:S(2)}) %collective-permute-start) | collective-permute-done | bytes 884768 | tf_op jit(solution)/shard_map/while/body/eval_jaxpr/ppermute | solution.py:19
  182.5 3.5 bitcast_dynamic-update-slice_fusion.14
  192.4 4.4 collective-permute-start
  202.6 12.7 %collective-permute-done = bf16[48,9216]{1,0:T(8,128)(2,1)S(1)} collective-permute-done((bf16[48,9216]{1,0:T(8,128)(2,1)S(1)}, bf16[48,9216]{1,0:T(8,128)(2,1)S(1)}, u32[]{:S(2)}, u32[]{:S(2)}) %collective-permute-start) | collective-permute-done | bytes 884768 | tf_op jit(solution)/shard_map/while/body/eval_jaxpr/ppermute | solution.py:19
  221.0 3.5 bitcast_dynamic-update-slice_fusion.14
  230.9 4.4 collective-permute-start
  241.1 11.7 %collective-permute-done = bf16[48,9216]{1,0:T(8,128)(2,1)S(1)} collective-permute-done((bf16[48,9216]{1,0:T(8,128)(2,1)S(1)}, bf16[48,9216]{1,0:T(8,128)(2,1)S(1)}, u32[]{:S(2)}, u32[]{:S(2)}) %collective-permute-start) | collective-permute-done | bytes 884768 | tf_op jit(solution)/shard_map/while/body/eval_jaxpr/ppermute | solution.py:19
  258.6 3.5 bitcast_dynamic-update-slice_fusion.14
  268.5 4.4 collective-permute-start
  278.8 10.8 %collective-permute-done = bf16[48,9216]{1,0:T(8,128)(2,1)S(1)} collective-permute-done((bf16[48,9216]{1,0:T(8,128)(2,1)S(1)}, bf16[48,9216]{1,0:T(8,128)(2,1)S(1)}, u32[]{:S(2)}, u32[]{:S(2)}) %collective-permute-start) | collective-permute-done | bytes 884768 | tf_op jit(solution)/shard_map/while/body/eval_jaxpr/ppermute | solution.py:19
  295.3 3.5 bitcast_dynamic-update-slice_fusion.14
  305.2 4.4 collective-permute-start
  315.5 9.9 collective-permute-done
  331.1 3.5 bitcast_dynamic-update-slice_fusion.14
  341.0 4.5 collective-permute-start
  351.3 8.9 collective-permute-done
  366.0 3.5 bitcast_dynamic-update-slice_fusion.14
  375.8 6.6 collective-permute-start
  388.2 8.0 collective-permute-done
  402.0 3.5 bitcast_dynamic-update-slice_fusion.14
  411.9 6.5 collective-permute-start
  424.3 7.1 collective-permute-done
  437.1 3.5 bitcast_dynamic-update-slice_fusion.14
  447.0 6.5 collective-permute-start
  459.4 6.1 collective-permute-done
  471.3 3.5 bitcast_dynamic-update-slice_fusion.14
  481.2 6.6 collective-permute-start
  493.6 5.2 collective-permute-done
  504.6 3.5 bitcast_dynamic-update-slice_fusion.14
  514.4 6.5 collective-permute-start
  526.8 4.7 collective-permute-done
  535.9 351.0 %while.49 = (s32[]{:T(128)}, bf16[48,9216]{1,0:T(8,128)(2,1)S(1)}, bf16[4,48,9216]{2,1,0:T(8,128)(2,1)}, bf16[4,48,9216]{2,1,0:T(8,128)(2,1)}, bf16[4,48,256]{2,...) while((s32[]{:T(128)}, bf16[48,9216]{1,0:T(8,128)(2,1)S(1)}, ...), condition=%wide.region_8.9_spmd, body=%wide.region_4.8_spmd.sunk | while | flops 466453248 | bytes 62279160 | solution.py:198
  557.4 10.9 %collective-permute-done.1 = bf16[48,9216]{1,0:T(8,128)(2,1)S(1)} collective-permute-done((bf16[48,9216]{1,0:T(8,128)(2,1)S(1)}, bf16[48,9216]{1,0:T(8,128)(2,1)S(1)}, u32[]{:S(2)}, u32[]{:S(2)}) %collective-permute-start.1) | collective-permute-done | bytes 884768 | tf_op jit(solution)/shard_map/while/body/eval_jaxpr/ppermute | solution.py:19
  572.3 3.3 bitcast_dynamic-update-slice_fusion.19
  589.6 10.9 %collective-permute-done.1 = bf16[48,9216]{1,0:T(8,128)(2,1)S(1)} collective-permute-done((bf16[48,9216]{1,0:T(8,128)(2,1)S(1)}, bf16[48,9216]{1,0:T(8,128)(2,1)S(1)}, u32[]{:S(2)}, u32[]{:S(2)}) %collective-permute-start.1) | collective-permute-done | bytes 884768 | tf_op jit(solution)/shard_map/while/body/eval_jaxpr/ppermute | solution.py:19
  604.5 3.3 bitcast_dynamic-update-slice_fusion.19
  621.8 10.9 %collective-permute-done.1 = bf16[48,9216]{1,0:T(8,128)(2,1)S(1)} collective-permute-done((bf16[48,9216]{1,0:T(8,128)(2,1)S(1)}, bf16[48,9216]{1,0:T(8,128)(2,1)S(1)}, u32[]{:S(2)}, u32[]{:S(2)}) %collective-permute-start.1) | collective-permute-done | bytes 884768 | tf_op jit(solution)/shard_map/while/body/eval_jaxpr/ppermute | solution.py:19
  636.7 3.3 bitcast_dynamic-update-slice_fusion.19
  654.0 10.9 %collective-permute-done.1 = bf16[48,9216]{1,0:T(8,128)(2,1)S(1)} collective-permute-done((bf16[48,9216]{1,0:T(8,128)(2,1)S(1)}, bf16[48,9216]{1,0:T(8,128)(2,1)S(1)}, u32[]{:S(2)}, u32[]{:S(2)}) %collective-permute-start.1) | collective-permute-done | bytes 884768 | tf_op jit(solution)/shard_map/while/body/eval_jaxpr/ppermute | solution.py:19
  668.8 3.3 bitcast_dynamic-update-slice_fusion.19
  686.2 10.4 collective-permute-done.1
  700.6 3.3 bitcast_dynamic-update-slice_fusion.19
  717.9 10.4 collective-permute-done.1
  732.3 3.3 bitcast_dynamic-update-slice_fusion.19
  749.6 10.4 collective-permute-done.1
  764.0 3.3 bitcast_dynamic-update-slice_fusion.19
  781.4 10.4 collective-permute-done.1
  795.6 3.3 bitcast_dynamic-update-slice_fusion.19
  813.0 10.5 collective-permute-done.1
  827.4 3.3 bitcast_dynamic-update-slice_fusion.19
  844.8 10.5 collective-permute-done.1
  859.2 3.3 bitcast_dynamic-update-slice_fusion.19
  876.5 10.4 collective-permute-done.1
  887.0 5.6 fusion.34
  892.6 5.7 fusion.33
  899.1 65.3 %all-reduce.1 = bf16[9216]{0:T(1024)(128)(2,1)S(1)} all-reduce(bf16[9216]{0:T(1024)(128)(2,1)S(1)} %multiply_convert_fusion.4), channel_id=4, replica_groups=mesh['section'=8,'fsdp'=16] {'fsdp'}, use_global_device_ids=true, to_apply=%region_12.13.clone | all-reduce | flops 9216 | bytes 36864
  965.1 17.9 %reduce-scatter.5.cloned.1.call-done = bf16[576,256]{1,0:T(8,128)(2,1)} async-done(((bf16[9216,256]{1,0:T(8,128)(2,1)}), bf16[576,256]{1,0:T(8,128)(2,1)}) %reduce-scatter.5.cloned.1.call-update) | async-done | bytes 294928 | tf_op jit(solution)/shard_map/reduce_scatter | solution.py:219
  984.7 84.2 %reduce-scatter.3.cloned.1.call-done = bf16[576,256]{1,0:T(8,128)(2,1)} async-done(((bf16[9216,256]{1,0:T(8,128)(2,1)}), bf16[576,256]{1,0:T(8,128)(2,1)}) %reduce-scatter.3.cloned.1.call-update) | async-done | bytes 294928 | tf_op jit(solution)/shard_map/reduce_scatter | solution.py:216
  (551 shorter events, 392.4 us)
Async XLA Ops:
  7.2 75.4 %all-gather.3.cloned.1.call-start = ((), (), s32[]{:S(2)}) async-start(), calls=%async_computation.2 | async-start | bytes 5013504 | tf_op jit(solution)/shard_map/all_gather | solution.py:86
  7.9 122.3 %all-gather.5.cloned.1.call-start = ((), (), s32[]{:S(2)}) async-start(), calls=%async_computation.3 | async-start | bytes 5013504 | tf_op jit(solution)/shard_map/all_gather | solution.py:87
  8.6 974.3 %reduce-scatter.5.cloned.1.call-start = ((), (), s32[]{:S(2)}) async-start(), calls=%async_computation.5 | async-start | bytes 5013504 | tf_op jit(solution)/shard_map/reduce_scatter | solution.py:219
  136.0 2.3 copy-start.1
  144.2 3.8 copy-start
  154.0 22.7 %collective-permute-start = (bf16[48,9216]{1,0:T(8,128)(2,1)S(1)}, bf16[48,9216]{1,0:T(8,128)(2,1)S(1)}, u32[]{:S(2)}, u32[]{:S(2)}) collective-permute-start(bf16[48,9216]{1,0:T(8,128)(2,1)S(1)} %bitcast.256), channel_id=1, source_target_pairs={{0,16},{16,32},{32,48},{48,64},{64,80},{80,96},{96,112},{1,17},{17... | collective-permute-start | bytes 2654216 | tf_op jit(solution)/shard_map/while/body/eval_jaxpr/ppermute | solution.py:19
  182.5 3.8 copy-start
  192.4 22.9 %collective-permute-start = (bf16[48,9216]{1,0:T(8,128)(2,1)S(1)}, bf16[48,9216]{1,0:T(8,128)(2,1)S(1)}, u32[]{:S(2)}, u32[]{:S(2)}) collective-permute-start(bf16[48,9216]{1,0:T(8,128)(2,1)S(1)} %bitcast.256), channel_id=1, source_target_pairs={{0,16},{16,32},{32,48},{48,64},{64,80},{80,96},{96,112},{1,17},{17... | collective-permute-start | bytes 2654216 | tf_op jit(solution)/shard_map/while/body/eval_jaxpr/ppermute | solution.py:19
  221.0 3.8 copy-start
  230.9 22.0 %collective-permute-start = (bf16[48,9216]{1,0:T(8,128)(2,1)S(1)}, bf16[48,9216]{1,0:T(8,128)(2,1)S(1)}, u32[]{:S(2)}, u32[]{:S(2)}) collective-permute-start(bf16[48,9216]{1,0:T(8,128)(2,1)S(1)} %bitcast.256), channel_id=1, source_target_pairs={{0,16},{16,32},{32,48},{48,64},{64,80},{80,96},{96,112},{1,17},{17... | collective-permute-start | bytes 2654216 | tf_op jit(solution)/shard_map/while/body/eval_jaxpr/ppermute | solution.py:19
  258.6 3.8 copy-start
  268.5 21.1 %collective-permute-start = (bf16[48,9216]{1,0:T(8,128)(2,1)S(1)}, bf16[48,9216]{1,0:T(8,128)(2,1)S(1)}, u32[]{:S(2)}, u32[]{:S(2)}) collective-permute-start(bf16[48,9216]{1,0:T(8,128)(2,1)S(1)} %bitcast.256), channel_id=1, source_target_pairs={{0,16},{16,32},{32,48},{48,64},{64,80},{80,96},{96,112},{1,17},{17... | collective-permute-start | bytes 2654216 | tf_op jit(solution)/shard_map/while/body/eval_jaxpr/ppermute | solution.py:19
  295.3 3.8 copy-start
  305.2 20.1 %collective-permute-start = (bf16[48,9216]{1,0:T(8,128)(2,1)S(1)}, bf16[48,9216]{1,0:T(8,128)(2,1)S(1)}, u32[]{:S(2)}, u32[]{:S(2)}) collective-permute-start(bf16[48,9216]{1,0:T(8,128)(2,1)S(1)} %bitcast.256), channel_id=1, source_target_pairs={{0,16},{16,32},{32,48},{48,64},{64,80},{80,96},{96,112},{1,17},{17... | collective-permute-start | bytes 2654216 | tf_op jit(solution)/shard_map/while/body/eval_jaxpr/ppermute | solution.py:19
  331.1 3.8 copy-start
  341.0 19.2 %collective-permute-start = (bf16[48,9216]{1,0:T(8,128)(2,1)S(1)}, bf16[48,9216]{1,0:T(8,128)(2,1)S(1)}, u32[]{:S(2)}, u32[]{:S(2)}) collective-permute-start(bf16[48,9216]{1,0:T(8,128)(2,1)S(1)} %bitcast.256), channel_id=1, source_target_pairs={{0,16},{16,32},{32,48},{48,64},{64,80},{80,96},{96,112},{1,17},{17... | collective-permute-start | bytes 2654216 | tf_op jit(solution)/shard_map/while/body/eval_jaxpr/ppermute | solution.py:19
  366.0 3.8 copy-start
  375.8 20.4 %collective-permute-start = (bf16[48,9216]{1,0:T(8,128)(2,1)S(1)}, bf16[48,9216]{1,0:T(8,128)(2,1)S(1)}, u32[]{:S(2)}, u32[]{:S(2)}) collective-permute-start(bf16[48,9216]{1,0:T(8,128)(2,1)S(1)} %bitcast.256), channel_id=1, source_target_pairs={{0,16},{16,32},{32,48},{48,64},{64,80},{80,96},{96,112},{1,17},{17... | collective-permute-start | bytes 2654216 | tf_op jit(solution)/shard_map/while/body/eval_jaxpr/ppermute | solution.py:19
  402.0 3.8 copy-start
  411.9 19.5 %collective-permute-start = (bf16[48,9216]{1,0:T(8,128)(2,1)S(1)}, bf16[48,9216]{1,0:T(8,128)(2,1)S(1)}, u32[]{:S(2)}, u32[]{:S(2)}) collective-permute-start(bf16[48,9216]{1,0:T(8,128)(2,1)S(1)} %bitcast.256), channel_id=1, source_target_pairs={{0,16},{16,32},{32,48},{48,64},{64,80},{80,96},{96,112},{1,17},{17... | collective-permute-start | bytes 2654216 | tf_op jit(solution)/shard_map/while/body/eval_jaxpr/ppermute | solution.py:19
  437.1 3.8 copy-start
  447.0 18.5 %collective-permute-start = (bf16[48,9216]{1,0:T(8,128)(2,1)S(1)}, bf16[48,9216]{1,0:T(8,128)(2,1)S(1)}, u32[]{:S(2)}, u32[]{:S(2)}) collective-permute-start(bf16[48,9216]{1,0:T(8,128)(2,1)S(1)} %bitcast.256), channel_id=1, source_target_pairs={{0,16},{16,32},{32,48},{48,64},{64,80},{80,96},{96,112},{1,17},{17... | collective-permute-start | bytes 2654216 | tf_op jit(solution)/shard_map/while/body/eval_jaxpr/ppermute | solution.py:19
  471.3 3.8 copy-start
  481.2 17.6 %collective-permute-start = (bf16[48,9216]{1,0:T(8,128)(2,1)S(1)}, bf16[48,9216]{1,0:T(8,128)(2,1)S(1)}, u32[]{:S(2)}, u32[]{:S(2)}) collective-permute-start(bf16[48,9216]{1,0:T(8,128)(2,1)S(1)} %bitcast.256), channel_id=1, source_target_pairs={{0,16},{16,32},{32,48},{48,64},{64,80},{80,96},{96,112},{1,17},{17... | collective-permute-start | bytes 2654216 | tf_op jit(solution)/shard_map/while/body/eval_jaxpr/ppermute | solution.py:19
  504.6 3.8 copy-start
  514.4 17.0 %collective-permute-start = (bf16[48,9216]{1,0:T(8,128)(2,1)S(1)}, bf16[48,9216]{1,0:T(8,128)(2,1)S(1)}, u32[]{:S(2)}, u32[]{:S(2)}) collective-permute-start(bf16[48,9216]{1,0:T(8,128)(2,1)S(1)} %bitcast.256), channel_id=1, source_target_pairs={{0,16},{16,32},{32,48},{48,64},{64,80},{80,96},{96,112},{1,17},{17... | collective-permute-start | bytes 2654216 | tf_op jit(solution)/shard_map/while/body/eval_jaxpr/ppermute | solution.py:19
  536.1 7.2 slice-start
  537.5 5.9 slice-start.1
  550.8 17.5 %collective-permute-start.1 = (bf16[48,9216]{1,0:T(8,128)(2,1)S(1)}, bf16[48,9216]{1,0:T(8,128)(2,1)S(1)}, u32[]{:S(2)}, u32[]{:S(2)}) collective-permute-start(bf16[48,9216]{1,0:T(8,128)(2,1)S(1)} %bitcast.257), channel_id=1, source_target_pairs={{16,0},{32,16},{48,32},{64,48},{80,64},{96,80},{112,96},{17,1},{33... | collective-permute-start | bytes 2654216 | tf_op jit(solution)/shard_map/while/body/eval_jaxpr/ppermute | solution.py:19
  568.3 7.2 slice-start
  569.7 5.9 slice-start.1
  583.0 17.5 %collective-permute-start.1 = (bf16[48,9216]{1,0:T(8,128)(2,1)S(1)}, bf16[48,9216]{1,0:T(8,128)(2,1)S(1)}, u32[]{:S(2)}, u32[]{:S(2)}) collective-permute-start(bf16[48,9216]{1,0:T(8,128)(2,1)S(1)} %bitcast.257), channel_id=1, source_target_pairs={{16,0},{32,16},{48,32},{64,48},{80,64},{96,80},{112,96},{17,1},{33... | collective-permute-start | bytes 2654216 | tf_op jit(solution)/shard_map/while/body/eval_jaxpr/ppermute | solution.py:19
  600.5 7.2 slice-start
  601.9 5.9 slice-start.1
  615.2 17.5 %collective-permute-start.1 = (bf16[48,9216]{1,0:T(8,128)(2,1)S(1)}, bf16[48,9216]{1,0:T(8,128)(2,1)S(1)}, u32[]{:S(2)}, u32[]{:S(2)}) collective-permute-start(bf16[48,9216]{1,0:T(8,128)(2,1)S(1)} %bitcast.257), channel_id=1, source_target_pairs={{16,0},{32,16},{48,32},{64,48},{80,64},{96,80},{112,96},{17,1},{33... | collective-permute-start | bytes 2654216 | tf_op jit(solution)/shard_map/while/body/eval_jaxpr/ppermute | solution.py:19
  632.7 7.2 slice-start
  634.1 5.9 slice-start.1
  647.4 17.5 %collective-permute-start.1 = (bf16[48,9216]{1,0:T(8,128)(2,1)S(1)}, bf16[48,9216]{1,0:T(8,128)(2,1)S(1)}, u32[]{:S(2)}, u32[]{:S(2)}) collective-permute-start(bf16[48,9216]{1,0:T(8,128)(2,1)S(1)} %bitcast.257), channel_id=1, source_target_pairs={{16,0},{32,16},{48,32},{64,48},{80,64},{96,80},{112,96},{17,1},{33... | collective-permute-start | bytes 2654216 | tf_op jit(solution)/shard_map/while/body/eval_jaxpr/ppermute | solution.py:19
  664.9 7.2 slice-start
  666.2 5.9 slice-start.1
  679.6 17.0 %collective-permute-start.1 = (bf16[48,9216]{1,0:T(8,128)(2,1)S(1)}, bf16[48,9216]{1,0:T(8,128)(2,1)S(1)}, u32[]{:S(2)}, u32[]{:S(2)}) collective-permute-start(bf16[48,9216]{1,0:T(8,128)(2,1)S(1)} %bitcast.257), channel_id=1, source_target_pairs={{16,0},{32,16},{48,32},{64,48},{80,64},{96,80},{112,96},{17,1},{33... | collective-permute-start | bytes 2654216 | tf_op jit(solution)/shard_map/while/body/eval_jaxpr/ppermute | solution.py:19
  696.6 7.2 slice-start
  698.0 5.9 slice-start.1
  711.3 17.0 %collective-permute-start.1 = (bf16[48,9216]{1,0:T(8,128)(2,1)S(1)}, bf16[48,9216]{1,0:T(8,128)(2,1)S(1)}, u32[]{:S(2)}, u32[]{:S(2)}) collective-permute-start(bf16[48,9216]{1,0:T(8,128)(2,1)S(1)} %bitcast.257), channel_id=1, source_target_pairs={{16,0},{32,16},{48,32},{64,48},{80,64},{96,80},{112,96},{17,1},{33... | collective-permute-start | bytes 2654216 | tf_op jit(solution)/shard_map/while/body/eval_jaxpr/ppermute | solution.py:19
  728.4 7.2 slice-start
  729.7 5.9 slice-start.1
  743.0 17.0 %collective-permute-start.1 = (bf16[48,9216]{1,0:T(8,128)(2,1)S(1)}, bf16[48,9216]{1,0:T(8,128)(2,1)S(1)}, u32[]{:S(2)}, u32[]{:S(2)}) collective-permute-start(bf16[48,9216]{1,0:T(8,128)(2,1)S(1)} %bitcast.257), channel_id=1, source_target_pairs={{16,0},{32,16},{48,32},{64,48},{80,64},{96,80},{112,96},{17,1},{33... | collective-permute-start | bytes 2654216 | tf_op jit(solution)/shard_map/while/body/eval_jaxpr/ppermute | solution.py:19
  760.1 7.2 slice-start
  761.4 5.9 slice-start.1
  774.7 17.0 %collective-permute-start.1 = (bf16[48,9216]{1,0:T(8,128)(2,1)S(1)}, bf16[48,9216]{1,0:T(8,128)(2,1)S(1)}, u32[]{:S(2)}, u32[]{:S(2)}) collective-permute-start(bf16[48,9216]{1,0:T(8,128)(2,1)S(1)} %bitcast.257), channel_id=1, source_target_pairs={{16,0},{32,16},{48,32},{64,48},{80,64},{96,80},{112,96},{17,1},{33... | collective-permute-start | bytes 2654216 | tf_op jit(solution)/shard_map/while/body/eval_jaxpr/ppermute | solution.py:19
  791.7 7.2 slice-start
  793.0 5.9 slice-start.1
  806.4 17.1 %collective-permute-start.1 = (bf16[48,9216]{1,0:T(8,128)(2,1)S(1)}, bf16[48,9216]{1,0:T(8,128)(2,1)S(1)}, u32[]{:S(2)}, u32[]{:S(2)}) collective-permute-start(bf16[48,9216]{1,0:T(8,128)(2,1)S(1)} %bitcast.257), channel_id=1, source_target_pairs={{16,0},{32,16},{48,32},{64,48},{80,64},{96,80},{112,96},{17,1},{33... | collective-permute-start | bytes 2654216 | tf_op jit(solution)/shard_map/while/body/eval_jaxpr/ppermute | solution.py:19
  823.5 7.2 slice-start
  824.8 5.9 slice-start.1
  838.2 17.1 %collective-permute-start.1 = (bf16[48,9216]{1,0:T(8,128)(2,1)S(1)}, bf16[48,9216]{1,0:T(8,128)(2,1)S(1)}, u32[]{:S(2)}, u32[]{:S(2)}) collective-permute-start(bf16[48,9216]{1,0:T(8,128)(2,1)S(1)} %bitcast.257), channel_id=1, source_target_pairs={{16,0},{32,16},{48,32},{64,48},{80,64},{96,80},{112,96},{17,1},{33... | collective-permute-start | bytes 2654216 | tf_op jit(solution)/shard_map/while/body/eval_jaxpr/ppermute | solution.py:19
  855.2 7.2 slice-start
  856.6 5.9 slice-start.1
  869.9 17.0 %collective-permute-start.1 = (bf16[48,9216]{1,0:T(8,128)(2,1)S(1)}, bf16[48,9216]{1,0:T(8,128)(2,1)S(1)}, u32[]{:S(2)}, u32[]{:S(2)}) collective-permute-start(bf16[48,9216]{1,0:T(8,128)(2,1)S(1)} %bitcast.257), channel_id=1, source_target_pairs={{16,0},{32,16},{48,32},{64,48},{80,64},{96,80},{112,96},{17,1},{33... | collective-permute-start | bytes 2654216 | tf_op jit(solution)/shard_map/while/body/eval_jaxpr/ppermute | solution.py:19
  892.6 176.3 %reduce-scatter.3.cloned.1.call-start = ((), (), s32[]{:S(2)}) async-start(), calls=%async_computation.4 | async-start | bytes 5013504 | tf_op jit(solution)/shard_map/reduce_scatter | solution.py:216
Sparse Core Ops, SparseCore 0:
  10.4 60.8 all-gather.2
  73.7 56.4 all-gather.4
  892.7 90.1 reduce-scatter.4
  987.4 81.4 reduce-scatter.2
where the time goes:
time: 1080 us
  waiting for transfers between devices  366 us (34%)
  other arithmetic  199 us (18%)
  matrix products  146 us (14%)
  blocking collectives  136 us (13%)
  local copies, waits for them, and re-layouts  117 us (11%)
  starting transfers between devices  72.8 us (7%)
  loops' own time  24.4 us (2%)
  between operations  15.2 us (1%)
    ppermute x22, waiting for transfers between devices, shifted(): return lax.ppermute(shard, axis, pairs)  215 us
    unnamed x2, blocking collectives  136 us
    dynamic_update_slice x66, other arithmetic, write_slot(): lax.dynamic_update_index_in_dim(piled_arrays, jnp.where(active, fresh_ite...  94.7 us
    reduce_scatter x1, waiting for transfers between devices, shards(): lax.psum_scatter(down_term.astype(jnp.bfloat16), 'fsdp', scatter_dimensio...  84.2 us
    ppermute x22, starting transfers between devices, shifted(): return lax.ppermute(shard, axis, pairs)  72.6 us
    dynamic_slice x88, local copies, waits for them, and re-layouts, write_slot(): former = lax.dynamic_index_in_dim(piled_arrays, index, 0, False)  72.5 us
    all_gather x1, waiting for transfers between devices, shards(): lax.all_gather(up_weight, 'fsdp', axis=1, tiled=True)  47.6 us
    dot_general x11, matrix products, forward_step(): bottleneck = jnp.dot(normed, down_mat, preferred_element_type=jnp.float32)  38.1 us
  transfers between devices with their start and end apart: 26, of which 25 were waited for; matrix products, arithmetic and copies ran while one was open for 12% of the time, Pallas kernels for 0%

commit v1 on v0

v1 whole, which is shorter than its diff:
```python
import functools
import math

import jax
import jax.numpy as jnp
from jax import lax
from jax.experimental import pallas as pl
from jax.experimental.pallas import tpu as pltpu
from jax.sharding import PartitionSpec as P

SQRT_HALF = 0.7071067811865476
INV_ROOT_TAU = 0.3989422804014327
CLIP_LEVEL = 448.0
NORM_EPSILON = 1e-05
LOWEST_EXPONENT = -9
HIGHEST_EXPONENT = -3

SECTIONS = 8
WIDTH = 9216
NECK = 256
BLOCK = 128
TOKENS = 48
MICRO = 4
ROWS = 16
CHUNKS = MICRO * TOKENS // ROWS
SHARD = 576
EXTRA = 16
WIDE = 1024
MEDIUM = 512

VM = pl.BlockSpec(memory_space=pltpu.VMEM)
SM = pl.BlockSpec(memory_space=pltpu.SMEM)
ANY = pl.BlockSpec(memory_space=pl.ANY)
NT = (((1,), (1,)), ((), ()))
TN = (((0,), (0,)), ((), ()))
F32 = jnp.float32
BF16 = jnp.bfloat16


def lane_sum(values):
    return jnp.sum(values, axis=-1, keepdims=True)


def clipped(values, limits, start):
    pieces = []
    for offset in range(0, values.shape[1], BLOCK):
        index = (start + offset) // BLOCK
        bound = jnp.broadcast_to(limits[:, index : index + 1], (values.shape[0], BLOCK))
        pieces.append(jnp.clip(values[:, offset : offset + BLOCK], -bound, bound))
    return jnp.concatenate(pieces, axis=1).astype(BF16)


def forward_kernel(
    tick,
    table,
    incoming,
    gain,
    down,
    up,
    base_in,
    base_out,
    limits,
    *refs,
):
    (outs, scratch) = (refs[6:13], refs[13:])
    layer_all, out_all, neck_all, act_all, normed_all, stat_all, delivered = outs
    rows_in, rows_out, bound, layer, section, neck, act, normed, stat, sems = scratch

    @pl.when(table[tick, 0] == 1)
    def _():
        row = pl.multiple_of(table[tick, 1], ROWS)
        base = pl.multiple_of(table[tick, 2], ROWS)
        here = pl.ds(row, ROWS)
        loads = [
            pltpu.make_async_copy(base_in.at[pl.ds(base, ROWS), :], rows_in, sems.at[0]),
            pltpu.make_async_copy(base_out.at[pl.ds(base, ROWS), :], rows_out, sems.at[1]),
            pltpu.make_async_copy(limits.at[here, :], bound, sems.at[2]),
        ]
        for copy in loads:
            copy.start()
        stores = [
            pltpu.make_async_copy(source, target.at[here, :], sems.at[3 + number])
            for number, (source, target) in enumerate(
                (
                    (layer, layer_all),
                    (section, out_all),
                    (neck, neck_all),
                    (act, act_all),
                    (normed, normed_all),
                    (stat, stat_all),
                )
            )
        ]
        loads[0].wait()
        total = jnp.zeros((ROWS, BLOCK), F32)
        for start in range(0, WIDTH, WIDE):
            span = slice(start, start + WIDE)
            values = (rows_in[:, span].astype(F32) + incoming[:, span].astype(F32)).astype(BF16)
            layer[:, span] = values
            values = values.astype(F32)
            for offset in range(0, WIDE, BLOCK):
                total += values[:, offset : offset + BLOCK]
        stores[0].start()
        mean = lane_sum(total) * (1.0 / WIDTH)
        total = jnp.zeros((ROWS, BLOCK), F32)
        for start in range(0, WIDTH, WIDE):
            values = layer[:, start : start + WIDE].astype(F32) - mean
            values = values * values
            for offset in range(0, WIDE, BLOCK):
                total += values[:, offset : offset + BLOCK]
        scale = lax.rsqrt(lane_sum(total) * (1.0 / WIDTH) + NORM_EPSILON)
        stat[:, :BLOCK] = jnp.broadcast_to(mean, (ROWS, BLOCK))
        stat[:, BLOCK:] = jnp.broadcast_to(scale, (ROWS, BLOCK))
        stores[5].start()
        result = jnp.zeros((ROWS, NECK), F32)
        for start in range(0, WIDTH, WIDE):
            span = slice(start, start + WIDE)
            values = (layer[:, span].astype(F32) - mean) * scale
            values = (values * gain[:, span]).astype(BF16)
            normed[:, span] = values
            result += jnp.dot(values, down[span, :], preferred_element_type=F32)
        stores[4].start()
        neck[...] = result
        stores[2].start()
        activated = (result * 0.5 * (1.0 + lax.erf(result * SQRT_HALF))).astype(BF16)
        act[...] = activated
        stores[3].start()
        loads[1].wait()
        loads[2].wait()
        edges = bound[...]
        for start in range(0, WIDTH, MEDIUM):
            span = slice(start, start + MEDIUM)
            branch = lax.dot_general(activated, up[span, :], NT, preferred_element_type=F32)
            value = (layer[:, span].astype(F32) + branch).astype(BF16)
            section[:, span] = value
            change = value.astype(F32) - rows_out[:, span].astype(F32)
            delivered[:, span] = clipped(change, edges, start)
        stores[1].start()
        for copy in stores:
            copy.wait()


def backward_kernel(
    tick,
    table,
    incoming,
    gain,
    down,
    up,
    loss_grad,
    limits,
    layer_all,
    neck_all,
    stat_all,
    *refs,
):
    (outs, scratch) = (refs[4:12], refs[12:])
    grad_all, cot_all, neckcot_all, gain_all, sent = outs[3:]
    cot, bound, layer, neck, stat, grad, neckcot, gains, hold, sems = scratch

    @pl.when(table[tick, 3] == 1)
    def _():
        row = pl.multiple_of(table[tick, 4], ROWS)
        here = pl.ds(row, ROWS)
        last = table[tick, 5] == 1
        loads = [
            pltpu.make_async_copy(limits.at[here, :], bound, sems.at[0]),
            pltpu.make_async_copy(layer_all.at[here, :], layer, sems.at[1]),
            pltpu.make_async_copy(neck_all.at[here, :], neck, sems.at[2]),
            pltpu.make_async_copy(stat_all.at[here, :], stat, sems.at[3]),
        ]
        for copy in loads:
            copy.start()
        stores = [
            pltpu.make_async_copy(grad, grad_all.at[here, :], sems.at[4]),
            pltpu.make_async_copy(cot, cot_all.at[here, :], sems.at[5]),
            pltpu.make_async_copy(neckcot, neckcot_all.at[here, :], sems.at[6]),
            pltpu.make_async_copy(
                gains, gain_all.at[pl.ds(pl.multiple_of(row // 2, 8), 8), :], sems.at[7]
            ),
        ]

        @pl.when(last)
        def _():
            fetch = pltpu.make_async_copy(loss_grad.at[here, :], cot, sems.at[8])
            fetch.start()
            fetch.wait()

        @pl.when(jnp.logical_not(last))
        def _():
            cot[...] = incoming[...]

        stores[1].start()
        result = jnp.zeros((ROWS, NECK), F32)
        for start in range(0, WIDTH, WIDE):
            span = slice(start, start + WIDE)
            result += jnp.dot(cot[:, span], up[span, :], preferred_element_type=F32)
        loads[2].wait()
        bottle = neck[...]
        slope = 0.5 * (1.0 + lax.erf(bottle * SQRT_HALF)) + bottle * INV_ROOT_TAU * jnp.exp(
            -0.5 * bottle * bottle
        )
        small = (result * slope).astype(BF16)
        neckcot[...] = small
        stores[2].start()
        loads[1].wait()
        loads[3].wait()
        mean = stat[:, :1]
        scale = stat[:, BLOCK : BLOCK + 1]
        first = jnp.zeros((ROWS, BLOCK), F32)
        second = jnp.zeros((ROWS, BLOCK), F32)
        for start in range(0, WIDTH, MEDIUM):
            span = slice(start, start + MEDIUM)
            wide = lax.dot_general(small, down[span, :], NT, preferred_element_type=F32)
            centred = (layer[:, span].astype(F32) - mean) * scale
            product = wide * centred
            gains[:, span] = product[:8, :] + product[8:, :]
            scaled = wide * gain[:, span]
            hold[:, span] = scaled
            product = scaled * centred
            for offset in range(0, MEDIUM, BLOCK):
                first += scaled[:, offset : offset + BLOCK]
                second += product[:, offset : offset + BLOCK]
        stores[3].start()
        first = lane_sum(first) * (1.0 / WIDTH)
        second = lane_sum(second) * (1.0 / WIDTH)
        loads[0].wait()
        edges = bound[...]
        for start in range(0, WIDTH, MEDIUM):
            span = slice(start, start + MEDIUM)
            centred = (layer[:, span].astype(F32) - mean) * scale
            value = cot[:, span].astype(F32) + scale * (hold[:, span] - first - centred * second)
            grad[:, span] = value.astype(BF16)
            sent[:, span] = clipped(value, edges, start)
        stores[0].start()
        for copy in stores:
            copy.wait()


def call_params(megabytes):
    return pltpu.CompilerParams(vmem_limit_bytes=megabytes << 20)


def forward_call(tick, table, incoming, gain, down, up, base_in, base_out, limits, state):
    shape = jax.ShapeDtypeStruct
    outs = [shape(item.shape, item.dtype) for item in state] + [shape((ROWS, WIDTH), BF16)]
    got = pl.pallas_call(
        functools.partial(forward_kernel, tick),
        out_shape=outs,
        in_specs=[SM, VM, VM, VM, VM, ANY, ANY, ANY] + [ANY] * 6,
        out_specs=[ANY] * 6 + [VM],
        scratch_shapes=[
            pltpu.VMEM((ROWS, WIDTH), BF16),
            pltpu.VMEM((ROWS, WIDTH), BF16),
            pltpu.VMEM((ROWS, WIDTH // BLOCK), F32),
            pltpu.VMEM((ROWS, WIDTH), BF16),
            pltpu.VMEM((ROWS, WIDTH), BF16),
            pltpu.VMEM((ROWS, NECK), F32),
            pltpu.VMEM((ROWS, NECK), BF16),
            pltpu.VMEM((ROWS, WIDTH), BF16),
            pltpu.VMEM((ROWS, 2 * BLOCK), F32),
            pltpu.SemaphoreType.DMA((9,)),
        ],
        input_output_aliases={8 + number: number for number in range(6)},
        compiler_params=call_params(24),
        cost_estimate=pl.CostEstimate(flops=150_000_000, bytes_accessed=9_000_000, transcendentals=0),
        name="section_forward",
    )(table, incoming, gain, down, up, base_in, base_out, limits, *state)
    return got[:6], got[6]


def backward_call(tick, table, incoming, gain, down, up, loss_grad, limits, saved, state):
    shape = jax.ShapeDtypeStruct
    kept = list(saved) + list(state)
    outs = [shape(item.shape, item.dtype) for item in kept] + [shape((ROWS, WIDTH), BF16)]
    got = pl.pallas_call(
        functools.partial(backward_kernel, tick),
        out_shape=outs,
        in_specs=[SM, VM, VM, VM, VM, ANY, ANY] + [ANY] * 7,
        out_specs=[ANY] * 7 + [VM],
        scratch_shapes=[
            pltpu.VMEM((ROWS, WIDTH), BF16),
            pltpu.VMEM((ROWS, WIDTH // BLOCK), F32),
            pltpu.VMEM((ROWS, WIDTH), BF16),
            pltpu.VMEM((ROWS, NECK), F32),
            pltpu.VMEM((ROWS, 2 * BLOCK), F32),
            pltpu.VMEM((ROWS, WIDTH), BF16),
            pltpu.VMEM((ROWS, NECK), BF16),
            pltpu.VMEM((8, WIDTH), F32),
            pltpu.VMEM((ROWS, WIDTH), F32),
            pltpu.SemaphoreType.DMA((9,)),
        ],
        input_output_aliases={7 + number: number for number in range(7)},
        compiler_params=call_params(24),
        cost_estimate=pl.CostEstimate(flops=150_000_000, bytes_accessed=9_000_000, transcendentals=0),
        name="section_backward",
    )(table, incoming, gain, down, up, loss_grad, limits, *kept)
    return got[:3], got[3:7], got[7]


def empty_buffers(shapes):
    return pl.pallas_call(
        lambda *refs: None,
        out_shape=[jax.ShapeDtypeStruct(dims, kind) for dims, kind in shapes],
        out_specs=[ANY] * len(shapes),
        name="empty_buffers",
    )()


def assemble_kernel(place, *refs):
    parts, outs, sems = refs[:16], refs[16:19], refs[19]
    copies = []
    for number, part in enumerate(parts):
        shard = place[number]
        for which, (start, size) in enumerate(((0, SHARD), (SHARD, SHARD), (2 * SHARD, EXTRA))):
            target = outs[which].at[pl.ds(pl.multiple_of(shard * size, 16), size), :]
            copies.append(
                pltpu.make_async_copy(
                    part.at[pl.ds(start, size), :], target, sems.at[number * 3 + which]
                )
            )
    for copy in copies:
        copy.start()
    for copy in copies:
        copy.wait()


def assemble(place, parts):
    return pl.pallas_call(
        assemble_kernel,
        out_shape=[
            jax.ShapeDtypeStruct((WIDTH, NECK), BF16),
            jax.ShapeDtypeStruct((WIDTH, NECK), BF16),
            jax.ShapeDtypeStruct((16 * EXTRA, NECK), BF16),
        ],
        in_specs=[SM] + [ANY] * 16,
        out_specs=[ANY] * 3,
        scratch_shapes=[pltpu.SemaphoreType.DMA((48,))],
        cost_estimate=pl.CostEstimate(flops=0, bytes_accessed=19_000_000, transcendentals=0),
        name="assemble_weights",
    )(place, *parts)


def fsdp_index(y, z, core):
    return y * 4 + z * 2 + core


def fsdp_pairs(move):
    return [
        (fsdp_index(y, z, core), fsdp_index(*move(y, z, core)))
        for y in range(4)
        for z in range(2)
        for core in range(2)
    ]


def to_core(value):
    return lax.ppermute(value, "fsdp", fsdp_pairs(lambda y, z, core: (y, z, 1 - core)))


def along_z(value):
    return lax.ppermute(value, "fsdp", fsdp_pairs(lambda y, z, core: (y, 1 - z, core)))


def along_y(value, by):
    return lax.ppermute(value, "fsdp", fsdp_pairs(lambda y, z, core: ((y + by) % 4, z, core)))


def gather_parts(own):
    parts = {(0, 0): own}
    parts[(0, 1)] = along_z(own)
    for by in (1, 3, 2):
        parts[(by, 0)] = along_y(own, -by)
    parts[(2, 1)] = along_z(parts[(2, 0)])
    for by in (1, 3):
        parts[(by, 1)] = along_y(parts[(0, 1)], -by)
    return parts


def gradient_kernel(order, normed, neckcot, cot, act, gains, mine, theirs, hold):
    factor = 1.0 / math.sqrt(MICRO * TOKENS * 16)
    core = order[8]
    both = 2 * SHARD
    for number, (left, right) in enumerate(((normed, neckcot), (cot, act))):
        hold[...] = (
            lax.dot_general(left[...], right[...], TN, preferred_element_type=F32) * factor
        ).astype(BF16)
        rows = slice(number * SHARD, (number + 1) * SHARD)
        mine[0, rows, :] = hold[pl.ds(pl.multiple_of(core * SHARD, SHARD), SHARD), :]
        theirs[0, rows, :] = hold[pl.ds(pl.multiple_of((1 - core) * SHARD, SHARD), SHARD), :]
    mine[0, both:, :] = gains[0, core]
    theirs[0, both:, :] = gains[0, 1 - core]


def gradient_blocks(order, first, count, normed, neckcot, cot, act, gains):
    rows = MICRO * TOKENS
    block = pl.BlockSpec((rows, 2 * SHARD), lambda i, order: (0, order[first + i]))
    small = pl.BlockSpec((rows, NECK), lambda i, order: (0, 0))
    result = pl.BlockSpec((1, 2 * SHARD + EXTRA, NECK), lambda i, order: (i, 0, 0))
    return pl.pallas_call(
        gradient_kernel,
        grid_spec=pltpu.PrefetchScalarGridSpec(
            num_scalar_prefetch=1,
            grid=(count,),
            in_specs=[
                block,
                small,
                block,
                small,
                pl.BlockSpec((1, 2, EXTRA, NECK), lambda i, order: (order[first + i], 0, 0, 0)),
            ],
            out_specs=[result, result],
            scratch_shapes=[pltpu.VMEM((2 * SHARD, NECK), BF16)],
        ),
        out_shape=[jax.ShapeDtypeStruct((count, 2 * SHARD + EXTRA, NECK), BF16)] * 2,
        compiler_params=call_params(24),
        name="gradient_blocks",
    )(order, normed, neckcot, cot, act, gains)


REDUCE_ORDER = ((1, 1), (3, 1), (2, 1), (1, 0), (3, 0), (2, 0), (0, 1), (0, 0))


def widen(value):
    return value.astype(F32)


def reduce_parts(order, normed, neckcot, cot, act, gains):
    blocks = {}
    for first in (0, 4):
        mine, theirs = gradient_blocks(order, first, 4, normed, neckcot, cot, act, gains)
        theirs = to_core(theirs)
        for number in range(4):
            blocks[REDUCE_ORDER[first + number]] = (mine[number], theirs[number])

    def summed(key, *others):
        mine, theirs = blocks[key]
        total = widen(mine) + widen(theirs)
        for other in others:
            total += widen(other)
        return total

    def narrow(value):
        return value.astype(BF16)

    first = along_y(narrow(summed((1, 1))), 1)
    second = along_y(narrow(summed((3, 1))), 3)
    third = along_z(narrow(summed((2, 1))))
    fourth = along_y(narrow(summed((1, 0))), 1)
    fifth = along_y(narrow(summed((3, 0))), 3)
    sixth = along_y(narrow(summed((2, 0), third)), 2)
    seventh = along_z(narrow(summed((0, 1), first, second)))
    return summed((0, 0), fourth, fifth, sixth, seventh)


def shards(
    in_base,
    out_base,
    sample_ids,
    send_exponent,
    grad_exponent,
    loss_grad,
    down_weight,
    up_weight,
    norm_gain,
):
    section = lax.axis_index("section")
    place = lax.axis_index("fsdp")
    y, z, core = place >> 2, (place >> 1) & 1, place & 1
    tokens = MICRO * TOKENS
    ticks = CHUNKS + 2 * SECTIONS - 2

    gain_rows = jnp.pad(norm_gain[0], (0, EXTRA * NECK - SHARD)).reshape(EXTRA, NECK)
    own = jnp.concatenate([down_weight[0], up_weight[0], gain_rows], axis=0)
    parts = gather_parts(own)
    pieces, places = [], []
    for (dy, dz), part in parts.items():
        spot = fsdp_index((y + dy) & 3, z ^ dz, core)
        pieces += [part, to_core(part)]
        places += [spot, spot + 1 - 2 * core]
    down, up, gain = assemble(jnp.stack(places).astype(jnp.int32), pieces)
    gain = gain.reshape(16, EXTRA * NECK)[:, :SHARD].reshape(1, WIDTH).astype(F32)

    tick = jnp.arange(ticks, dtype=jnp.int32)

    def lane(chunk):
        active = (chunk >= 0) & (chunk < CHUNKS)
        chunk = jnp.clip(chunk, 0, CHUNKS - 1)
        return active.astype(jnp.int32), chunk

    per = TOKENS // ROWS
    ahead, chunk = lane(tick - section)
    base = sample_ids[chunk // per] * TOKENS + (chunk % per) * ROWS
    back, reverse = lane(tick - 2 * (SECTIONS - 1) + section)
    last = jnp.full((ticks,), section == SECTIONS - 1).astype(jnp.int32)
    table = jnp.stack([ahead, chunk * ROWS, base, back, reverse * ROWS, last], axis=1)

    def limit(exponent):
        exponent = exponent[0].reshape(tokens, WIDTH // BLOCK)
        level = jnp.zeros(exponent.shape, F32)
        for value in range(LOWEST_EXPONENT, HIGHEST_EXPONENT):
            level = jnp.where(exponent == value, F32(CLIP_LEVEL * 2.0**value), level)
        return level

    send_limit, back_limit = limit(send_exponent), limit(grad_exponent)
    base_in = in_base.reshape(-1, WIDTH)
    base_out = out_base.reshape(-1, WIDTH)
    loss = loss_grad.reshape(tokens, WIDTH)

    buffers = empty_buffers(
        [
            ((tokens, WIDTH), BF16),
            ((tokens, WIDTH), BF16),
            ((tokens, NECK), F32),
            ((tokens, NECK), BF16),
            ((tokens, WIDTH), BF16),
            ((tokens, 2 * BLOCK), F32),
            ((tokens, WIDTH), BF16),
            ((tokens, WIDTH), BF16),
            ((tokens, NECK), BF16),
            ((tokens // 2, WIDTH), F32),
        ]
    )
    layer, out, neck, act, normed, stat = buffers[:6]
    cots = buffers[6:]
    zero = jnp.zeros((ROWS, WIDTH), BF16)
    arriving, returning = zero, zero
    for step in range(ticks):
        if step < CHUNKS + SECTIONS - 1:
            (layer, out, neck, act, normed, stat), delivered = forward_call(
                step,
                table,
                arriving,
                gain,
                down,
                up,
                base_in,
                base_out,
                send_limit,
                (layer, out, neck, act, normed, stat),
            )
            pairs = [(s, s + 1) for s in range(SECTIONS - 1) if 0 <= step - s < CHUNKS]
            arriving = lax.ppermute(delivered, "section", pairs) if pairs else zero
        if step >= SECTIONS - 1:
            (layer, neck, stat), cots, sent = backward_call(
                step,
                table,
                returning,
                gain,
                down,
                up,
                loss,
                back_limit,
                (layer, neck, stat),
                cots,
            )
            pairs = [
                (s, s - 1)
                for s in range(1, SECTIONS)
                if 0 <= step - 2 * (SECTIONS - 1) + s < CHUNKS
            ]
            returning = lax.ppermute(sent, "section", pairs) if pairs else zero

    grad, cot, neckcot, gain_sums = cots
    factor = 1.0 / math.sqrt(tokens * 16)
    gains = (jnp.sum(gain_sums, axis=0) * factor).astype(BF16).reshape(8, 2, SHARD)
    gains = jnp.pad(gains, ((0, 0), (0, 0), (0, EXTRA * NECK - SHARD))).reshape(8, 2, EXTRA, NECK)
    order = [((y + dy) & 3) * 2 + (z ^ dz) for dy, dz in REDUCE_ORDER] + [core]
    order = jnp.stack(order).astype(jnp.int32)
    total = reduce_parts(order, normed, neckcot, cot, act, gains)
    shape = (1, MICRO, TOKENS, WIDTH)
    return (
        out.reshape(shape),
        grad.reshape(shape),
        total[None, :SHARD],
        total[None, SHARD : 2 * SHARD],
        total[2 * SHARD :].reshape(1, EXTRA * NECK)[:, :SHARD],
    )


def solution(mesh):
    in_specs = (
        P("section", None, "fsdp", None),
        P("section", None, "fsdp", None),
        P(),
        P("section", None, "fsdp", None),
        P("section", None, "fsdp", None),
        P(None, "fsdp", None),
        P("section", "fsdp", None),
        P("section", "fsdp", None),
        P("section", "fsdp"),
    )
    out_specs = (
        P("section", None, "fsdp", None),
        P("section", None, "fsdp", None),
        P("section", "fsdp", None),
        P("section", "fsdp", None),
        P("section", "fsdp"),
    )
    return jax.shard_map(shards, mesh=mesh, in_specs=in_specs, out_specs=out_specs, check_vma=False)
```

time: 1080 us -> 1010 us (0.935)
  Pallas kernels: 0 us -> 449 us
  other arithmetic: 199 us -> 13.5 us
  matrix products: 146 us -> 0 us
  blocking collectives: 136 us -> 0 us
  waiting for transfers between devices: 366 us -> 233 us
  local copies, waits for them, and re-layouts: 117 us -> 179 us
  starting transfers between devices: 72.8 us -> 122 us
  loops' own time: 24.4 us -> 0 us
  between operations: 15.2 us -> 2.57 us
    pallas_call x0 -> x42, Pallas kernels: none -> 449 us  [the longest x1 292 us: assemble(): pl.pallas_call(assemble_kernel, out_shape=[jax.ShapeDtypeStruct((WIDTH, N...]
    unnamed x5 -> x302, local copies, waits for them, and re-layouts: 1.57 us -> 167 us
    dot_general x46 -> x0, matrix products: 146 us -> none  [the longest x11 38.1 us: forward_step(): bottleneck = jnp.dot(normed, down_mat, preferred_element_type=jnp.float32)]
    unnamed x2 -> x0, blocking collectives: 136 us -> none
    reduce_scatter x2 -> x0, waiting for transfers between devices: 102 us -> none  [the longest x1 84.2 us: shards(): lax.psum_scatter(down_term.astype(jnp.bfloat16), 'fsdp', scatter_dimensio...]
    dynamic_update_slice x66 -> x0, other arithmetic: 94.7 us -> none  [write_slot(): lax.dynamic_update_index_in_dim(piled_arrays, jnp.where(active, fresh_ite...]
    dynamic_slice x99 -> x0, local copies, waits for them, and re-layouts: 78.9 us -> none  [the longest x88 72.5 us: write_slot(): former = lax.dynamic_index_in_dim(piled_arrays, index, 0, False)]
    ppermute x22 -> x60, starting transfers between devices: 72.6 us -> 122 us  [the longest x18 54.2 us: shards(): arriving = lax.ppermute(delivered, 'section', pairs) if pairs else zero]
  transfers between devices with their start and end apart: 26 -> 60, of which waited for: 25 -> 30; matrix products, arithmetic and copies ran while one was open for 12% -> 1% of each run, Pallas kernels for 0% -> 6%
where the time goes in v1:
time: 1010 us; the launch traced here: 998 us
  Pallas kernels  449 us (44%)
  waiting for transfers between devices  233 us (23%)
  local copies, waits for them, and re-layouts  179 us (18%)
  starting transfers between devices  122 us (12%)
  other arithmetic  13.5 us (1%)
    pallas_call x1, Pallas kernels, assemble(): pl.pallas_call(assemble_kernel, out_shape=[jax.ShapeDtypeStruct((WIDTH, N...  292 us
    unnamed x302, local copies, waits for them, and re-layouts  167 us
    ppermute x18, waiting for transfers between devices, shards(): returning = lax.ppermute(sent, 'section', pairs) if pairs else zero  139 us
    pallas_call x19, Pallas kernels, backward_call(): pl.pallas_call(functools.partial(backward_kernel, tick), out_shape=outs,...  75.6 us
    pallas_call x19, Pallas kernels, forward_call(): pl.pallas_call(functools.partial(forward_kernel, tick), out_shape=outs, i...  74.4 us
    ppermute x10, waiting for transfers between devices, along_y(): lax.ppermute(value, 'fsdp', fsdp_pairs(lambda y, z, core: ((y + by) % 4,...  55.7 us
    ppermute x18, starting transfers between devices, shards(): arriving = lax.ppermute(delivered, 'section', pairs) if pairs else zero  54.2 us
    ppermute x18, waiting for transfers between devices, shards(): arriving = lax.ppermute(delivered, 'section', pairs) if pairs else zero  35.7 us
  transfers between devices with their start and end apart: 60, of which 30 were waited for; matrix products, arithmetic and copies ran while one was open for 1% of the time, Pallas kernels for 6%

profile of v1, /device:TPU:0, one launch (start us, length us, event | category | flops | bytes accessed | tf_op | source)
XLA Modules:
  0.0 998.3 jit_solution(7644854551489646687)
XLA Ops:
  9.1 3.9 collective-permute-start.1
  12.9 7.5 collective-permute-done.7.refs_8_
  20.5 4.0 collective-permute-start.9
  24.4 7.7 collective-permute-done.5.refs_6_
  39.1 11.0 %collective-permute-done.13.refs_14_ = bf16[1168,256]{1,0:T(8,128)(2,1)} collective-permute-done((bf16[1168,256]{1,0:T(8,128)(2,1)}, bf16[1168,256]{1,0:T(8,128)(2,1)}, u32[]{:S(2)}, u32[]{:S(2)}) %collective-permute-start.13) | collective-permute-done | bytes 598048 | tf_op jit(solution)/shard_map/ppermute | solution.py:366
  57.2 292.2 %assemble_weights.1 = (bf16[9216,256]{1,0:T(8,128)(2,1)}, bf16[9216,256]{1,0:T(8,128)(2,1)}, bf16[256,256]{1,0:T(8,128)(2,1)}) custom-call(s32[16]{0:T(128)} %stack.110.place, bf16[1168,256]{1,0:T(8,128)(2,1)} %copy-done.139, bf16[1168,256]{1,0:T(8,128)(2,1)} %copy-done.142, bf16[1168,256]{1,0:T(8,128)(2,1)} %collective-permute-done.1.refs_2_, ...), custom_call_target="tpu_custom_call" | custom-call | bytes 19000000 | tf_op jit(solution)/shard_map/assemble_weights/pallas_call | solution.py:329
  369.5 5.6 section_forward.19
  376.4 7.1 collective-permute-done.15.incoming
  388.0 5.6 section_forward.20
  393.6 4.4 collective-permute-start.16
  398.0 6.2 collective-permute-done.16.incoming
  404.2 5.8 section_forward.21
  410.0 4.4 collective-permute-start.17
  414.4 5.3 collective-permute-done.17.incoming
  419.8 5.6 section_forward.22
  425.4 4.4 collective-permute-start.18
  429.8 4.4 collective-permute-done.18.incoming
  434.2 5.6 section_forward.23
  439.8 4.4 collective-permute-start.19
  444.2 4.2 collective-permute-done.19.incoming
  448.4 5.6 section_forward.24
  454.0 4.4 collective-permute-start.20
  458.4 4.2 collective-permute-done.20.incoming
  462.6 5.6 section_forward.25
  468.2 4.4 collective-permute-start.21
  472.6 4.1 collective-permute-done.21.incoming
  476.8 6.0 section_forward.26
  484.1 4.4 collective-permute-start.22
  501.5 5.6 section_forward.27
  521.9 5.6 section_forward.28
  528.1 6.5 collective-permute-start.25
  545.8 5.6 section_forward.29
  552.0 6.5 collective-permute-start.27
  569.5 5.6 section_forward.30
  617.7 35.9 %collective-permute-done.36.incoming = bf16[16,9216]{1,0:T(8,128)(2,1)S(1)} collective-permute-done((bf16[16,9216]{1,0:T(8,128)(2,1)S(1)}, bf16[16,9216]{1,0:T(8,128)(2,1)S(1)}, u32[]{:S(2)}, u32[]{:S(2)}) %collective-permute-start.36) | collective-permute-done | bytes 294944 | tf_op jit(solution)/shard_map/ppermute | solution.py:562
  658.5 5.6 section_backward.26
  671.4 10.2 %collective-permute-done.38.incoming = bf16[16,9216]{1,0:T(8,128)(2,1)S(1)} collective-permute-done((bf16[16,9216]{1,0:T(8,128)(2,1)S(1)}, bf16[16,9216]{1,0:T(8,128)(2,1)S(1)}, u32[]{:S(2)}, u32[]{:S(2)}) %collective-permute-start.38) | collective-permute-done | bytes 294944 | tf_op jit(solution)/shard_map/ppermute | solution.py:562
  686.6 5.7 section_backward.27
  699.7 5.8 collective-permute-done.40.incoming
  710.4 5.6 section_backward.28
  723.3 10.2 %collective-permute-done.42.incoming = bf16[16,9216]{1,0:T(8,128)(2,1)S(1)} collective-permute-done((bf16[16,9216]{1,0:T(8,128)(2,1)S(1)}, bf16[16,9216]{1,0:T(8,128)(2,1)S(1)}, u32[]{:S(2)}, u32[]{:S(2)}) %collective-permute-start.42) | collective-permute-done | bytes 294944 | tf_op jit(solution)/shard_map/ppermute | solution.py:562
  738.4 5.6 section_backward.29
  751.5 5.7 collective-permute-done.43.incoming
  762.1 5.7 section_backward.30
  769.2 9.4 collective-permute-done.44.incoming
  778.6 5.6 section_backward.31
  785.4 9.6 collective-permute-done.45.incoming
  795.0 5.6 section_backward.32
  801.9 10.9 %collective-permute-done.46.incoming = bf16[16,9216]{1,0:T(8,128)(2,1)S(1)} collective-permute-done((bf16[16,9216]{1,0:T(8,128)(2,1)S(1)}, bf16[16,9216]{1,0:T(8,128)(2,1)S(1)}, u32[]{:S(2)}, u32[]{:S(2)}) %collective-permute-start.46) | collective-permute-done | bytes 294944 | tf_op jit(solution)/shard_map/ppermute | solution.py:562
  812.8 5.6 section_backward.33
  819.7 12.4 %collective-permute-done.47.incoming = bf16[16,9216]{1,0:T(8,128)(2,1)S(1)} collective-permute-done((bf16[16,9216]{1,0:T(8,128)(2,1)S(1)}, bf16[16,9216]{1,0:T(8,128)(2,1)S(1)}, u32[]{:S(2)}, u32[]{:S(2)}) %collective-permute-start.47) | collective-permute-done | bytes 294944 | tf_op jit(solution)/shard_map/ppermute | solution.py:562
  832.1 5.6 section_backward.34
  838.9 13.1 %collective-permute-done.48.incoming = bf16[16,9216]{1,0:T(8,128)(2,1)S(1)} collective-permute-done((bf16[16,9216]{1,0:T(8,128)(2,1)S(1)}, bf16[16,9216]{1,0:T(8,128)(2,1)S(1)}, u32[]{:S(2)}, u32[]{:S(2)}) %collective-permute-start.48) | collective-permute-done | bytes 294944 | tf_op jit(solution)/shard_map/ppermute | solution.py:562
  852.0 5.6 section_backward.35
  858.8 8.5 collective-permute-done.49.incoming
  867.4 6.5 section_backward.36
  882.0 7.0 collective-permute-done.50.incoming
  904.1 6.4 section_backward.37
  932.0 3.5 gradient_blocks.2
  937.2 7.4 collective-permute-start.58
  944.6 8.9 collective-permute-start.57
  960.0 10.2 %collective-permute-done.57 = bf16[1168,256]{1,0:T(8,128)(2,1)S(1)} collective-permute-done((bf16[1168,256]{1,0:T(8,128)(2,1)S(1)}, bf16[1168,256]{1,0:T(8,128)(2,1)S(1)}, u32[]{:S(2)}, u32[]{:S(2)}) %collective-permute-start.57) | collective-permute-done | bytes 598048 | tf_op jit(solution)/shard_map/ppermute | solution.py:366
  977.3 5.4 collective-permute-done.53
  982.8 12.8 %collective-permute-done.56 = bf16[1168,256]{1,0:T(8,128)(2,1)S(1)} collective-permute-done((bf16[1168,256]{1,0:T(8,128)(2,1)S(1)}, bf16[1168,256]{1,0:T(8,128)(2,1)S(1)}, u32[]{:S(2)}, u32[]{:S(2)}) %collective-permute-start.56) | collective-permute-done | bytes 598048 | tf_op jit(solution)/shard_map/ppermute | solution.py:366
  (432 shorter events, 266.8 us)
Async XLA Ops:
  2.5 18.0 %collective-permute-start.7 = (bf16[1168,256]{1,0:T(8,128)(2,1)S(1)}, bf16[1168,256]{1,0:T(8,128)(2,1)S(1)}, u32[]{:S(2)}, u32[]{:S(2)}) collective-permute-start(bf16[1168,256]{1,0:T(8,128)(2,1)S(1)} %pad_maximum_fusion.refs_0_), channel_id=1, source_target_pairs={{0,8},{1,9},{2,10},{3,11},{4,12},{5,13},{6,14},{7,15},{8,0},{9,1},... | collective-permute-start | bytes 1794056 | tf_op jit(solution)/shard_map/ppermute | solution.py:366
  5.8 26.3 %collective-permute-start.5 = (bf16[1168,256]{1,0:T(8,128)(2,1)S(1)}, bf16[1168,256]{1,0:T(8,128)(2,1)S(1)}, u32[]{:S(2)}, u32[]{:S(2)}) collective-permute-start(bf16[1168,256]{1,0:T(8,128)(2,1)S(1)} %pad_maximum_fusion.refs_0_), channel_id=1, source_target_pairs={{0,4},{1,5},{2,6},{3,7},{4,8},{5,9},{6,10},{7,11},{8,12},{9,13},{1... | collective-permute-start | bytes 1794056 | tf_op jit(solution)/shard_map/ppermute | solution.py:366
  6.5 26.2 %collective-permute-start.3 = (bf16[1168,256]{1,0:T(8,128)(2,1)S(1)}, bf16[1168,256]{1,0:T(8,128)(2,1)}, u32[]{:S(2)}, u32[]{:S(2)}) collective-permute-start(bf16[1168,256]{1,0:T(8,128)(2,1)S(1)} %pad_maximum_fusion.refs_0_), channel_id=1, source_target_pairs={{0,12},{1,13},{2,14},{3,15},{4,0},{5,1},{6,2},{7,3},{8,4},{9,5},{1... | collective-permute-start | bytes 1794056 | tf_op jit(solution)/shard_map/ppermute | solution.py:366
  9.1 23.6 %collective-permute-start.1 = (bf16[1168,256]{1,0:T(8,128)(2,1)S(1)}, bf16[1168,256]{1,0:T(8,128)(2,1)}, u32[]{:S(2)}, u32[]{:S(2)}) collective-permute-start(bf16[1168,256]{1,0:T(8,128)(2,1)S(1)} %pad_maximum_fusion.refs_0_), channel_id=1, source_target_pairs={{0,2},{1,3},{2,0},{3,1},{4,6},{5,7},{6,4},{7,5},{8,10},{9,11},{10,... | collective-permute-start | bytes 1794056 | tf_op jit(solution)/shard_map/ppermute | solution.py:362
  12.9 21.5 %collective-permute-start = (bf16[1168,256]{1,0:T(8,128)(2,1)S(1)}, bf16[1168,256]{1,0:T(8,128)(2,1)S(1)}, u32[]{:S(2)}, u32[]{:S(2)}) collective-permute-start(bf16[1168,256]{1,0:T(8,128)(2,1)S(1)} %pad_maximum_fusion.refs_0_), channel_id=1, source_target_pairs={{0,1},{1,0},{2,3},{3,2},{4,5},{5,4},{6,7},{7,6},{8,9},{9,8},{10,11... | collective-permute-start | bytes 1794056 | tf_op jit(solution)/shard_map/ppermute | solution.py:358
  20.5 35.1 %copy-start.140 = (bf16[1168,256]{1,0:T(8,128)(2,1)}, bf16[1168,256]{1,0:T(8,128)(2,1)S(1)}, u32[]{:S(2)}) copy-start(bf16[1168,256]{1,0:T(8,128)(2,1)S(1)} %collective-permute-done.7.refs_8_) | copy-start | bytes 1794052
  20.5 18.0 %collective-permute-start.9 = (bf16[1168,256]{1,0:T(8,128)(2,1)S(1)}, bf16[1168,256]{1,0:T(8,128)(2,1)}, u32[]{:S(2)}, u32[]{:S(2)}) collective-permute-start(bf16[1168,256]{1,0:T(8,128)(2,1)S(1)} %collective-permute-done.7.refs_8_), channel_id=1, source_target_pairs={{0,2},{1,3},{2,0},{3,1},{4,6},{5,7},{6,4},{7,5},{8,10},{9,11},{10,... | collective-permute-start | bytes 1794056 | tf_op jit(solution)/shard_map/ppermute | solution.py:362
  32.1 6.4 collective-permute-start.8
  32.7 6.4 collective-permute-start.6
  32.7 17.4 %collective-permute-start.13 = (bf16[1168,256]{1,0:T(8,128)(2,1)}, bf16[1168,256]{1,0:T(8,128)(2,1)}, u32[]{:S(2)}, u32[]{:S(2)}) collective-permute-start(bf16[1168,256]{1,0:T(8,128)(2,1)} %collective-permute-done.1.refs_2_), channel_id=1, source_target_pairs={{0,4},{1,5},{2,6},{3,7},{4,8},{5,9},{6,10},{7,11},{8,12},{9,13},{1... | collective-permute-start | bytes 1794056 | tf_op jit(solution)/shard_map/ppermute | solution.py:366
  35.3 15.5 %collective-permute-start.11 = (bf16[1168,256]{1,0:T(8,128)(2,1)}, bf16[1168,256]{1,0:T(8,128)(2,1)}, u32[]{:S(2)}, u32[]{:S(2)}) collective-permute-start(bf16[1168,256]{1,0:T(8,128)(2,1)} %collective-permute-done.1.refs_2_), channel_id=1, source_target_pairs={{0,12},{1,13},{2,14},{3,15},{4,0},{5,1},{6,2},{7,3},{8,4},{9,5},{1... | collective-permute-start | bytes 1794056 | tf_op jit(solution)/shard_map/ppermute | solution.py:366
  38.5 18.7 %collective-permute-start.2 = (bf16[1168,256]{1,0:T(8,128)(2,1)}, bf16[1168,256]{1,0:T(8,128)(2,1)}, u32[]{:S(2)}, u32[]{:S(2)}) collective-permute-start(bf16[1168,256]{1,0:T(8,128)(2,1)} %collective-permute-done.1.refs_2_), channel_id=1, source_target_pairs={{0,1},{1,0},{2,3},{3,2},{4,5},{5,4},{6,7},{7,6},{8,9},{9,8},{10,11... | collective-permute-start | bytes 1794056 | tf_op jit(solution)/shard_map/ppermute | solution.py:358
  38.5 18.7 %collective-permute-start.4 = (bf16[1168,256]{1,0:T(8,128)(2,1)}, bf16[1168,256]{1,0:T(8,128)(2,1)}, u32[]{:S(2)}, u32[]{:S(2)}) collective-permute-start(bf16[1168,256]{1,0:T(8,128)(2,1)} %collective-permute-done.3.refs_4_), channel_id=1, source_target_pairs={{0,1},{1,0},{2,3},{3,2},{4,5},{5,4},{6,7},{7,6},{8,9},{9,8},{10,11... | collective-permute-start | bytes 1794056 | tf_op jit(solution)/shard_map/ppermute | solution.py:358
  39.0 18.2 %collective-permute-start.10 = (bf16[1168,256]{1,0:T(8,128)(2,1)}, bf16[1168,256]{1,0:T(8,128)(2,1)}, u32[]{:S(2)}, u32[]{:S(2)}) collective-permute-start(bf16[1168,256]{1,0:T(8,128)(2,1)} %collective-permute-done.9.refs_10_), channel_id=1, source_target_pairs={{0,1},{1,0},{2,3},{3,2},{4,5},{5,4},{6,7},{7,6},{8,9},{9,8},{10,11... | collective-permute-start | bytes 1794056 | tf_op jit(solution)/shard_map/ppermute | solution.py:358
  50.1 7.1 collective-permute-start.14
  50.8 6.4 collective-permute-start.12
  57.2 296.7 %copy-start.4 = (bf16[192,9216]{1,0:T(8,128)(2,1)S(1)}, bf16[192,9216]{1,0:T(8,128)(2,1)}, u32[]{:S(2)}) copy-start(bf16[192,9216]{1,0:T(8,128)(2,1)} %get-tuple-element.305.refs_0_) | copy-start | bytes 10616836
  375.1 8.4 collective-permute-start.15
  393.6 10.6 %collective-permute-start.16 = (bf16[16,9216]{1,0:T(8,128)(2,1)S(1)}, bf16[16,9216]{1,0:T(8,128)(2,1)S(1)}, u32[]{:S(2)}, u32[]{:S(2)}) collective-permute-start(bf16[16,9216]{1,0:T(8,128)(2,1)S(1)} %get-tuple-element.318), channel_id=1, source_target_pairs={{0,16},{16,32},{1,17},{17,33},{2,18},{18,34},{3,19},{19,35},{4,20}... | collective-permute-start | bytes 884744 | tf_op jit(solution)/shard_map/ppermute | solution.py:543
  410.0 9.8 collective-permute-start.17
  425.4 8.8 collective-permute-start.18
  439.8 8.6 collective-permute-start.19
  454.0 8.6 collective-permute-start.20
  462.6 38.0 %slice-start = ((s8[4423680]{0:T(1024)(128)(4,1)}), s8[4194304]{0:T(1024)(128)(4,1)S(1)}, s32[]{:S(2)}) async-start(s8[4423680]{0:T(1024)(128)(4,1)} %bitcast.82), calls=%async_computation | async-start | bytes 8388608
  462.6 38.0 %slice-start.2 = ((s8[4423680]{0:T(1024)(128)(4,1)}), s8[4194304]{0:T(1024)(128)(4,1)S(1)}, s32[]{:S(2)}) async-start(s8[4423680]{0:T(1024)(128)(4,1)} %bitcast.103), calls=%async_computation.2 | async-start | bytes 8388608
  468.2 8.6 collective-permute-start.21
  484.1 15.3 %collective-permute-start.22 = (bf16[16,9216]{1,0:T(8,128)(2,1)S(1)}, bf16[16,9216]{1,0:T(8,128)(2,1)S(1)}, u32[]{:S(2)}, u32[]{:S(2)}) collective-permute-start(bf16[16,9216]{1,0:T(8,128)(2,1)S(1)} %get-tuple-element.360), channel_id=1, source_target_pairs={{0,16},{16,32},{32,48},{48,64},{64,80},{80,96},{96,112},{1,17},{17... | collective-permute-start | bytes 884744 | tf_op jit(solution)/shard_map/ppermute | solution.py:543
  498.8 12.1 %collective-permute-start.24 = (bf16[16,9216]{1,0:T(8,128)(2,1)S(1)}, bf16[16,9216]{1,0:T(8,128)(2,1)S(1)}, u32[]{:S(2)}, u32[]{:S(2)}) collective-permute-start(bf16[16,9216]{1,0:T(8,128)(2,1)S(1)} %get-tuple-element.375), channel_id=1, source_target_pairs={{112,96},{113,97},{114,98},{115,99},{116,100},{117,101},{118,102},... | collective-permute-start | bytes 884744 | tf_op jit(solution)/shard_map/ppermute | solution.py:562
  507.8 12.1 %collective-permute-start.23 = (bf16[16,9216]{1,0:T(8,128)(2,1)S(1)}, bf16[16,9216]{1,0:T(8,128)(2,1)S(1)}, u32[]{:S(2)}, u32[]{:S(2)}) collective-permute-start(bf16[16,9216]{1,0:T(8,128)(2,1)S(1)} %get-tuple-element.374), channel_id=1, source_target_pairs={{0,16},{16,32},{32,48},{48,64},{64,80},{80,96},{96,112},{1,17},{17... | collective-permute-start | bytes 884744 | tf_op jit(solution)/shard_map/ppermute | solution.py:543
  519.2 15.4 %collective-permute-start.26 = (bf16[16,9216]{1,0:T(8,128)(2,1)S(1)}, bf16[16,9216]{1,0:T(8,128)(2,1)S(1)}, u32[]{:S(2)}, u32[]{:S(2)}) collective-permute-start(bf16[16,9216]{1,0:T(8,128)(2,1)S(1)} %get-tuple-element.390), channel_id=1, source_target_pairs={{96,80},{112,96},{97,81},{113,97},{98,82},{114,98},{99,83},{115,99... | collective-permute-start | bytes 884744 | tf_op jit(solution)/shard_map/ppermute | solution.py:562
  528.1 15.6 %collective-permute-start.25 = (bf16[16,9216]{1,0:T(8,128)(2,1)S(1)}, bf16[16,9216]{1,0:T(8,128)(2,1)S(1)}, u32[]{:S(2)}, u32[]{:S(2)}) collective-permute-start(bf16[16,9216]{1,0:T(8,128)(2,1)S(1)} %get-tuple-element.389), channel_id=1, source_target_pairs={{0,16},{16,32},{32,48},{48,64},{64,80},{80,96},{96,112},{1,17},{17... | collective-permute-start | bytes 884744 | tf_op jit(solution)/shard_map/ppermute | solution.py:543
  543.1 15.4 %collective-permute-start.28 = (bf16[16,9216]{1,0:T(8,128)(2,1)S(1)}, bf16[16,9216]{1,0:T(8,128)(2,1)S(1)}, u32[]{:S(2)}, u32[]{:S(2)}) collective-permute-start(bf16[16,9216]{1,0:T(8,128)(2,1)S(1)} %get-tuple-element.405), channel_id=1, source_target_pairs={{80,64},{96,80},{112,96},{81,65},{97,81},{113,97},{82,66},{98,82},... | collective-permute-start | bytes 884744 | tf_op jit(solution)/shard_map/ppermute | solution.py:562
  552.0 15.4 %collective-permute-start.27 = (bf16[16,9216]{1,0:T(8,128)(2,1)S(1)}, bf16[16,9216]{1,0:T(8,128)(2,1)S(1)}, u32[]{:S(2)}, u32[]{:S(2)}) collective-permute-start(bf16[16,9216]{1,0:T(8,128)(2,1)S(1)} %get-tuple-element.404), channel_id=1, source_target_pairs={{0,16},{16,32},{32,48},{48,64},{64,80},{80,96},{96,112},{1,17},{17... | collective-permute-start | bytes 884744 | tf_op jit(solution)/shard_map/ppermute | solution.py:543
  566.8 10.9 %collective-permute-start.30 = (bf16[16,9216]{1,0:T(8,128)(2,1)S(1)}, bf16[16,9216]{1,0:T(8,128)(2,1)S(1)}, u32[]{:S(2)}, u32[]{:S(2)}) collective-permute-start(bf16[16,9216]{1,0:T(8,128)(2,1)S(1)} %get-tuple-element.420), channel_id=1, source_target_pairs={{64,48},{80,64},{96,80},{112,96},{65,49},{81,65},{97,81},{113,97},... | collective-permute-start | bytes 884744 | tf_op jit(solution)/shard_map/ppermute | solution.py:562
  575.7 10.9 %collective-permute-start.29 = (bf16[16,9216]{1,0:T(8,128)(2,1)S(1)}, bf16[16,9216]{1,0:T(8,128)(2,1)S(1)}, u32[]{:S(2)}, u32[]{:S(2)}) collective-permute-start(bf16[16,9216]{1,0:T(8,128)(2,1)S(1)} %get-tuple-element.419), channel_id=1, source_target_pairs={{0,16},{16,32},{32,48},{48,64},{64,80},{80,96},{96,112},{1,17},{17... | collective-permute-start | bytes 884744 | tf_op jit(solution)/shard_map/ppermute | solution.py:543
  585.9 4.9 collective-permute-start.32
  590.2 10.0 %collective-permute-start.31 = (bf16[16,9216]{1,0:T(8,128)(2,1)S(1)}, bf16[16,9216]{1,0:T(8,128)(2,1)S(1)}, u32[]{:S(2)}, u32[]{:S(2)}) collective-permute-start(bf16[16,9216]{1,0:T(8,128)(2,1)S(1)} %get-tuple-element.434), channel_id=1, source_target_pairs={{16,32},{32,48},{48,64},{64,80},{80,96},{96,112},{17,33},{33,49},{... | collective-permute-start | bytes 884744 | tf_op jit(solution)/shard_map/ppermute | solution.py:543
  599.5 4.9 collective-permute-start.34
  603.8 10.2 %collective-permute-start.33 = (bf16[16,9216]{1,0:T(8,128)(2,1)S(1)}, bf16[16,9216]{1,0:T(8,128)(2,1)S(1)}, u32[]{:S(2)}, u32[]{:S(2)}) collective-permute-start(bf16[16,9216]{1,0:T(8,128)(2,1)S(1)} %get-tuple-element.449), channel_id=1, source_target_pairs={{32,48},{48,64},{64,80},{80,96},{96,112},{33,49},{49,65},{65,81},{... | collective-permute-start | bytes 884744 | tf_op jit(solution)/shard_map/ppermute | solution.py:543
  612.7 40.8 %collective-permute-start.36 = (bf16[16,9216]{1,0:T(8,128)(2,1)S(1)}, bf16[16,9216]{1,0:T(8,128)(2,1)S(1)}, u32[]{:S(2)}, u32[]{:S(2)}) collective-permute-start(bf16[16,9216]{1,0:T(8,128)(2,1)S(1)} %get-tuple-element.465), channel_id=1, source_target_pairs={{16,0},{32,16},{48,32},{64,48},{80,64},{96,80},{112,96},{17,1},{33... | collective-permute-start | bytes 884744 | tf_op jit(solution)/shard_map/ppermute | solution.py:562
  617.0 50.8 %collective-permute-start.35 = (bf16[16,9216]{1,0:T(8,128)(2,1)S(1)}, bf16[16,9216]{1,0:T(8,128)(2,1)S(1)}, u32[]{:S(2)}, u32[]{:S(2)}) collective-permute-start(bf16[16,9216]{1,0:T(8,128)(2,1)S(1)} %get-tuple-element.464), channel_id=1, source_target_pairs={{48,64},{64,80},{80,96},{96,112},{49,65},{65,81},{81,97},{97,113},... | collective-permute-start | bytes 884744 | tf_op jit(solution)/shard_map/ppermute | solution.py:543
  666.5 15.2 %collective-permute-start.38 = (bf16[16,9216]{1,0:T(8,128)(2,1)S(1)}, bf16[16,9216]{1,0:T(8,128)(2,1)S(1)}, u32[]{:S(2)}, u32[]{:S(2)}) collective-permute-start(bf16[16,9216]{1,0:T(8,128)(2,1)S(1)} %get-tuple-element.480), channel_id=1, source_target_pairs={{16,0},{32,16},{48,32},{64,48},{80,64},{96,80},{112,96},{17,1},{33... | collective-permute-start | bytes 884744 | tf_op jit(solution)/shard_map/ppermute | solution.py:562
  670.7 25.3 %collective-permute-start.37 = (bf16[16,9216]{1,0:T(8,128)(2,1)S(1)}, bf16[16,9216]{1,0:T(8,128)(2,1)S(1)}, u32[]{:S(2)}, u32[]{:S(2)}) collective-permute-start(bf16[16,9216]{1,0:T(8,128)(2,1)S(1)} %get-tuple-element.479), channel_id=1, source_target_pairs={{64,80},{80,96},{96,112},{65,81},{81,97},{97,113},{66,82},{82,98},... | collective-permute-start | bytes 884744 | tf_op jit(solution)/shard_map/ppermute | solution.py:543
  694.7 10.7 %collective-permute-start.40 = (bf16[16,9216]{1,0:T(8,128)(2,1)S(1)}, bf16[16,9216]{1,0:T(8,128)(2,1)S(1)}, u32[]{:S(2)}, u32[]{:S(2)}) collective-permute-start(bf16[16,9216]{1,0:T(8,128)(2,1)S(1)} %get-tuple-element.495), channel_id=1, source_target_pairs={{16,0},{32,16},{48,32},{64,48},{80,64},{96,80},{112,96},{17,1},{33... | collective-permute-start | bytes 884744 | tf_op jit(solution)/shard_map/ppermute | solution.py:562
  699.0 20.6 %collective-permute-start.39 = (bf16[16,9216]{1,0:T(8,128)(2,1)S(1)}, bf16[16,9216]{1,0:T(8,128)(2,1)S(1)}, u32[]{:S(2)}, u32[]{:S(2)}) collective-permute-start(bf16[16,9216]{1,0:T(8,128)(2,1)S(1)} %get-tuple-element.494), channel_id=1, source_target_pairs={{80,96},{96,112},{81,97},{97,113},{82,98},{98,114},{83,99},{99,115... | collective-permute-start | bytes 884744 | tf_op jit(solution)/shard_map/ppermute | solution.py:543
  718.3 15.2 %collective-permute-start.42 = (bf16[16,9216]{1,0:T(8,128)(2,1)S(1)}, bf16[16,9216]{1,0:T(8,128)(2,1)S(1)}, u32[]{:S(2)}, u32[]{:S(2)}) collective-permute-start(bf16[16,9216]{1,0:T(8,128)(2,1)S(1)} %get-tuple-element.510), channel_id=1, source_target_pairs={{16,0},{32,16},{48,32},{64,48},{80,64},{96,80},{112,96},{17,1},{33... | collective-permute-start | bytes 884744 | tf_op jit(solution)/shard_map/ppermute | solution.py:562
  722.6 25.1 %collective-permute-start.41 = (bf16[16,9216]{1,0:T(8,128)(2,1)S(1)}, bf16[16,9216]{1,0:T(8,128)(2,1)S(1)}, u32[]{:S(2)}, u32[]{:S(2)}) collective-permute-start(bf16[16,9216]{1,0:T(8,128)(2,1)S(1)} %get-tuple-element.509), channel_id=1, source_target_pairs={{96,112},{97,113},{98,114},{99,115},{100,116},{101,117},{102,118},... | collective-permute-start | bytes 884744 | tf_op jit(solution)/shard_map/ppermute | solution.py:543
  746.4 10.7 %collective-permute-start.43 = (bf16[16,9216]{1,0:T(8,128)(2,1)S(1)}, bf16[16,9216]{1,0:T(8,128)(2,1)S(1)}, u32[]{:S(2)}, u32[]{:S(2)}) collective-permute-start(bf16[16,9216]{1,0:T(8,128)(2,1)S(1)} %get-tuple-element.525), channel_id=1, source_target_pairs={{16,0},{32,16},{48,32},{64,48},{80,64},{96,80},{112,96},{17,1},{33... | collective-permute-start | bytes 884744 | tf_op jit(solution)/shard_map/ppermute | solution.py:562
  767.9 10.7 %collective-permute-start.44 = (bf16[16,9216]{1,0:T(8,128)(2,1)S(1)}, bf16[16,9216]{1,0:T(8,128)(2,1)S(1)}, u32[]{:S(2)}, u32[]{:S(2)}) collective-permute-start(bf16[16,9216]{1,0:T(8,128)(2,1)S(1)} %get-tuple-element.533), channel_id=1, source_target_pairs={{16,0},{32,16},{48,32},{64,48},{80,64},{96,80},{112,96},{17,1},{33... | collective-permute-start | bytes 884744 | tf_op jit(solution)/shard_map/ppermute | solution.py:562
  784.1 10.9 %collective-permute-start.45 = (bf16[16,9216]{1,0:T(8,128)(2,1)S(1)}, bf16[16,9216]{1,0:T(8,128)(2,1)S(1)}, u32[]{:S(2)}, u32[]{:S(2)}) collective-permute-start(bf16[16,9216]{1,0:T(8,128)(2,1)S(1)} %get-tuple-element.541), channel_id=1, source_target_pairs={{16,0},{32,16},{48,32},{64,48},{80,64},{96,80},{17,1},{33,17},{49,... | collective-permute-start | bytes 884744 | tf_op jit(solution)/shard_map/ppermute | solution.py:562
  800.6 12.2 %collective-permute-start.46 = (bf16[16,9216]{1,0:T(8,128)(2,1)S(1)}, bf16[16,9216]{1,0:T(8,128)(2,1)S(1)}, u32[]{:S(2)}, u32[]{:S(2)}) collective-permute-start(bf16[16,9216]{1,0:T(8,128)(2,1)S(1)} %get-tuple-element.549), channel_id=1, source_target_pairs={{16,0},{32,16},{48,32},{64,48},{80,64},{17,1},{33,17},{49,33},{65,... | collective-permute-start | bytes 884744 | tf_op jit(solution)/shard_map/ppermute | solution.py:562
  818.4 13.7 %collective-permute-start.47 = (bf16[16,9216]{1,0:T(8,128)(2,1)S(1)}, bf16[16,9216]{1,0:T(8,128)(2,1)S(1)}, u32[]{:S(2)}, u32[]{:S(2)}) collective-permute-start(bf16[16,9216]{1,0:T(8,128)(2,1)S(1)} %get-tuple-element.557), channel_id=1, source_target_pairs={{16,0},{32,16},{48,32},{64,48},{17,1},{33,17},{49,33},{65,49},{18,... | collective-permute-start | bytes 884744 | tf_op jit(solution)/shard_map/ppermute | solution.py:562
  837.6 14.4 %collective-permute-start.48 = (bf16[16,9216]{1,0:T(8,128)(2,1)S(1)}, bf16[16,9216]{1,0:T(8,128)(2,1)S(1)}, u32[]{:S(2)}, u32[]{:S(2)}) collective-permute-start(bf16[16,9216]{1,0:T(8,128)(2,1)S(1)} %get-tuple-element.565), channel_id=1, source_target_pairs={{16,0},{32,16},{48,32},{17,1},{33,17},{49,33},{18,2},{34,18},{50,3... | collective-permute-start | bytes 884744 | tf_op jit(solution)/shard_map/ppermute | solution.py:562
  857.5 9.8 collective-permute-start.49
  880.1 8.9 collective-permute-start.50
  931.9 4.7 collective-permute-start.52
  935.5 22.5 %collective-permute-start.51 = (bf16[4,1168,256]{2,1,0:T(8,128)(2,1)S(1)}, bf16[4,1168,256]{2,1,0:T(8,128)(2,1)S(1)}, u32[]{:S(2)}, u32[]{:S(2)}) collective-permute-start(bf16[4,1168,256]{2,1,0:T(8,128)(2,1)S(1)} %get-tuple-element.596), channel_id=1, source_target_pairs={{0,1},{1,0},{2,3},{3,2},{4,5},{5,4},{6,7},{7,6},{8,9},{9,8},{10,11... | collective-permute-start | bytes 7176200 | tf_op jit(solution)/shard_map/ppermute | solution.py:358
  937.2 22.8 %collective-permute-start.58 = (bf16[1168,256]{1,0:T(8,128)(2,1)S(1)}, bf16[1168,256]{1,0:T(8,128)(2,1)S(1)}, u32[]{:S(2)}, u32[]{:S(2)}) collective-permute-start(bf16[1168,256]{1,0:T(8,128)(2,1)S(1)} %get-tuple-element.600), channel_id=1, source_target_pairs={{0,12},{1,13},{2,14},{3,15},{4,0},{5,1},{6,2},{7,3},{8,4},{9,5},{1... | collective-permute-start | bytes 1794056 | tf_op jit(solution)/shard_map/ppermute | solution.py:366
  944.6 25.5 %collective-permute-start.57 = (bf16[1168,256]{1,0:T(8,128)(2,1)S(1)}, bf16[1168,256]{1,0:T(8,128)(2,1)S(1)}, u32[]{:S(2)}, u32[]{:S(2)}) collective-permute-start(bf16[1168,256]{1,0:T(8,128)(2,1)S(1)} %get-tuple-element.601), channel_id=1, source_target_pairs={{0,4},{1,5},{2,6},{3,7},{4,8},{5,9},{6,10},{7,11},{8,12},{9,13},{1... | collective-permute-start | bytes 1794056 | tf_op jit(solution)/shard_map/ppermute | solution.py:366
  953.5 16.8 %collective-permute-start.55 = (bf16[1168,256]{1,0:T(8,128)(2,1)S(1)}, bf16[1168,256]{1,0:T(8,128)(2,1)S(1)}, u32[]{:S(2)}, u32[]{:S(2)}) collective-permute-start(bf16[1168,256]{1,0:T(8,128)(2,1)S(1)} %get-tuple-element.602), channel_id=1, source_target_pairs={{0,2},{1,3},{2,0},{3,1},{4,6},{5,7},{6,4},{7,5},{8,10},{9,11},{10,... | collective-permute-start | bytes 1794056 | tf_op jit(solution)/shard_map/ppermute | solution.py:362
  956.5 26.2 %collective-permute-start.53 = (bf16[1168,256]{1,0:T(8,128)(2,1)S(1)}, bf16[1168,256]{1,0:T(8,128)(2,1)S(1)}, u32[]{:S(2)}, u32[]{:S(2)}) collective-permute-start(bf16[1168,256]{1,0:T(8,128)(2,1)S(1)} %get-tuple-element.599), channel_id=1, source_target_pairs={{0,4},{1,5},{2,6},{3,7},{4,8},{5,9},{6,10},{7,11},{8,12},{9,13},{1... | collective-permute-start | bytes 1794056 | tf_op jit(solution)/shard_map/ppermute | solution.py:366
  958.2 24.5 %collective-permute-start.54 = (bf16[1168,256]{1,0:T(8,128)(2,1)S(1)}, bf16[1168,256]{1,0:T(8,128)(2,1)S(1)}, u32[]{:S(2)}, u32[]{:S(2)}) collective-permute-start(bf16[1168,256]{1,0:T(8,128)(2,1)S(1)} %fusion.7), channel_id=1, source_target_pairs={{0,12},{1,13},{2,14},{3,15},{4,0},{5,1},{6,2},{7,3},{8,4},{9,5},{1... | collective-permute-start | bytes 1794056 | tf_op jit(solution)/shard_map/ppermute | solution.py:366
  970.9 24.7 %collective-permute-start.56 = (bf16[1168,256]{1,0:T(8,128)(2,1)S(1)}, bf16[1168,256]{1,0:T(8,128)(2,1)S(1)}, u32[]{:S(2)}, u32[]{:S(2)}) collective-permute-start(bf16[1168,256]{1,0:T(8,128)(2,1)S(1)} %get-tuple-element.603), channel_id=1, source_target_pairs={{0,8},{1,9},{2,10},{3,11},{4,12},{5,13},{6,14},{7,15},{8,0},{9,1},... | collective-permute-start | bytes 1794056 | tf_op jit(solution)/shard_map/ppermute | solution.py:366
  974.1 21.5 %collective-permute-start.59 = (bf16[1168,256]{1,0:T(8,128)(2,1)S(1)}, bf16[1168,256]{1,0:T(8,128)(2,1)S(1)}, u32[]{:S(2)}, u32[]{:S(2)}) collective-permute-start(bf16[1168,256]{1,0:T(8,128)(2,1)S(1)} %get-tuple-element.604), channel_id=1, source_target_pairs={{0,2},{1,3},{2,0},{3,1},{4,6},{5,7},{6,4},{7,5},{8,10},{9,11},{10,... | collective-permute-start | bytes 1794056 | tf_op jit(solution)/shard_map/ppermute | solution.py:362
  (146 other events, 407.4 us)

commit v2 on v1

--- a/solution.py
+++ b/solution.py
@@ -30,15 +30,25 @@
 
 VM = pl.BlockSpec(memory_space=pltpu.VMEM)
 SM = pl.BlockSpec(memory_space=pltpu.SMEM)
-ANY = pl.BlockSpec(memory_space=pl.ANY)
+ANY = pl.BlockSpec(memory_space=pltpu.HBM)
 NT = (((1,), (1,)), ((), ()))
 TN = (((0,), (0,)), ((), ()))
 F32 = jnp.float32
 BF16 = jnp.bfloat16
 
 
+def in_hbm(value):
+    return pltpu.with_memory_space_constraint(value, pltpu.HBM)
+
+
 def lane_sum(values):
     return jnp.sum(values, axis=-1, keepdims=True)
+
+
+def gain_row(gain, start, size):
+    first = start // BLOCK
+    rows = [gain[first + number : first + number + 1, :] for number in range(size // BLOCK)]
+    return jnp.concatenate(rows, axis=1)
 
 
 def clipped(values, limits, start):
@@ -116,7 +126,7 @@
         for start in range(0, WIDTH, WIDE):
             span = slice(start, start + WIDE)
             values = (layer[:, span].astype(F32) - mean) * scale
-            values = (values * gain[:, span]).astype(BF16)
+            values = (values * gain_row(gain, start, WIDE)).astype(BF16)
             normed[:, span] = values
             result += jnp.dot(values, down[span, :], preferred_element_type=F32)
         stores[4].start()
@@ -155,8 +165,11 @@
     *refs,
 ):
     (outs, scratch) = (refs[4:12], refs[12:])
-    grad_all, cot_all, neckcot_all, gain_all, sent = outs[3:]
-    cot, bound, layer, neck, stat, grad, neckcot, gains, hold, sems = scratch
+    gain_before = refs[3]
+    grad_all, cot_all, neckcot_all, gain_sums, sent = outs[3:]
+    cot, bound, layer, neck, stat, grad, neckcot, hold, sems = scratch
+
+    gain_sums[...] = gain_before[...]
 
     @pl.when(table[tick, 3] == 1)
     def _():
@@ -175,9 +188,6 @@
             pltpu.make_async_copy(grad, grad_all.at[here, :], sems.at[4]),
             pltpu.make_async_copy(cot, cot_all.at[here, :], sems.at[5]),
             pltpu.make_async_copy(neckcot, neckcot_all.at[here, :], sems.at[6]),
-            pltpu.make_async_copy(
-                gains, gain_all.at[pl.ds(pl.multiple_of(row // 2, 8), 8), :], sems.at[7]
-            ),
         ]
 
         @pl.when(last)
@@ -214,14 +224,13 @@
             wide = lax.dot_general(small, down[span, :], NT, preferred_element_type=F32)
             centred = (layer[:, span].astype(F32) - mean) * scale
             product = wide * centred
-            gains[:, span] = product[:8, :] + product[8:, :]
-            scaled = wide * gain[:, span]
+            gain_sums[:, span] += product[:8, :] + product[8:, :]
+            scaled = wide * gain_row(gain, start, MEDIUM)
             hold[:, span] = scaled
             product = scaled * centred
             for offset in range(0, MEDIUM, BLOCK):
                 first += scaled[:, offset : offset + BLOCK]
                 second += product[:, offset : offset + BLOCK]
-        stores[3].start()
         first = lane_sum(first) * (1.0 / WIDTH)
         second = lane_sum(second) * (1.0 / WIDTH)
         loads[0].wait()
@@ -262,10 +271,10 @@
             pltpu.SemaphoreType.DMA((9,)),
         ],
         input_output_aliases={8 + number: number for number in range(6)},
-        compiler_params=call_params(24),
+        compiler_params=call_params(8),
         cost_estimate=pl.CostEstimate(flops=150_000_000, bytes_accessed=9_000_000, transcendentals=0),
         name="section_forward",
-    )(table, incoming, gain, down, up, base_in, base_out, limits, *state)
+    )(table, incoming, gain, down, up, in_hbm(base_in), in_hbm(base_out), limits, *map(in_hbm, state))
     return got[:6], got[6]
 
 
@@ -276,8 +285,8 @@
     got = pl.pallas_call(
         functools.partial(backward_kernel, tick),
         out_shape=outs,
-        in_specs=[SM, VM, VM, VM, VM, ANY, ANY] + [ANY] * 7,
-        out_specs=[ANY] * 7 + [VM],
+        in_specs=[SM, VM, VM, VM, VM, ANY, ANY] + [ANY] * 6 + [VM],
+        out_specs=[ANY] * 6 + [VM, VM],
         scratch_shapes=[
             pltpu.VMEM((ROWS, WIDTH), BF16),
             pltpu.VMEM((ROWS, WIDTH // BLOCK), F32),
@@ -286,15 +295,14 @@
             pltpu.VMEM((ROWS, 2 * BLOCK), F32),
             pltpu.VMEM((ROWS, WIDTH), BF16),
             pltpu.VMEM((ROWS, NECK), BF16),
-            pltpu.VMEM((8, WIDTH), F32),
             pltpu.VMEM((ROWS, WIDTH), F32),
             pltpu.SemaphoreType.DMA((9,)),
         ],
         input_output_aliases={7 + number: number for number in range(7)},
-        compiler_params=call_params(24),
+        compiler_params=call_params(8),
         cost_estimate=pl.CostEstimate(flops=150_000_000, bytes_accessed=9_000_000, transcendentals=0),
         name="section_backward",
-    )(table, incoming, gain, down, up, loss_grad, limits, *kept)
+    )(table, incoming, gain, down, up, in_hbm(loss_grad), limits, *map(in_hbm, kept[:-1]), kept[-1])
     return got[:3], got[3:7], got[7]
 
 
@@ -308,21 +316,17 @@
 
 
 def assemble_kernel(place, *refs):
-    parts, outs, sems = refs[:16], refs[16:19], refs[19]
-    copies = []
+    parts, (down, up, gain) = refs[:16], refs[16:]
+    per = 2 * SHARD // BLOCK
     for number, part in enumerate(parts):
         shard = place[number]
-        for which, (start, size) in enumerate(((0, SHARD), (SHARD, SHARD), (2 * SHARD, EXTRA))):
-            target = outs[which].at[pl.ds(pl.multiple_of(shard * size, 16), size), :]
-            copies.append(
-                pltpu.make_async_copy(
-                    part.at[pl.ds(start, size), :], target, sems.at[number * 3 + which]
-                )
-            )
-    for copy in copies:
-        copy.start()
-    for copy in copies:
-        copy.wait()
+        rows = pl.ds(pl.multiple_of(shard * SHARD, SHARD), SHARD)
+        down[rows, :] = part[:SHARD, :]
+        up[rows, :] = part[SHARD : 2 * SHARD, :]
+        if number % 2 == 0:
+            piece = part[2 * SHARD :, :BLOCK].astype(F32)
+            for line in range(per):
+                gain[pl.ds((shard >> 1) * per + line, 1), :] = piece[line : line + 1, :]
 
 
 def assemble(place, parts):
@@ -331,11 +335,11 @@
         out_shape=[
             jax.ShapeDtypeStruct((WIDTH, NECK), BF16),
             jax.ShapeDtypeStruct((WIDTH, NECK), BF16),
-            jax.ShapeDtypeStruct((16 * EXTRA, NECK), BF16),
+            jax.ShapeDtypeStruct((WIDTH // BLOCK, BLOCK), F32),
         ],
-        in_specs=[SM] + [ANY] * 16,
-        out_specs=[ANY] * 3,
-        scratch_shapes=[pltpu.SemaphoreType.DMA((48,))],
+        in_specs=[SM] + [VM] * 16,
+        out_specs=[VM] * 3,
+        compiler_params=call_params(8),
         cost_estimate=pl.CostEstimate(flops=0, bytes_accessed=19_000_000, transcendentals=0),
         name="assemble_weights",
     )(place, *parts)
@@ -388,8 +392,13 @@
         rows = slice(number * SHARD, (number + 1) * SHARD)
         mine[0, rows, :] = hold[pl.ds(pl.multiple_of(core * SHARD, SHARD), SHARD), :]
         theirs[0, rows, :] = hold[pl.ds(pl.multiple_of((1 - core) * SHARD, SHARD), SHARD), :]
-    mine[0, both:, :] = gains[0, core]
-    theirs[0, both:, :] = gains[0, 1 - core]
+    sums = jnp.sum(gains[...], axis=0, keepdims=True) * factor
+    lines = [sums[:, start : start + BLOCK] for start in range(0, both, BLOCK)]
+    lines.append(jnp.zeros((EXTRA - len(lines), BLOCK), F32))
+    lines = jnp.concatenate(lines, axis=0).astype(BF16)
+    lines = jnp.concatenate([lines, lines], axis=1)
+    mine[0, both:, :] = lines
+    theirs[0, both:, :] = lines
 
 
 def gradient_blocks(order, first, count, normed, neckcot, cot, act, gains):
@@ -407,15 +416,15 @@
                 small,
                 block,
                 small,
-                pl.BlockSpec((1, 2, EXTRA, NECK), lambda i, order: (order[first + i], 0, 0, 0)),
+                pl.BlockSpec((8, 2 * SHARD), lambda i, order: (0, order[first + i])),
             ],
             out_specs=[result, result],
             scratch_shapes=[pltpu.VMEM((2 * SHARD, NECK), BF16)],
         ),
         out_shape=[jax.ShapeDtypeStruct((count, 2 * SHARD + EXTRA, NECK), BF16)] * 2,
-        compiler_params=call_params(24),
+        compiler_params=call_params(8),
         name="gradient_blocks",
-    )(order, normed, neckcot, cot, act, gains)
+    )(order, in_hbm(normed), neckcot, in_hbm(cot), act, gains)
 
 
 REDUCE_ORDER = ((1, 1), (3, 1), (2, 1), (1, 0), (3, 0), (2, 0), (0, 1), (0, 0))
@@ -470,7 +479,13 @@
     tokens = MICRO * TOKENS
     ticks = CHUNKS + 2 * SECTIONS - 2
 
-    gain_rows = jnp.pad(norm_gain[0], (0, EXTRA * NECK - SHARD)).reshape(EXTRA, NECK)
+    other = to_core(norm_gain)
+    pair = jnp.where(
+        core == 0,
+        jnp.concatenate([norm_gain, other], axis=1),
+        jnp.concatenate([other, norm_gain], axis=1),
+    ).reshape(2 * SHARD // BLOCK, BLOCK)
+    gain_rows = jnp.pad(pair, ((0, EXTRA - pair.shape[0]), (0, NECK - BLOCK)))
     own = jnp.concatenate([down_weight[0], up_weight[0], gain_rows], axis=0)
     parts = gather_parts(own)
     pieces, places = [], []
@@ -479,7 +494,6 @@
         pieces += [part, to_core(part)]
         places += [spot, spot + 1 - 2 * core]
     down, up, gain = assemble(jnp.stack(places).astype(jnp.int32), pieces)
-    gain = gain.reshape(16, EXTRA * NECK)[:, :SHARD].reshape(1, WIDTH).astype(F32)
 
     tick = jnp.arange(ticks, dtype=jnp.int32)
 
@@ -518,11 +532,10 @@
             ((tokens, WIDTH), BF16),
             ((tokens, WIDTH), BF16),
             ((tokens, NECK), BF16),
-            ((tokens // 2, WIDTH), F32),
         ]
     )
     layer, out, neck, act, normed, stat = buffers[:6]
-    cots = buffers[6:]
+    cots = [*buffers[6:], jnp.zeros((8, WIDTH), F32)]
     zero = jnp.zeros((ROWS, WIDTH), BF16)
     arriving, returning = zero, zero
     for step in range(ticks):
@@ -562,19 +575,18 @@
             returning = lax.ppermute(sent, "section", pairs) if pairs else zero
 
     grad, cot, neckcot, gain_sums = cots
-    factor = 1.0 / math.sqrt(tokens * 16)
-    gains = (jnp.sum(gain_sums, axis=0) * factor).astype(BF16).reshape(8, 2, SHARD)
-    gains = jnp.pad(gains, ((0, 0), (0, 0), (0, EXTRA * NECK - SHARD))).reshape(8, 2, EXTRA, NECK)
     order = [((y + dy) & 3) * 2 + (z ^ dz) for dy, dz in REDUCE_ORDER] + [core]
     order = jnp.stack(order).astype(jnp.int32)
-    total = reduce_parts(order, normed, neckcot, cot, act, gains)
+    total = reduce_parts(order, normed, neckcot, cot, act, gain_sums)
     shape = (1, MICRO, TOKENS, WIDTH)
     return (
         out.reshape(shape),
         grad.reshape(shape),
         total[None, :SHARD],
         total[None, SHARD : 2 * SHARD],
-        total[2 * SHARD :].reshape(1, EXTRA * NECK)[:, :SHARD],
+        lax.dynamic_slice_in_dim(
+            total[2 * SHARD : 2 * SHARD + 9, :BLOCK].reshape(1, 2 * SHARD), core * SHARD, SHARD, 1
+        ),
     )
 
 

time: 1010 us -> 588 us (0.58)
  Pallas kernels: 449 us -> 169 us
  local copies, waits for them, and re-layouts: 179 us -> 11.1 us
  waiting for transfers between devices: 233 us -> 259 us
    pallas_call x1, Pallas kernels: 292 us -> 3.32 us  [assemble(): pl.pallas_call(assemble_kernel, out_shape=[jax.ShapeDtypeStruct((WIDTH, N...]
    unnamed x302 -> x22, local copies, waits for them, and re-layouts: 167 us -> 7.52 us
    ppermute x18, waiting for transfers between devices: 139 us -> 153 us  [shards(): returning = lax.ppermute(sent, 'section', pairs) if pairs else zero]
    ppermute x18, waiting for transfers between devices: 35.7 us -> 48.3 us  [shards(): arriving = lax.ppermute(delivered, 'section', pairs) if pairs else zero]
  transfers between devices with their start and end apart: 60 -> 61, of which waited for: 30 -> 35; matrix products, arithmetic and copies ran while one was open for 1% -> 2% of each run, Pallas kernels for 6% -> 11%
where the time goes in v2:
time: 588 us; the launch traced here: 579 us
  waiting for transfers between devices  259 us (44%)
  Pallas kernels  169 us (29%)
  starting transfers between devices  127 us (22%)
  other arithmetic  11.1 us (2%)
  local copies, waits for them, and re-layouts  11.1 us (2%)
    ppermute x18, waiting for transfers between devices, shards(): returning = lax.ppermute(sent, 'section', pairs) if pairs else zero  153 us
    pallas_call x19, Pallas kernels, forward_call(): pl.pallas_call(functools.partial(forward_kernel, tick), out_shape=outs, i...  83.1 us
    pallas_call x19, Pallas kernels, backward_call(): pl.pallas_call(functools.partial(backward_kernel, tick), out_shape=outs,...  72.9 us
    ppermute x18, starting transfers between devices, shards(): arriving = lax.ppermute(delivered, 'section', pairs) if pairs else zero  58.9 us
    ppermute x10, waiting for transfers between devices, along_y(): lax.ppermute(value, 'fsdp', fsdp_pairs(lambda y, z, core: ((y + by) % 4,...  54 us
    ppermute x18, waiting for transfers between devices, shards(): arriving = lax.ppermute(delivered, 'section', pairs) if pairs else zero  48.3 us
    ppermute x10, starting transfers between devices, along_y(): lax.ppermute(value, 'fsdp', fsdp_pairs(lambda y, z, core: ((y + by) % 4,...  32.4 us
    ppermute x18, starting transfers between devices, shards(): returning = lax.ppermute(sent, 'section', pairs) if pairs else zero  19.6 us
  transfers between devices with their start and end apart: 61, of which 35 were waited for; matrix products, arithmetic and copies ran while one was open for 2% of the time, Pallas kernels for 11%

profile of v2, /device:TPU:0, one launch (start us, length us, event | category | flops | bytes accessed | tf_op | source)
XLA Modules:
  0.0 578.7 jit_solution(5354281163776718077)
XLA Ops:
  14.5 7.5 %collective-permute-done.8.refs_8_ = bf16[1168,256]{1,0:T(8,128)(2,1)S(1)} collective-permute-done((bf16[1168,256]{1,0:T(8,128)(2,1)S(1)}, bf16[1168,256]{1,0:T(8,128)(2,1)S(1)}, u32[]{:S(2)}, u32[]{:S(2)}) %collective-permute-start.8) | collective-permute-done | bytes 598048 | tf_op jit(solution)/shard_map/ppermute | solution.py:370
  26.0 8.1 %collective-permute-done.6.refs_6_ = bf16[1168,256]{1,0:T(8,128)(2,1)S(1)} collective-permute-done((bf16[1168,256]{1,0:T(8,128)(2,1)S(1)}, bf16[1168,256]{1,0:T(8,128)(2,1)S(1)}, u32[]{:S(2)}, u32[]{:S(2)}) %collective-permute-start.6) | collective-permute-done | bytes 598048 | tf_op jit(solution)/shard_map/ppermute | solution.py:370
  41.0 10.7 %collective-permute-done.14.refs_14_ = bf16[1168,256]{1,0:T(8,128)(2,1)} collective-permute-done((bf16[1168,256]{1,0:T(8,128)(2,1)S(1)}, bf16[1168,256]{1,0:T(8,128)(2,1)}, u32[]{:S(2)}, u32[]{:S(2)}) %collective-permute-start.14) | collective-permute-done | bytes 598048 | tf_op jit(solution)/shard_map/ppermute | solution.py:370
  62.4 6.5 %section_forward.19 = (bf16[192,9216]{1,0:T(8,128)(2,1)}, bf16[192,9216]{1,0:T(8,128)(2,1)}, f32[192,256]{1,0:T(8,128)}, bf16[192,256]{1,0:T(8,128)(2,1)}, bf16[...) custom-call(s32[26,6]{1,0:T(8,128)S(1)} %copy.290.table, ...), custom_call_target="tpu_custom_call", output_to_operand_aliasing={{0}: (8, {}), {1}: (9, {}), {2}: (10, {}), {3}: (11, {}), {... | custom-call | flops 150000000 | bytes 9000000 | tf_op jit(solution)/shard_map/section_forward/pallas_call | solution.py:256
  70.2 7.1 %collective-permute-done.16.incoming = bf16[16,9216]{1,0:T(8,128)(2,1)S(1)} collective-permute-done((bf16[16,9216]{1,0:T(8,128)(2,1)S(1)}, bf16[16,9216]{1,0:T(8,128)(2,1)S(1)}, u32[]{:S(2)}, u32[]{:S(2)}) %collective-permute-start.16) | collective-permute-done | bytes 294944 | tf_op jit(solution)/shard_map/ppermute | solution.py:556
  77.3 6.3 %section_forward.20 = (bf16[192,9216]{1,0:T(8,128)(2,1)}, bf16[192,9216]{1,0:T(8,128)(2,1)}, f32[192,256]{1,0:T(8,128)}, bf16[192,256]{1,0:T(8,128)(2,1)}, bf16[...) custom-call(s32[26,6]{1,0:T(8,128)S(1)} %copy.290.table, ...), custom_call_target="tpu_custom_call", output_to_operand_aliasing={{0}: (8, {}), {1}: (9, {}), {2}: (10, {}), {3}: (11, {}), {... | custom-call | flops 150000000 | bytes 9000000 | tf_op jit(solution)/shard_map/section_forward/pallas_call | solution.py:256
  83.6 4.4 collective-permute-start.17
  88.0 6.2 %collective-permute-done.17.incoming = bf16[16,9216]{1,0:T(8,128)(2,1)S(1)} collective-permute-done((bf16[16,9216]{1,0:T(8,128)(2,1)S(1)}, bf16[16,9216]{1,0:T(8,128)(2,1)S(1)}, u32[]{:S(2)}, u32[]{:S(2)}) %collective-permute-start.17) | collective-permute-done | bytes 294944 | tf_op jit(solution)/shard_map/ppermute | solution.py:556
  94.2 6.5 %section_forward.21 = (bf16[192,9216]{1,0:T(8,128)(2,1)}, bf16[192,9216]{1,0:T(8,128)(2,1)}, f32[192,256]{1,0:T(8,128)}, bf16[192,256]{1,0:T(8,128)(2,1)}, bf16[...) custom-call(s32[26,6]{1,0:T(8,128)S(1)} %copy.290.table, ...), custom_call_target="tpu_custom_call", output_to_operand_aliasing={{0}: (8, {}), {1}: (9, {}), {2}: (10, {}), {3}: (11, {}), {... | custom-call | flops 150000000 | bytes 9000000 | tf_op jit(solution)/shard_map/section_forward/pallas_call | solution.py:256
  100.7 4.4 collective-permute-start.18
  105.1 5.3 collective-permute-done.18.incoming
  110.4 6.3 %section_forward.22 = (bf16[192,9216]{1,0:T(8,128)(2,1)}, bf16[192,9216]{1,0:T(8,128)(2,1)}, f32[192,256]{1,0:T(8,128)}, bf16[192,256]{1,0:T(8,128)(2,1)}, bf16[...) custom-call(s32[26,6]{1,0:T(8,128)S(1)} %copy.290.table, ...), custom_call_target="tpu_custom_call", output_to_operand_aliasing={{0}: (8, {}), {1}: (9, {}), {2}: (10, {}), {3}: (11, {}), {... | custom-call | flops 150000000 | bytes 9000000 | tf_op jit(solution)/shard_map/section_forward/pallas_call | solution.py:256
  116.7 4.4 collective-permute-start.19
  121.1 4.4 collective-permute-done.19.incoming
  125.6 6.3 %section_forward.23 = (bf16[192,9216]{1,0:T(8,128)(2,1)}, bf16[192,9216]{1,0:T(8,128)(2,1)}, f32[192,256]{1,0:T(8,128)}, bf16[192,256]{1,0:T(8,128)(2,1)}, bf16[...) custom-call(s32[26,6]{1,0:T(8,128)S(1)} %copy.290.table, ...), custom_call_target="tpu_custom_call", output_to_operand_aliasing={{0}: (8, {}), {1}: (9, {}), {2}: (10, {}), {3}: (11, {}), {... | custom-call | flops 150000000 | bytes 9000000 | tf_op jit(solution)/shard_map/section_forward/pallas_call | solution.py:256
  131.8 4.4 collective-permute-start.20
  136.2 4.2 collective-permute-done.20.incoming
  140.5 6.3 %section_forward.24 = (bf16[192,9216]{1,0:T(8,128)(2,1)}, bf16[192,9216]{1,0:T(8,128)(2,1)}, f32[192,256]{1,0:T(8,128)}, bf16[192,256]{1,0:T(8,128)(2,1)}, bf16[...) custom-call(s32[26,6]{1,0:T(8,128)S(1)} %copy.290.table, ...), custom_call_target="tpu_custom_call", output_to_operand_aliasing={{0}: (8, {}), {1}: (9, {}), {2}: (10, {}), {3}: (11, {}), {... | custom-call | flops 150000000 | bytes 9000000 | tf_op jit(solution)/shard_map/section_forward/pallas_call | solution.py:256
  146.7 4.4 collective-permute-start.21
  151.1 4.2 collective-permute-done.21.incoming
  155.3 6.3 %section_forward.25 = (bf16[192,9216]{1,0:T(8,128)(2,1)}, bf16[192,9216]{1,0:T(8,128)(2,1)}, f32[192,256]{1,0:T(8,128)}, bf16[192,256]{1,0:T(8,128)(2,1)}, bf16[...) custom-call(s32[26,6]{1,0:T(8,128)S(1)} %copy.290.table, ...), custom_call_target="tpu_custom_call", output_to_operand_aliasing={{0}: (8, {}), {1}: (9, {}), {2}: (10, {}), {3}: (11, {}), {... | custom-call | flops 150000000 | bytes 9000000 | tf_op jit(solution)/shard_map/section_forward/pallas_call | solution.py:256
  161.6 4.4 collective-permute-start.22
  166.1 4.1 collective-permute-done.22.incoming
  170.2 6.7 %section_forward.26 = (bf16[192,9216]{1,0:T(8,128)(2,1)}, bf16[192,9216]{1,0:T(8,128)(2,1)}, f32[192,256]{1,0:T(8,128)}, bf16[192,256]{1,0:T(8,128)(2,1)}, bf16[...) custom-call(s32[26,6]{1,0:T(8,128)S(1)} %copy.290.table, ...), custom_call_target="tpu_custom_call", output_to_operand_aliasing={{0}: (8, {}), {1}: (9, {}), {2}: (10, {}), {3}: (11, {}), {... | custom-call | flops 150000000 | bytes 9000000 | tf_op jit(solution)/shard_map/section_forward/pallas_call | solution.py:256
  176.9 4.4 collective-permute-start.23
  185.5 6.3 %section_forward.27 = (bf16[192,9216]{1,0:T(8,128)(2,1)}, bf16[192,9216]{1,0:T(8,128)(2,1)}, f32[192,256]{1,0:T(8,128)}, bf16[192,256]{1,0:T(8,128)(2,1)}, bf16[...) custom-call(s32[26,6]{1,0:T(8,128)S(1)} %copy.290.table, ...), custom_call_target="tpu_custom_call", output_to_operand_aliasing={{0}: (8, {}), {1}: (9, {}), {2}: (10, {}), {3}: (11, {}), {... | custom-call | flops 150000000 | bytes 9000000 | tf_op jit(solution)/shard_map/section_forward/pallas_call | solution.py:256
  191.8 4.4 collective-permute-start.24
  200.4 6.3 %section_forward.28 = (bf16[192,9216]{1,0:T(8,128)(2,1)}, bf16[192,9216]{1,0:T(8,128)(2,1)}, f32[192,256]{1,0:T(8,128)}, bf16[192,256]{1,0:T(8,128)(2,1)}, bf16[...) custom-call(s32[26,6]{1,0:T(8,128)S(1)} %copy.290.table, ...), custom_call_target="tpu_custom_call", output_to_operand_aliasing={{0}: (8, {}), {1}: (9, {}), {2}: (10, {}), {3}: (11, {}), {... | custom-call | flops 150000000 | bytes 9000000 | tf_op jit(solution)/shard_map/section_forward/pallas_call | solution.py:256
  206.7 5.3 collective-permute-start.26
  216.2 6.3 %section_forward.29 = (bf16[192,9216]{1,0:T(8,128)(2,1)}, bf16[192,9216]{1,0:T(8,128)(2,1)}, f32[192,256]{1,0:T(8,128)}, bf16[192,256]{1,0:T(8,128)(2,1)}, bf16[...) custom-call(s32[26,6]{1,0:T(8,128)S(1)} %copy.290.table, ...), custom_call_target="tpu_custom_call", output_to_operand_aliasing={{0}: (8, {}), {1}: (9, {}), {2}: (10, {}), {3}: (11, {}), {... | custom-call | flops 150000000 | bytes 9000000 | tf_op jit(solution)/shard_map/section_forward/pallas_call | solution.py:256
  222.5 6.5 %collective-permute-start.28 = (bf16[16,9216]{1,0:T(8,128)(2,1)S(1)}, bf16[16,9216]{1,0:T(8,128)(2,1)S(1)}, u32[]{:S(2)}, u32[]{:S(2)}) collective-permute-start(bf16[16,9216]{1,0:T(8,128)(2,1)S(1)} %get-tuple-element.402), channel_id=1, source_target_pairs={{0,16},{16,32},{32,48},{48,64},{64,80},{80,96},{96,112},{1,17},{17... | collective-permute-start | bytes 884744 | tf_op jit(solution)/shard_map/ppermute | solution.py:556
  233.2 6.3 %section_forward.30 = (bf16[192,9216]{1,0:T(8,128)(2,1)}, bf16[192,9216]{1,0:T(8,128)(2,1)}, f32[192,256]{1,0:T(8,128)}, bf16[192,256]{1,0:T(8,128)(2,1)}, bf16[...) custom-call(s32[26,6]{1,0:T(8,128)S(1)} %copy.290.table, ...), custom_call_target="tpu_custom_call", output_to_operand_aliasing={{0}: (8, {}), {1}: (9, {}), {2}: (10, {}), {3}: (11, {}), {... | custom-call | flops 150000000 | bytes 9000000 | tf_op jit(solution)/shard_map/section_forward/pallas_call | solution.py:256
  239.5 6.5 %collective-permute-start.30 = (bf16[16,9216]{1,0:T(8,128)(2,1)S(1)}, bf16[16,9216]{1,0:T(8,128)(2,1)S(1)}, u32[]{:S(2)}, u32[]{:S(2)}) collective-permute-start(bf16[16,9216]{1,0:T(8,128)(2,1)S(1)} %get-tuple-element.417), channel_id=1, source_target_pairs={{0,16},{16,32},{32,48},{48,64},{64,80},{80,96},{96,112},{1,17},{17... | collective-permute-start | bytes 884744 | tf_op jit(solution)/shard_map/ppermute | solution.py:556
  259.3 40.4 %collective-permute-done.37.incoming = bf16[16,9216]{1,0:T(8,128)(2,1)S(1)} collective-permute-done((bf16[16,9216]{1,0:T(8,128)(2,1)S(1)}, bf16[16,9216]{1,0:T(8,128)(2,1)S(1)}, u32[]{:S(2)}, u32[]{:S(2)}) %collective-permute-start.37) | collective-permute-done | bytes 294944 | tf_op jit(solution)/shard_map/ppermute | solution.py:575
  299.7 5.4 section_backward.26
  308.0 11.9 %collective-permute-done.39.incoming = bf16[16,9216]{1,0:T(8,128)(2,1)S(1)} collective-permute-done((bf16[16,9216]{1,0:T(8,128)(2,1)S(1)}, bf16[16,9216]{1,0:T(8,128)(2,1)S(1)}, u32[]{:S(2)}, u32[]{:S(2)}) %collective-permute-start.39) | collective-permute-done | bytes 294944 | tf_op jit(solution)/shard_map/ppermute | solution.py:575
  319.9 5.5 section_backward.27
  328.3 7.3 %collective-permute-done.41.incoming = bf16[16,9216]{1,0:T(8,128)(2,1)S(1)} collective-permute-done((bf16[16,9216]{1,0:T(8,128)(2,1)S(1)}, bf16[16,9216]{1,0:T(8,128)(2,1)S(1)}, u32[]{:S(2)}, u32[]{:S(2)}) %collective-permute-start.41) | collective-permute-done | bytes 294944 | tf_op jit(solution)/shard_map/ppermute | solution.py:575
  335.6 5.4 section_backward.28
  343.9 15.5 %collective-permute-done.43.incoming = bf16[16,9216]{1,0:T(8,128)(2,1)S(1)} collective-permute-done((bf16[16,9216]{1,0:T(8,128)(2,1)S(1)}, bf16[16,9216]{1,0:T(8,128)(2,1)S(1)}, u32[]{:S(2)}, u32[]{:S(2)}) %collective-permute-start.43) | collective-permute-done | bytes 294944 | tf_op jit(solution)/shard_map/ppermute | solution.py:575
  359.4 5.4 section_backward.29
  367.7 11.7 %collective-permute-done.44.incoming = bf16[16,9216]{1,0:T(8,128)(2,1)S(1)} collective-permute-done((bf16[16,9216]{1,0:T(8,128)(2,1)S(1)}, bf16[16,9216]{1,0:T(8,128)(2,1)S(1)}, u32[]{:S(2)}, u32[]{:S(2)}) %collective-permute-start.44) | collective-permute-done | bytes 294944 | tf_op jit(solution)/shard_map/ppermute | solution.py:575
  379.4 5.6 section_backward.30
  386.3 11.9 %collective-permute-done.45.incoming = bf16[16,9216]{1,0:T(8,128)(2,1)S(1)} collective-permute-done((bf16[16,9216]{1,0:T(8,128)(2,1)S(1)}, bf16[16,9216]{1,0:T(8,128)(2,1)S(1)}, u32[]{:S(2)}, u32[]{:S(2)}) %collective-permute-start.45) | collective-permute-done | bytes 294944 | tf_op jit(solution)/shard_map/ppermute | solution.py:575
  398.2 5.4 section_backward.31
  404.9 11.2 %collective-permute-done.46.incoming = bf16[16,9216]{1,0:T(8,128)(2,1)S(1)} collective-permute-done((bf16[16,9216]{1,0:T(8,128)(2,1)S(1)}, bf16[16,9216]{1,0:T(8,128)(2,1)S(1)}, u32[]{:S(2)}, u32[]{:S(2)}) %collective-permute-start.46) | collective-permute-done | bytes 294944 | tf_op jit(solution)/shard_map/ppermute | solution.py:575
  416.1 5.4 section_backward.32
  422.7 9.0 %collective-permute-done.47.incoming = bf16[16,9216]{1,0:T(8,128)(2,1)S(1)} collective-permute-done((bf16[16,9216]{1,0:T(8,128)(2,1)S(1)}, bf16[16,9216]{1,0:T(8,128)(2,1)S(1)}, u32[]{:S(2)}, u32[]{:S(2)}) %collective-permute-start.47) | collective-permute-done | bytes 294944 | tf_op jit(solution)/shard_map/ppermute | solution.py:575
  431.7 5.4 section_backward.33
  438.4 8.5 %collective-permute-done.48.incoming = bf16[16,9216]{1,0:T(8,128)(2,1)S(1)} collective-permute-done((bf16[16,9216]{1,0:T(8,128)(2,1)S(1)}, bf16[16,9216]{1,0:T(8,128)(2,1)S(1)}, u32[]{:S(2)}, u32[]{:S(2)}) %collective-permute-start.48) | collective-permute-done | bytes 294944 | tf_op jit(solution)/shard_map/ppermute | solution.py:575
  446.9 5.4 section_backward.34
  453.6 8.9 %collective-permute-done.49.incoming = bf16[16,9216]{1,0:T(8,128)(2,1)S(1)} collective-permute-done((bf16[16,9216]{1,0:T(8,128)(2,1)S(1)}, bf16[16,9216]{1,0:T(8,128)(2,1)S(1)}, u32[]{:S(2)}, u32[]{:S(2)}) %collective-permute-start.49) | collective-permute-done | bytes 294944 | tf_op jit(solution)/shard_map/ppermute | solution.py:575
  462.6 5.4 section_backward.35
  469.2 9.4 %collective-permute-done.50.incoming = bf16[16,9216]{1,0:T(8,128)(2,1)S(1)} collective-permute-done((bf16[16,9216]{1,0:T(8,128)(2,1)S(1)}, bf16[16,9216]{1,0:T(8,128)(2,1)S(1)}, u32[]{:S(2)}, u32[]{:S(2)}) %collective-permute-start.50) | collective-permute-done | bytes 294944 | tf_op jit(solution)/shard_map/ppermute | solution.py:575
  478.7 5.6 section_backward.36
  485.7 7.4 %collective-permute-done.51.incoming = bf16[16,9216]{1,0:T(8,128)(2,1)S(1)} collective-permute-done((bf16[16,9216]{1,0:T(8,128)(2,1)S(1)}, bf16[16,9216]{1,0:T(8,128)(2,1)S(1)}, u32[]{:S(2)}, u32[]{:S(2)}) %collective-permute-start.51) | collective-permute-done | bytes 294944 | tf_op jit(solution)/shard_map/ppermute | solution.py:575
  497.8 6.1 %section_backward.37 = (bf16[192,9216]{1,0:T(8,128)(2,1)}, f32[192,256]{1,0:T(8,128)}, f32[192,256]{1,0:T(8,128)}, bf16[192,9216]{1,0:T(8,128)(2,1)}, bf16[192,9...) custom-call(s32[26,6]{1,0:T(8,128)S(1)} %copy.290.table, ...), custom_call_target="tpu_custom_call", output_to_operand_aliasing={{0}: (7, {}), {1}: (8, {}), {2}: (9, {}), {3}: (10, {}), {4... | custom-call | flops 150000000 | bytes 9000000 | tf_op jit(solution)/shard_map/section_backward/pallas_call | solution.py:285
  504.8 4.9 gradient_blocks.3
  509.8 4.9 gradient_blocks.2
  515.9 7.3 %collective-permute-start.59 = (bf16[1168,256]{1,0:T(8,128)(2,1)S(1)}, bf16[1168,256]{1,0:T(8,128)(2,1)S(1)}, u32[]{:S(2)}, u32[]{:S(2)}) collective-permute-start(bf16[1168,256]{1,0:T(8,128)(2,1)S(1)} %get-tuple-element.598), channel_id=1, source_target_pairs={{0,12},{1,13},{2,14},{3,15},{4,0},{5,1},{6,2},{7,3},{8,4},{9,5},{1... | collective-permute-start | bytes 1794056 | tf_op jit(solution)/shard_map/ppermute | solution.py:370
  523.3 8.9 %collective-permute-start.58 = (bf16[1168,256]{1,0:T(8,128)(2,1)S(1)}, bf16[1168,256]{1,0:T(8,128)(2,1)S(1)}, u32[]{:S(2)}, u32[]{:S(2)}) collective-permute-start(bf16[1168,256]{1,0:T(8,128)(2,1)S(1)} %get-tuple-element.599), channel_id=1, source_target_pairs={{0,4},{1,5},{2,6},{3,7},{4,8},{5,9},{6,10},{7,11},{8,12},{9,13},{1... | collective-permute-start | bytes 1794056 | tf_op jit(solution)/shard_map/ppermute | solution.py:370
  539.5 9.3 %collective-permute-done.58 = bf16[1168,256]{1,0:T(8,128)(2,1)S(1)} collective-permute-done((bf16[1168,256]{1,0:T(8,128)(2,1)S(1)}, bf16[1168,256]{1,0:T(8,128)(2,1)S(1)}, u32[]{:S(2)}, u32[]{:S(2)}) %collective-permute-start.58) | collective-permute-done | bytes 598048 | tf_op jit(solution)/shard_map/ppermute | solution.py:370
  557.0 4.5 collective-permute-done.54
  561.5 12.8 %collective-permute-done.57 = bf16[1168,256]{1,0:T(8,128)(2,1)} collective-permute-done((bf16[1168,256]{1,0:T(8,128)(2,1)}, bf16[1168,256]{1,0:T(8,128)(2,1)}, u32[]{:S(2)}, u32[]{:S(2)}) %collective-permute-start.57) | collective-permute-done | bytes 598048 | tf_op jit(solution)/shard_map/ppermute | solution.py:370
  (143 shorter events, 113.5 us)
Async XLA Ops:
  0.6 1.5 collective-permute-start
  4.0 18.0 %collective-permute-start.8 = (bf16[1168,256]{1,0:T(8,128)(2,1)S(1)}, bf16[1168,256]{1,0:T(8,128)(2,1)S(1)}, u32[]{:S(2)}, u32[]{:S(2)}) collective-permute-start(bf16[1168,256]{1,0:T(8,128)(2,1)S(1)} %fusion.7.refs_0_), channel_id=1, source_target_pairs={{0,8},{1,9},{2,10},{3,11},{4,12},{5,13},{6,14},{7,15},{8,0},{9,1},... | collective-permute-start | bytes 1794056 | tf_op jit(solution)/shard_map/ppermute | solution.py:370
  7.4 26.7 %collective-permute-start.6 = (bf16[1168,256]{1,0:T(8,128)(2,1)S(1)}, bf16[1168,256]{1,0:T(8,128)(2,1)S(1)}, u32[]{:S(2)}, u32[]{:S(2)}) collective-permute-start(bf16[1168,256]{1,0:T(8,128)(2,1)S(1)} %fusion.7.refs_0_), channel_id=1, source_target_pairs={{0,4},{1,5},{2,6},{3,7},{4,8},{5,9},{6,10},{7,11},{8,12},{9,13},{1... | collective-permute-start | bytes 1794056 | tf_op jit(solution)/shard_map/ppermute | solution.py:370
  8.1 26.4 %collective-permute-start.4 = (bf16[1168,256]{1,0:T(8,128)(2,1)S(1)}, bf16[1168,256]{1,0:T(8,128)(2,1)S(1)}, u32[]{:S(2)}, u32[]{:S(2)}) collective-permute-start(bf16[1168,256]{1,0:T(8,128)(2,1)S(1)} %fusion.7.refs_0_), channel_id=1, source_target_pairs={{0,12},{1,13},{2,14},{3,15},{4,0},{5,1},{6,2},{7,3},{8,4},{9,5},{1... | collective-permute-start | bytes 1794056 | tf_op jit(solution)/shard_map/ppermute | solution.py:370
  10.6 23.9 %collective-permute-start.2 = (bf16[1168,256]{1,0:T(8,128)(2,1)S(1)}, bf16[1168,256]{1,0:T(8,128)(2,1)S(1)}, u32[]{:S(2)}, u32[]{:S(2)}) collective-permute-start(bf16[1168,256]{1,0:T(8,128)(2,1)S(1)} %fusion.7.refs_0_), channel_id=1, source_target_pairs={{0,2},{1,3},{2,0},{3,1},{4,6},{5,7},{6,4},{7,5},{8,10},{9,11},{10,... | collective-permute-start | bytes 1794056 | tf_op jit(solution)/shard_map/ppermute | solution.py:366
  14.5 21.8 %collective-permute-start.1 = (bf16[1168,256]{1,0:T(8,128)(2,1)S(1)}, bf16[1168,256]{1,0:T(8,128)(2,1)S(1)}, u32[]{:S(2)}, u32[]{:S(2)}) collective-permute-start(bf16[1168,256]{1,0:T(8,128)(2,1)S(1)} %fusion.7.refs_0_), channel_id=1, source_target_pairs={{0,1},{1,0},{2,3},{3,2},{4,5},{5,4},{6,7},{7,6},{8,9},{9,8},{10,11... | collective-permute-start | bytes 1794056 | tf_op jit(solution)/shard_map/ppermute | solution.py:362
  22.0 18.4 %collective-permute-start.10 = (bf16[1168,256]{1,0:T(8,128)(2,1)S(1)}, bf16[1168,256]{1,0:T(8,128)(2,1)}, u32[]{:S(2)}, u32[]{:S(2)}) collective-permute-start(bf16[1168,256]{1,0:T(8,128)(2,1)S(1)} %collective-permute-done.8.refs_8_), channel_id=1, source_target_pairs={{0,2},{1,3},{2,0},{3,1},{4,6},{5,7},{6,4},{7,5},{8,10},{9,11},{10,... | collective-permute-start | bytes 1794056 | tf_op jit(solution)/shard_map/ppermute | solution.py:366
  34.0 6.4 %collective-permute-start.9 = (bf16[1168,256]{1,0:T(8,128)(2,1)S(1)}, bf16[1168,256]{1,0:T(8,128)(2,1)}, u32[]{:S(2)}, u32[]{:S(2)}) collective-permute-start(bf16[1168,256]{1,0:T(8,128)(2,1)S(1)} %collective-permute-done.8.refs_8_), channel_id=1, source_target_pairs={{0,1},{1,0},{2,3},{3,2},{4,5},{5,4},{6,7},{7,6},{8,9},{9,8},{10,11... | collective-permute-start | bytes 1794056 | tf_op jit(solution)/shard_map/ppermute | solution.py:362
  34.5 6.5 %collective-permute-start.7 = (bf16[1168,256]{1,0:T(8,128)(2,1)S(1)}, bf16[1168,256]{1,0:T(8,128)(2,1)}, u32[]{:S(2)}, u32[]{:S(2)}) collective-permute-start(bf16[1168,256]{1,0:T(8,128)(2,1)S(1)} %collective-permute-done.6.refs_6_), channel_id=1, source_target_pairs={{0,1},{1,0},{2,3},{3,2},{4,5},{5,4},{6,7},{7,6},{8,9},{9,8},{10,11... | collective-permute-start | bytes 1794056 | tf_op jit(solution)/shard_map/ppermute | solution.py:362
  34.6 17.2 %collective-permute-start.14 = (bf16[1168,256]{1,0:T(8,128)(2,1)S(1)}, bf16[1168,256]{1,0:T(8,128)(2,1)}, u32[]{:S(2)}, u32[]{:S(2)}) collective-permute-start(bf16[1168,256]{1,0:T(8,128)(2,1)S(1)} %collective-permute-done.2.refs_2_), channel_id=1, source_target_pairs={{0,4},{1,5},{2,6},{3,7},{4,8},{5,9},{6,10},{7,11},{8,12},{9,13},{1... | collective-permute-start | bytes 1794056 | tf_op jit(solution)/shard_map/ppermute | solution.py:370
  37.2 15.3 %collective-permute-start.12 = (bf16[1168,256]{1,0:T(8,128)(2,1)S(1)}, bf16[1168,256]{1,0:T(8,128)(2,1)}, u32[]{:S(2)}, u32[]{:S(2)}) collective-permute-start(bf16[1168,256]{1,0:T(8,128)(2,1)S(1)} %collective-permute-done.2.refs_2_), channel_id=1, source_target_pairs={{0,12},{1,13},{2,14},{3,15},{4,0},{5,1},{6,2},{7,3},{8,4},{9,5},{1... | collective-permute-start | bytes 1794056 | tf_op jit(solution)/shard_map/ppermute | solution.py:370
  40.4 17.5 %collective-permute-start.3 = (bf16[1168,256]{1,0:T(8,128)(2,1)S(1)}, bf16[1168,256]{1,0:T(8,128)(2,1)}, u32[]{:S(2)}, u32[]{:S(2)}) collective-permute-start(bf16[1168,256]{1,0:T(8,128)(2,1)S(1)} %collective-permute-done.2.refs_2_), channel_id=1, source_target_pairs={{0,1},{1,0},{2,3},{3,2},{4,5},{5,4},{6,7},{7,6},{8,9},{9,8},{10,11... | collective-permute-start | bytes 1794056 | tf_op jit(solution)/shard_map/ppermute | solution.py:362
  40.4 17.5 %collective-permute-start.5 = (bf16[1168,256]{1,0:T(8,128)(2,1)S(1)}, bf16[1168,256]{1,0:T(8,128)(2,1)}, u32[]{:S(2)}, u32[]{:S(2)}) collective-permute-start(bf16[1168,256]{1,0:T(8,128)(2,1)S(1)} %collective-permute-done.4.refs_4_), channel_id=1, source_target_pairs={{0,1},{1,0},{2,3},{3,2},{4,5},{5,4},{6,7},{7,6},{8,9},{9,8},{10,11... | collective-permute-start | bytes 1794056 | tf_op jit(solution)/shard_map/ppermute | solution.py:362
  40.9 17.0 %collective-permute-start.11 = (bf16[1168,256]{1,0:T(8,128)(2,1)}, bf16[1168,256]{1,0:T(8,128)(2,1)}, u32[]{:S(2)}, u32[]{:S(2)}) collective-permute-start(bf16[1168,256]{1,0:T(8,128)(2,1)} %collective-permute-done.10.refs_10_), channel_id=1, source_target_pairs={{0,1},{1,0},{2,3},{3,2},{4,5},{5,4},{6,7},{7,6},{8,9},{9,8},{10,11... | collective-permute-start | bytes 1794056 | tf_op jit(solution)/shard_map/ppermute | solution.py:362
  51.7 6.2 %collective-permute-start.15 = (bf16[1168,256]{1,0:T(8,128)(2,1)}, bf16[1168,256]{1,0:T(8,128)(2,1)}, u32[]{:S(2)}, u32[]{:S(2)}) collective-permute-start(bf16[1168,256]{1,0:T(8,128)(2,1)} %collective-permute-done.14.refs_14_), channel_id=1, source_target_pairs={{0,1},{1,0},{2,3},{3,2},{4,5},{5,4},{6,7},{7,6},{8,9},{9,8},{10,11... | collective-permute-start | bytes 1794056 | tf_op jit(solution)/shard_map/ppermute | solution.py:362
  52.5 5.4 collective-permute-start.13
  62.3 416.3 %copy-start = (bf16[9216,256]{1,0:T(8,128)(2,1)}, bf16[9216,256]{1,0:T(8,128)(2,1)S(1)}, u32[]{:S(2)}) copy-start(bf16[9216,256]{1,0:T(8,128)(2,1)S(1)} %get-tuple-element.302.down) | copy-start | bytes 14155780
  62.3 416.3 %copy-start.2 = (bf16[9216,256]{1,0:T(8,128)(2,1)}, bf16[9216,256]{1,0:T(8,128)(2,1)S(1)}, u32[]{:S(2)}) copy-start(bf16[9216,256]{1,0:T(8,128)(2,1)S(1)} %get-tuple-element.303.up) | copy-start | bytes 14155780
  68.9 8.4 %collective-permute-start.16 = (bf16[16,9216]{1,0:T(8,128)(2,1)S(1)}, bf16[16,9216]{1,0:T(8,128)(2,1)S(1)}, u32[]{:S(2)}, u32[]{:S(2)}) collective-permute-start(bf16[16,9216]{1,0:T(8,128)(2,1)S(1)} %get-tuple-element.310), channel_id=1, source_target_pairs={{0,16},{1,17},{2,18},{3,19},{4,20},{5,21},{6,22},{7,23},{8,24},{9,... | collective-permute-start | bytes 884744 | tf_op jit(solution)/shard_map/ppermute | solution.py:556
  83.6 10.6 %collective-permute-start.17 = (bf16[16,9216]{1,0:T(8,128)(2,1)S(1)}, bf16[16,9216]{1,0:T(8,128)(2,1)S(1)}, u32[]{:S(2)}, u32[]{:S(2)}) collective-permute-start(bf16[16,9216]{1,0:T(8,128)(2,1)S(1)} %get-tuple-element.317), channel_id=1, source_target_pairs={{0,16},{16,32},{1,17},{17,33},{2,18},{18,34},{3,19},{19,35},{4,20}... | collective-permute-start | bytes 884744 | tf_op jit(solution)/shard_map/ppermute | solution.py:556
  100.7 9.8 %collective-permute-start.18 = (bf16[16,9216]{1,0:T(8,128)(2,1)S(1)}, bf16[16,9216]{1,0:T(8,128)(2,1)S(1)}, u32[]{:S(2)}, u32[]{:S(2)}) collective-permute-start(bf16[16,9216]{1,0:T(8,128)(2,1)S(1)} %get-tuple-element.324), channel_id=1, source_target_pairs={{0,16},{16,32},{32,48},{1,17},{17,33},{33,49},{2,18},{18,34},{34,5... | collective-permute-start | bytes 884744 | tf_op jit(solution)/shard_map/ppermute | solution.py:556
  116.7 8.8 %collective-permute-start.19 = (bf16[16,9216]{1,0:T(8,128)(2,1)S(1)}, bf16[16,9216]{1,0:T(8,128)(2,1)S(1)}, u32[]{:S(2)}, u32[]{:S(2)}) collective-permute-start(bf16[16,9216]{1,0:T(8,128)(2,1)S(1)} %get-tuple-element.331), channel_id=1, source_target_pairs={{0,16},{16,32},{32,48},{48,64},{1,17},{17,33},{33,49},{49,65},{2,1... | collective-permute-start | bytes 884744 | tf_op jit(solution)/shard_map/ppermute | solution.py:556
  131.8 8.6 %collective-permute-start.20 = (bf16[16,9216]{1,0:T(8,128)(2,1)S(1)}, bf16[16,9216]{1,0:T(8,128)(2,1)S(1)}, u32[]{:S(2)}, u32[]{:S(2)}) collective-permute-start(bf16[16,9216]{1,0:T(8,128)(2,1)S(1)} %get-tuple-element.338), channel_id=1, source_target_pairs={{0,16},{16,32},{32,48},{48,64},{64,80},{1,17},{17,33},{33,49},{49,... | collective-permute-start | bytes 884744 | tf_op jit(solution)/shard_map/ppermute | solution.py:556
  146.7 8.6 %collective-permute-start.21 = (bf16[16,9216]{1,0:T(8,128)(2,1)S(1)}, bf16[16,9216]{1,0:T(8,128)(2,1)S(1)}, u32[]{:S(2)}, u32[]{:S(2)}) collective-permute-start(bf16[16,9216]{1,0:T(8,128)(2,1)S(1)} %get-tuple-element.345), channel_id=1, source_target_pairs={{0,16},{16,32},{32,48},{48,64},{64,80},{80,96},{1,17},{17,33},{33,... | collective-permute-start | bytes 884744 | tf_op jit(solution)/shard_map/ppermute | solution.py:556
  161.6 8.6 %collective-permute-start.22 = (bf16[16,9216]{1,0:T(8,128)(2,1)S(1)}, bf16[16,9216]{1,0:T(8,128)(2,1)S(1)}, u32[]{:S(2)}, u32[]{:S(2)}) collective-permute-start(bf16[16,9216]{1,0:T(8,128)(2,1)S(1)} %get-tuple-element.352), channel_id=1, source_target_pairs={{0,16},{16,32},{32,48},{48,64},{64,80},{80,96},{96,112},{1,17},{17... | collective-permute-start | bytes 884744 | tf_op jit(solution)/shard_map/ppermute | solution.py:556
  176.9 8.6 %collective-permute-start.23 = (bf16[16,9216]{1,0:T(8,128)(2,1)S(1)}, bf16[16,9216]{1,0:T(8,128)(2,1)S(1)}, u32[]{:S(2)}, u32[]{:S(2)}) collective-permute-start(bf16[16,9216]{1,0:T(8,128)(2,1)S(1)} %get-tuple-element.359), channel_id=1, source_target_pairs={{0,16},{16,32},{32,48},{48,64},{64,80},{80,96},{96,112},{1,17},{17... | collective-permute-start | bytes 884744 | tf_op jit(solution)/shard_map/ppermute | solution.py:556
  182.3 13.9 %collective-permute-start.25 = (bf16[16,9216]{1,0:T(8,128)(2,1)S(1)}, bf16[16,9216]{1,0:T(8,128)(2,1)S(1)}, u32[]{:S(2)}, u32[]{:S(2)}) collective-permute-start(bf16[16,9216]{1,0:T(8,128)(2,1)S(1)} %get-tuple-element.373), channel_id=1, source_target_pairs={{112,96},{113,97},{114,98},{115,99},{116,100},{117,101},{118,102},... | collective-permute-start | bytes 884744 | tf_op jit(solution)/shard_map/ppermute | solution.py:575
  191.8 8.6 %collective-permute-start.24 = (bf16[16,9216]{1,0:T(8,128)(2,1)S(1)}, bf16[16,9216]{1,0:T(8,128)(2,1)S(1)}, u32[]{:S(2)}, u32[]{:S(2)}) collective-permute-start(bf16[16,9216]{1,0:T(8,128)(2,1)S(1)} %get-tuple-element.372), channel_id=1, source_target_pairs={{0,16},{16,32},{32,48},{48,64},{64,80},{80,96},{96,112},{1,17},{17... | collective-permute-start | bytes 884744 | tf_op jit(solution)/shard_map/ppermute | solution.py:556
  197.2 14.8 %collective-permute-start.27 = (bf16[16,9216]{1,0:T(8,128)(2,1)S(1)}, bf16[16,9216]{1,0:T(8,128)(2,1)S(1)}, u32[]{:S(2)}, u32[]{:S(2)}) collective-permute-start(bf16[16,9216]{1,0:T(8,128)(2,1)S(1)} %get-tuple-element.388), channel_id=1, source_target_pairs={{96,80},{112,96},{97,81},{113,97},{98,82},{114,98},{99,83},{115,99... | collective-permute-start | bytes 884744 | tf_op jit(solution)/shard_map/ppermute | solution.py:575
  206.7 9.5 %collective-permute-start.26 = (bf16[16,9216]{1,0:T(8,128)(2,1)S(1)}, bf16[16,9216]{1,0:T(8,128)(2,1)S(1)}, u32[]{:S(2)}, u32[]{:S(2)}) collective-permute-start(bf16[16,9216]{1,0:T(8,128)(2,1)S(1)} %get-tuple-element.387), channel_id=1, source_target_pairs={{0,16},{16,32},{32,48},{48,64},{64,80},{80,96},{96,112},{1,17},{17... | collective-permute-start | bytes 884744 | tf_op jit(solution)/shard_map/ppermute | solution.py:556
  213.1 15.9 %collective-permute-start.29 = (bf16[16,9216]{1,0:T(8,128)(2,1)S(1)}, bf16[16,9216]{1,0:T(8,128)(2,1)S(1)}, u32[]{:S(2)}, u32[]{:S(2)}) collective-permute-start(bf16[16,9216]{1,0:T(8,128)(2,1)S(1)} %get-tuple-element.403), channel_id=1, source_target_pairs={{80,64},{96,80},{112,96},{81,65},{97,81},{113,97},{82,66},{98,82},... | collective-permute-start | bytes 884744 | tf_op jit(solution)/shard_map/ppermute | solution.py:575
  222.5 10.7 %collective-permute-start.28 = (bf16[16,9216]{1,0:T(8,128)(2,1)S(1)}, bf16[16,9216]{1,0:T(8,128)(2,1)S(1)}, u32[]{:S(2)}, u32[]{:S(2)}) collective-permute-start(bf16[16,9216]{1,0:T(8,128)(2,1)S(1)} %get-tuple-element.402), channel_id=1, source_target_pairs={{0,16},{16,32},{32,48},{48,64},{64,80},{80,96},{96,112},{1,17},{17... | collective-permute-start | bytes 884744 | tf_op jit(solution)/shard_map/ppermute | solution.py:556
  229.9 16.0 %collective-permute-start.31 = (bf16[16,9216]{1,0:T(8,128)(2,1)S(1)}, bf16[16,9216]{1,0:T(8,128)(2,1)S(1)}, u32[]{:S(2)}, u32[]{:S(2)}) collective-permute-start(bf16[16,9216]{1,0:T(8,128)(2,1)S(1)} %get-tuple-element.418), channel_id=1, source_target_pairs={{64,48},{80,64},{96,80},{112,96},{65,49},{81,65},{97,81},{113,97},... | collective-permute-start | bytes 884744 | tf_op jit(solution)/shard_map/ppermute | solution.py:575
  239.5 10.7 %collective-permute-start.30 = (bf16[16,9216]{1,0:T(8,128)(2,1)S(1)}, bf16[16,9216]{1,0:T(8,128)(2,1)S(1)}, u32[]{:S(2)}, u32[]{:S(2)}) collective-permute-start(bf16[16,9216]{1,0:T(8,128)(2,1)S(1)} %get-tuple-element.417), channel_id=1, source_target_pairs={{0,16},{16,32},{32,48},{48,64},{64,80},{80,96},{96,112},{1,17},{17... | collective-permute-start | bytes 884744 | tf_op jit(solution)/shard_map/ppermute | solution.py:556
  246.9 4.8 collective-permute-start.33
  251.1 2.7 collective-permute-start.32
  253.1 2.3 collective-permute-start.35
  254.7 2.9 collective-permute-start.34
  256.4 43.3 %collective-permute-start.37 = (bf16[16,9216]{1,0:T(8,128)(2,1)S(1)}, bf16[16,9216]{1,0:T(8,128)(2,1)S(1)}, u32[]{:S(2)}, u32[]{:S(2)}) collective-permute-start(bf16[16,9216]{1,0:T(8,128)(2,1)S(1)} %get-tuple-element.463), channel_id=1, source_target_pairs={{16,0},{32,16},{48,32},{64,48},{80,64},{96,80},{112,96},{17,1},{33... | collective-permute-start | bytes 884744 | tf_op jit(solution)/shard_map/ppermute | solution.py:575
  258.6 47.7 %collective-permute-start.36 = (bf16[16,9216]{1,0:T(8,128)(2,1)S(1)}, bf16[16,9216]{1,0:T(8,128)(2,1)S(1)}, u32[]{:S(2)}, u32[]{:S(2)}) collective-permute-start(bf16[16,9216]{1,0:T(8,128)(2,1)S(1)} %get-tuple-element.462), channel_id=1, source_target_pairs={{48,64},{64,80},{80,96},{96,112},{49,65},{65,81},{81,97},{97,113},... | collective-permute-start | bytes 884744 | tf_op jit(solution)/shard_map/ppermute | solution.py:556
  305.0 14.8 %collective-permute-start.39 = (bf16[16,9216]{1,0:T(8,128)(2,1)S(1)}, bf16[16,9216]{1,0:T(8,128)(2,1)S(1)}, u32[]{:S(2)}, u32[]{:S(2)}) collective-permute-start(bf16[16,9216]{1,0:T(8,128)(2,1)S(1)} %get-tuple-element.478), channel_id=1, source_target_pairs={{16,0},{32,16},{48,32},{64,48},{80,64},{96,80},{112,96},{17,1},{33... | collective-permute-start | bytes 884744 | tf_op jit(solution)/shard_map/ppermute | solution.py:575
  307.3 19.4 %collective-permute-start.38 = (bf16[16,9216]{1,0:T(8,128)(2,1)S(1)}, bf16[16,9216]{1,0:T(8,128)(2,1)S(1)}, u32[]{:S(2)}, u32[]{:S(2)}) collective-permute-start(bf16[16,9216]{1,0:T(8,128)(2,1)S(1)} %get-tuple-element.477), channel_id=1, source_target_pairs={{64,80},{80,96},{96,112},{65,81},{81,97},{97,113},{66,82},{82,98},... | collective-permute-start | bytes 884744 | tf_op jit(solution)/shard_map/ppermute | solution.py:556
  325.4 10.2 %collective-permute-start.41 = (bf16[16,9216]{1,0:T(8,128)(2,1)S(1)}, bf16[16,9216]{1,0:T(8,128)(2,1)S(1)}, u32[]{:S(2)}, u32[]{:S(2)}) collective-permute-start(bf16[16,9216]{1,0:T(8,128)(2,1)S(1)} %get-tuple-element.493), channel_id=1, source_target_pairs={{16,0},{32,16},{48,32},{64,48},{80,64},{96,80},{112,96},{17,1},{33... | collective-permute-start | bytes 884744 | tf_op jit(solution)/shard_map/ppermute | solution.py:575
  327.6 14.7 %collective-permute-start.40 = (bf16[16,9216]{1,0:T(8,128)(2,1)S(1)}, bf16[16,9216]{1,0:T(8,128)(2,1)S(1)}, u32[]{:S(2)}, u32[]{:S(2)}) collective-permute-start(bf16[16,9216]{1,0:T(8,128)(2,1)S(1)} %get-tuple-element.492), channel_id=1, source_target_pairs={{80,96},{96,112},{81,97},{97,113},{82,98},{98,114},{83,99},{99,115... | collective-permute-start | bytes 884744 | tf_op jit(solution)/shard_map/ppermute | solution.py:556
  341.0 18.5 %collective-permute-start.43 = (bf16[16,9216]{1,0:T(8,128)(2,1)S(1)}, bf16[16,9216]{1,0:T(8,128)(2,1)S(1)}, u32[]{:S(2)}, u32[]{:S(2)}) collective-permute-start(bf16[16,9216]{1,0:T(8,128)(2,1)S(1)} %get-tuple-element.508), channel_id=1, source_target_pairs={{16,0},{32,16},{48,32},{64,48},{80,64},{96,80},{112,96},{17,1},{33... | collective-permute-start | bytes 884744 | tf_op jit(solution)/shard_map/ppermute | solution.py:575
  343.2 22.9 %collective-permute-start.42 = (bf16[16,9216]{1,0:T(8,128)(2,1)S(1)}, bf16[16,9216]{1,0:T(8,128)(2,1)S(1)}, u32[]{:S(2)}, u32[]{:S(2)}) collective-permute-start(bf16[16,9216]{1,0:T(8,128)(2,1)S(1)} %get-tuple-element.507), channel_id=1, source_target_pairs={{96,112},{97,113},{98,114},{99,115},{100,116},{101,117},{102,118},... | collective-permute-start | bytes 884744 | tf_op jit(solution)/shard_map/ppermute | solution.py:556
  364.8 14.6 %collective-permute-start.44 = (bf16[16,9216]{1,0:T(8,128)(2,1)S(1)}, bf16[16,9216]{1,0:T(8,128)(2,1)S(1)}, u32[]{:S(2)}, u32[]{:S(2)}) collective-permute-start(bf16[16,9216]{1,0:T(8,128)(2,1)S(1)} %get-tuple-element.523), channel_id=1, source_target_pairs={{16,0},{32,16},{48,32},{64,48},{80,64},{96,80},{112,96},{17,1},{33... | collective-permute-start | bytes 884744 | tf_op jit(solution)/shard_map/ppermute | solution.py:575
  385.0 13.2 %collective-permute-start.45 = (bf16[16,9216]{1,0:T(8,128)(2,1)S(1)}, bf16[16,9216]{1,0:T(8,128)(2,1)S(1)}, u32[]{:S(2)}, u32[]{:S(2)}) collective-permute-start(bf16[16,9216]{1,0:T(8,128)(2,1)S(1)} %get-tuple-element.531), channel_id=1, source_target_pairs={{16,0},{32,16},{48,32},{64,48},{80,64},{96,80},{112,96},{17,1},{33... | collective-permute-start | bytes 884744 | tf_op jit(solution)/shard_map/ppermute | solution.py:575
  403.6 12.5 %collective-permute-start.46 = (bf16[16,9216]{1,0:T(8,128)(2,1)S(1)}, bf16[16,9216]{1,0:T(8,128)(2,1)S(1)}, u32[]{:S(2)}, u32[]{:S(2)}) collective-permute-start(bf16[16,9216]{1,0:T(8,128)(2,1)S(1)} %get-tuple-element.539), channel_id=1, source_target_pairs={{16,0},{32,16},{48,32},{64,48},{80,64},{96,80},{17,1},{33,17},{49,... | collective-permute-start | bytes 884744 | tf_op jit(solution)/shard_map/ppermute | solution.py:575
  421.4 10.3 %collective-permute-start.47 = (bf16[16,9216]{1,0:T(8,128)(2,1)S(1)}, bf16[16,9216]{1,0:T(8,128)(2,1)S(1)}, u32[]{:S(2)}, u32[]{:S(2)}) collective-permute-start(bf16[16,9216]{1,0:T(8,128)(2,1)S(1)} %get-tuple-element.547), channel_id=1, source_target_pairs={{16,0},{32,16},{48,32},{64,48},{80,64},{17,1},{33,17},{49,33},{65,... | collective-permute-start | bytes 884744 | tf_op jit(solution)/shard_map/ppermute | solution.py:575
  437.1 9.8 %collective-permute-start.48 = (bf16[16,9216]{1,0:T(8,128)(2,1)S(1)}, bf16[16,9216]{1,0:T(8,128)(2,1)S(1)}, u32[]{:S(2)}, u32[]{:S(2)}) collective-permute-start(bf16[16,9216]{1,0:T(8,128)(2,1)S(1)} %get-tuple-element.555), channel_id=1, source_target_pairs={{16,0},{32,16},{48,32},{64,48},{17,1},{33,17},{49,33},{65,49},{18,... | collective-permute-start | bytes 884744 | tf_op jit(solution)/shard_map/ppermute | solution.py:575
  452.3 10.2 %collective-permute-start.49 = (bf16[16,9216]{1,0:T(8,128)(2,1)S(1)}, bf16[16,9216]{1,0:T(8,128)(2,1)S(1)}, u32[]{:S(2)}, u32[]{:S(2)}) collective-permute-start(bf16[16,9216]{1,0:T(8,128)(2,1)S(1)} %get-tuple-element.563), channel_id=1, source_target_pairs={{16,0},{32,16},{48,32},{17,1},{33,17},{49,33},{18,2},{34,18},{50,3... | collective-permute-start | bytes 884744 | tf_op jit(solution)/shard_map/ppermute | solution.py:575
  467.9 10.7 %collective-permute-start.50 = (bf16[16,9216]{1,0:T(8,128)(2,1)S(1)}, bf16[16,9216]{1,0:T(8,128)(2,1)S(1)}, u32[]{:S(2)}, u32[]{:S(2)}) collective-permute-start(bf16[16,9216]{1,0:T(8,128)(2,1)S(1)} %get-tuple-element.571), channel_id=1, source_target_pairs={{16,0},{32,16},{17,1},{33,17},{18,2},{34,18},{19,3},{35,19},{20,4}... | collective-permute-start | bytes 884744 | tf_op jit(solution)/shard_map/ppermute | solution.py:575
  484.3 8.8 %collective-permute-start.51 = (bf16[16,9216]{1,0:T(8,128)(2,1)S(1)}, bf16[16,9216]{1,0:T(8,128)(2,1)S(1)}, u32[]{:S(2)}, u32[]{:S(2)}) collective-permute-start(bf16[16,9216]{1,0:T(8,128)(2,1)S(1)} %get-tuple-element.579), channel_id=1, source_target_pairs={{16,0},{17,1},{18,2},{19,3},{20,4},{21,5},{22,6},{23,7},{24,8},{25... | collective-permute-start | bytes 884744 | tf_op jit(solution)/shard_map/ppermute | solution.py:575
  509.7 5.6 collective-permute-start.53
  514.7 22.0 %collective-permute-start.52 = (bf16[4,1168,256]{2,1,0:T(8,128)(2,1)S(1)}, bf16[4,1168,256]{2,1,0:T(8,128)(2,1)S(1)}, u32[]{:S(2)}, u32[]{:S(2)}) collective-permute-start(bf16[4,1168,256]{2,1,0:T(8,128)(2,1)S(1)} %get-tuple-element.594), channel_id=1, source_target_pairs={{0,1},{1,0},{2,3},{3,2},{4,5},{5,4},{6,7},{7,6},{8,9},{9,8},{10,11... | collective-permute-start | bytes 7176200 | tf_op jit(solution)/shard_map/ppermute | solution.py:362
  515.9 23.6 %collective-permute-start.59 = (bf16[1168,256]{1,0:T(8,128)(2,1)S(1)}, bf16[1168,256]{1,0:T(8,128)(2,1)S(1)}, u32[]{:S(2)}, u32[]{:S(2)}) collective-permute-start(bf16[1168,256]{1,0:T(8,128)(2,1)S(1)} %get-tuple-element.598), channel_id=1, source_target_pairs={{0,12},{1,13},{2,14},{3,15},{4,0},{5,1},{6,2},{7,3},{8,4},{9,5},{1... | collective-permute-start | bytes 1794056 | tf_op jit(solution)/shard_map/ppermute | solution.py:370
  523.3 25.5 %collective-permute-start.58 = (bf16[1168,256]{1,0:T(8,128)(2,1)S(1)}, bf16[1168,256]{1,0:T(8,128)(2,1)S(1)}, u32[]{:S(2)}, u32[]{:S(2)}) collective-permute-start(bf16[1168,256]{1,0:T(8,128)(2,1)S(1)} %get-tuple-element.599), channel_id=1, source_target_pairs={{0,4},{1,5},{2,6},{3,7},{4,8},{5,9},{6,10},{7,11},{8,12},{9,13},{1... | collective-permute-start | bytes 1794056 | tf_op jit(solution)/shard_map/ppermute | solution.py:370
  532.2 16.8 %collective-permute-start.56 = (bf16[1168,256]{1,0:T(8,128)(2,1)S(1)}, bf16[1168,256]{1,0:T(8,128)(2,1)S(1)}, u32[]{:S(2)}, u32[]{:S(2)}) collective-permute-start(bf16[1168,256]{1,0:T(8,128)(2,1)S(1)} %get-tuple-element.600), channel_id=1, source_target_pairs={{0,2},{1,3},{2,0},{3,1},{4,6},{5,7},{6,4},{7,5},{8,10},{9,11},{10,... | collective-permute-start | bytes 1794056 | tf_op jit(solution)/shard_map/ppermute | solution.py:366
  535.1 26.3 %collective-permute-start.54 = (bf16[1168,256]{1,0:T(8,128)(2,1)S(1)}, bf16[1168,256]{1,0:T(8,128)(2,1)}, u32[]{:S(2)}, u32[]{:S(2)}) collective-permute-start(bf16[1168,256]{1,0:T(8,128)(2,1)S(1)} %get-tuple-element.597), channel_id=1, source_target_pairs={{0,4},{1,5},{2,6},{3,7},{4,8},{5,9},{6,10},{7,11},{8,12},{9,13},{1... | collective-permute-start | bytes 1794056 | tf_op jit(solution)/shard_map/ppermute | solution.py:370
  536.7 12.3 %copy-start.8 = (bf16[4,1168,256]{2,1,0:T(8,128)(2,1)}, bf16[4,1168,256]{2,1,0:T(8,128)(2,1)S(1)}, u32[]{:S(2)}) copy-start(bf16[4,1168,256]{2,1,0:T(8,128)(2,1)S(1)} %collective-permute-done.52) | copy-start | bytes 7176196
  537.8 23.7 %collective-permute-start.55 = (bf16[1168,256]{1,0:T(8,128)(2,1)}, bf16[1168,256]{1,0:T(8,128)(2,1)}, u32[]{:S(2)}, u32[]{:S(2)}) collective-permute-start(bf16[1168,256]{1,0:T(8,128)(2,1)} %fusion.9), channel_id=1, source_target_pairs={{0,12},{1,13},{2,14},{3,15},{4,0},{5,1},{6,2},{7,3},{8,4},{9,5},{1... | collective-permute-start | bytes 1794056 | tf_op jit(solution)/shard_map/ppermute | solution.py:370
  550.6 23.7 %collective-permute-start.57 = (bf16[1168,256]{1,0:T(8,128)(2,1)}, bf16[1168,256]{1,0:T(8,128)(2,1)}, u32[]{:S(2)}, u32[]{:S(2)}) collective-permute-start(bf16[1168,256]{1,0:T(8,128)(2,1)} %get-tuple-element.601), channel_id=1, source_target_pairs={{0,8},{1,9},{2,10},{3,11},{4,12},{5,13},{6,14},{7,15},{8,0},{9,1},... | collective-permute-start | bytes 1794056 | tf_op jit(solution)/shard_map/ppermute | solution.py:370
  553.7 20.6 %collective-permute-start.60 = (bf16[1168,256]{1,0:T(8,128)(2,1)}, bf16[1168,256]{1,0:T(8,128)(2,1)}, u32[]{:S(2)}, u32[]{:S(2)}) collective-permute-start(bf16[1168,256]{1,0:T(8,128)(2,1)} %get-tuple-element.602), channel_id=1, source_target_pairs={{0,2},{1,3},{2,0},{3,1},{4,6},{5,7},{6,4},{7,5},{8,10},{9,11},{10,... | collective-permute-start | bytes 1794056 | tf_op jit(solution)/shard_map/ppermute | solution.py:366
  (7 other events, 24.3 us)

commit v3 on v2

--- a/solution.py
+++ b/solution.py
@@ -24,6 +24,8 @@
 ROWS = 16
 CHUNKS = MICRO * TOKENS // ROWS
 SHARD = 576
+STRIDE = 2
+DEPTH = STRIDE * (SECTIONS - 1)
 EXTRA = 16
 WIDE = 1024
 MEDIUM = 512
@@ -370,15 +372,16 @@
     return lax.ppermute(value, "fsdp", fsdp_pairs(lambda y, z, core: ((y + by) % 4, z, core)))
 
 
-def gather_parts(own):
+def gather_parts(own, beside):
     parts = {(0, 0): own}
     parts[(0, 1)] = along_z(own)
     for by in (1, 3, 2):
         parts[(by, 0)] = along_y(own, -by)
+    parts[(0, 1)], made = beside(parts[(0, 1)])
     parts[(2, 1)] = along_z(parts[(2, 0)])
     for by in (1, 3):
         parts[(by, 1)] = along_y(parts[(0, 1)], -by)
-    return parts
+    return parts, made
 
 
 def gradient_kernel(order, normed, neckcot, cot, act, gains, mine, theirs, hold):
@@ -477,7 +480,7 @@
     place = lax.axis_index("fsdp")
     y, z, core = place >> 2, (place >> 1) & 1, place & 1
     tokens = MICRO * TOKENS
-    ticks = CHUNKS + 2 * SECTIONS - 2
+    ticks = CHUNKS + 2 * DEPTH
 
     other = to_core(norm_gain)
     pair = jnp.where(
@@ -487,7 +490,35 @@
     ).reshape(2 * SHARD // BLOCK, BLOCK)
     gain_rows = jnp.pad(pair, ((0, EXTRA - pair.shape[0]), (0, NECK - BLOCK)))
     own = jnp.concatenate([down_weight[0], up_weight[0], gain_rows], axis=0)
-    parts = gather_parts(own)
+    def schedule(early):
+        early, ids, sending, going_back = lax.optimization_barrier(
+            (early, sample_ids, send_exponent, grad_exponent)
+        )
+        tick = jnp.arange(ticks, dtype=jnp.int32)
+
+        def lane(chunk):
+            active = (chunk >= 0) & (chunk < CHUNKS)
+            chunk = jnp.clip(chunk, 0, CHUNKS - 1)
+            return active.astype(jnp.int32), chunk
+
+        per = TOKENS // ROWS
+        ahead, chunk = lane(tick - STRIDE * section)
+        base = ids[chunk // per] * TOKENS + (chunk % per) * ROWS
+        back, reverse = lane(tick - 2 * DEPTH + STRIDE * section)
+        last = jnp.full((ticks,), section == SECTIONS - 1).astype(jnp.int32)
+        table = jnp.stack([ahead, chunk * ROWS, base, back, reverse * ROWS, last], axis=1)
+
+        def limit(exponent):
+            exponent = exponent[0].reshape(tokens, WIDTH // BLOCK)
+            level = jnp.zeros(exponent.shape, F32)
+            for value in range(LOWEST_EXPONENT, HIGHEST_EXPONENT):
+                level = jnp.where(exponent == value, F32(CLIP_LEVEL * 2.0**value), level)
+            return level
+
+        made = (table, limit(sending), limit(going_back))
+        return lax.optimization_barrier((early, made))
+
+    parts, (table, send_limit, back_limit) = gather_parts(own, schedule)
     pieces, places = [], []
     for (dy, dz), part in parts.items():
         spot = fsdp_index((y + dy) & 3, z ^ dz, core)
@@ -495,28 +526,6 @@
         places += [spot, spot + 1 - 2 * core]
     down, up, gain = assemble(jnp.stack(places).astype(jnp.int32), pieces)
 
-    tick = jnp.arange(ticks, dtype=jnp.int32)
-
-    def lane(chunk):
-        active = (chunk >= 0) & (chunk < CHUNKS)
-        chunk = jnp.clip(chunk, 0, CHUNKS - 1)
-        return active.astype(jnp.int32), chunk
-
-    per = TOKENS // ROWS
-    ahead, chunk = lane(tick - section)
-    base = sample_ids[chunk // per] * TOKENS + (chunk % per) * ROWS
-    back, reverse = lane(tick - 2 * (SECTIONS - 1) + section)
-    last = jnp.full((ticks,), section == SECTIONS - 1).astype(jnp.int32)
-    table = jnp.stack([ahead, chunk * ROWS, base, back, reverse * ROWS, last], axis=1)
-
-    def limit(exponent):
-        exponent = exponent[0].reshape(tokens, WIDTH // BLOCK)
-        level = jnp.zeros(exponent.shape, F32)
-        for value in range(LOWEST_EXPONENT, HIGHEST_EXPONENT):
-            level = jnp.where(exponent == value, F32(CLIP_LEVEL * 2.0**value), level)
-        return level
-
-    send_limit, back_limit = limit(send_exponent), limit(grad_exponent)
     base_in = in_base.reshape(-1, WIDTH)
     base_out = out_base.reshape(-1, WIDTH)
     loss = loss_grad.reshape(tokens, WIDTH)
@@ -537,13 +546,15 @@
     layer, out, neck, act, normed, stat = buffers[:6]
     cots = [*buffers[6:], jnp.zeros((8, WIDTH), F32)]
     zero = jnp.zeros((ROWS, WIDTH), BF16)
-    arriving, returning = zero, zero
+    onward = [(s, s + 1) for s in range(SECTIONS - 1)]
+    inverse = [(s + 1, s) for s in range(SECTIONS - 1)]
+    arriving, returning = [zero] * STRIDE, [zero] * STRIDE
     for step in range(ticks):
-        if step < CHUNKS + SECTIONS - 1:
+        if step < CHUNKS + DEPTH:
             (layer, out, neck, act, normed, stat), delivered = forward_call(
                 step,
                 table,
-                arriving,
+                arriving.pop(0),
                 gain,
                 down,
                 up,
@@ -552,13 +563,12 @@
                 send_limit,
                 (layer, out, neck, act, normed, stat),
             )
-            pairs = [(s, s + 1) for s in range(SECTIONS - 1) if 0 <= step - s < CHUNKS]
-            arriving = lax.ppermute(delivered, "section", pairs) if pairs else zero
-        if step >= SECTIONS - 1:
+            arriving.append(lax.ppermute(delivered, "section", onward))
+        if step >= DEPTH:
             (layer, neck, stat), cots, sent = backward_call(
                 step,
                 table,
-                returning,
+                returning.pop(0),
                 gain,
                 down,
                 up,
@@ -567,12 +577,7 @@
                 (layer, neck, stat),
                 cots,
             )
-            pairs = [
-                (s, s - 1)
-                for s in range(1, SECTIONS)
-                if 0 <= step - 2 * (SECTIONS - 1) + s < CHUNKS
-            ]
-            returning = lax.ppermute(sent, "section", pairs) if pairs else zero
+            returning.append(lax.ppermute(sent, "section", inverse))
 
     grad, cot, neckcot, gain_sums = cots
     order = [((y + dy) & 3) * 2 + (z ^ dz) for dy, dz in REDUCE_ORDER] + [core]

time: 588 us -> 543 us (0.923)
  waiting for transfers between devices: 259 us -> 142 us
  starting transfers between devices: 127 us -> 177 us
  Pallas kernels: 169 us -> 188 us
    ppermute x36 -> x48, waiting for transfers between devices: 201 us -> 76.4 us  [the longest x24 74.5 us: shards(): returning.append(lax.ppermute(sent, 'section', inverse))]
    ppermute x36 -> x48, starting transfers between devices: 78.5 us -> 152 us  [the longest x24 121 us: shards(): arriving.append(lax.ppermute(delivered, 'section', onward))]
    ppermute x10, starting transfers between devices: 32.4 us -> 15.5 us  [along_y(): lax.ppermute(value, 'fsdp', fsdp_pairs(lambda y, z, core: ((y + by) % 4,...]
    pallas_call x19 -> x26, Pallas kernels: 72.9 us -> 82.5 us  [backward_call(): pl.pallas_call(functools.partial(backward_kernel, tick), out_shape=outs,...]
    pallas_call x19 -> x26, Pallas kernels: 83.1 us -> 92.4 us  [forward_call(): pl.pallas_call(functools.partial(forward_kernel, tick), out_shape=outs, i...]
    ppermute x4, waiting for transfers between devices: 1.91 us -> 9.82 us  [along_z(): lax.ppermute(value, 'fsdp', fsdp_pairs(lambda y, z, core: (y, 1 - z, core)))]
    ppermute x4, starting transfers between devices: 14.1 us -> 8.13 us  [along_z(): lax.ppermute(value, 'fsdp', fsdp_pairs(lambda y, z, core: (y, 1 - z, core)))]
  transfers between devices with their start and end apart: 61 -> 73, of which waited for: 35 -> 28; matrix products, arithmetic and copies ran while one was open for 2% -> 2% of each run, Pallas kernels for 11% -> 31%
where the time goes in v3:
time: 543 us; the launch traced here: 533 us
  Pallas kernels  188 us (35%)
  starting transfers between devices  177 us (33%)
  waiting for transfers between devices  142 us (26%)
  local copies, waits for them, and re-layouts  12.9 us (2%)
  other arithmetic  11.3 us (2%)
    ppermute x24, starting transfers between devices, shards(): arriving.append(lax.ppermute(delivered, 'section', onward))  121 us
    pallas_call x26, Pallas kernels, forward_call(): pl.pallas_call(functools.partial(forward_kernel, tick), out_shape=outs, i...  92.4 us
    pallas_call x26, Pallas kernels, backward_call(): pl.pallas_call(functools.partial(backward_kernel, tick), out_shape=outs,...  82.5 us
    ppermute x24, waiting for transfers between devices, shards(): returning.append(lax.ppermute(sent, 'section', inverse))  74.5 us
    ppermute x10, waiting for transfers between devices, along_y(): lax.ppermute(value, 'fsdp', fsdp_pairs(lambda y, z, core: ((y + by) % 4,...  51.3 us
    ppermute x24, starting transfers between devices, shards(): returning.append(lax.ppermute(sent, 'section', inverse))  31 us
    ppermute x10, starting transfers between devices, along_y(): lax.ppermute(value, 'fsdp', fsdp_pairs(lambda y, z, core: ((y + by) % 4,...  15.5 us
  transfers between devices with their start and end apart: 73, of which 28 were waited for; matrix products, arithmetic and copies ran while one was open for 2% of the time, Pallas kernels for 31%

profile of v3, /device:TPU:0, one launch (start us, length us, event | category | flops | bytes accessed | tf_op | source)
XLA Modules:
  0.0 533.2 jit_solution(13538170452348045162)
XLA Ops:
  4.0 4.0 collective-permute-start.1
  8.1 3.2 collective-permute-start.8
  11.9 2.6 collective-permute-start.4
  14.5 7.4 %collective-permute-done.1.refs_2_ = bf16[1168,256]{1,0:T(8,128)(2,1)S(1)} collective-permute-done((bf16[1168,256]{1,0:T(8,128)(2,1)S(1)}, bf16[1168,256]{1,0:T(8,128)(2,1)S(1)}, u32[]{:S(2)}, u32[]{:S(2)}) %collective-permute-start.1) | collective-permute-done | bytes 598048 | tf_op jit(solution)/shard_map/ppermute | solution.py:368
  23.3 2.6 fusion.15
  27.0 3.3 collective-permute-start.10
  30.3 7.4 %collective-permute-done.6.refs_6_ = bf16[1168,256]{1,0:T(8,128)(2,1)S(1)} collective-permute-done((bf16[1168,256]{1,0:T(8,128)(2,1)S(1)}, bf16[1168,256]{1,0:T(8,128)(2,1)S(1)}, u32[]{:S(2)}, u32[]{:S(2)}) %collective-permute-start.6) | collective-permute-done | bytes 598048 | tf_op jit(solution)/shard_map/ppermute | solution.py:372
  41.3 2.4 collective-permute-done.10.refs_10_
  46.0 8.9 %collective-permute-done.14.refs_14_ = bf16[1168,256]{1,0:T(8,128)(2,1)} collective-permute-done((bf16[1168,256]{1,0:T(8,128)(2,1)S(1)}, bf16[1168,256]{1,0:T(8,128)(2,1)}, u32[]{:S(2)}, u32[]{:S(2)}) %collective-permute-start.14) | collective-permute-done | bytes 598048 | tf_op jit(solution)/shard_map/ppermute | solution.py:372
  60.3 3.1 assemble_weights.1
  63.5 6.6 %section_forward.26 = (bf16[192,9216]{1,0:T(8,128)(2,1)}, bf16[192,9216]{1,0:T(8,128)(2,1)}, f32[192,256]{1,0:T(8,128)}, bf16[192,256]{1,0:T(8,128)(2,1)}, bf16[...) custom-call(s32[40,6]{1,0:T(8,128)S(1)} %copy.388.table, ...), custom_call_target="tpu_custom_call", output_to_operand_aliasing={{0}: (8, {}), {1}: (9, {}), {2}: (10, {}), {3}: (11, {}), {... | custom-call | flops 150000000 | bytes 9000000 | tf_op jit(solution)/shard_map/section_forward/pallas_call | solution.py:258
  71.4 6.4 %section_forward.27 = (bf16[192,9216]{1,0:T(8,128)(2,1)}, bf16[192,9216]{1,0:T(8,128)(2,1)}, f32[192,256]{1,0:T(8,128)}, bf16[192,256]{1,0:T(8,128)(2,1)}, bf16[...) custom-call(s32[40,6]{1,0:T(8,128)S(1)} %copy.388.table, ...), custom_call_target="tpu_custom_call", output_to_operand_aliasing={{0}: (8, {}), {1}: (9, {}), {2}: (10, {}), {3}: (11, {}), {... | custom-call | flops 150000000 | bytes 9000000 | tf_op jit(solution)/shard_map/section_forward/pallas_call | solution.py:258
  79.1 6.9 %section_forward.28 = (bf16[192,9216]{1,0:T(8,128)(2,1)}, bf16[192,9216]{1,0:T(8,128)(2,1)}, f32[192,256]{1,0:T(8,128)}, bf16[192,256]{1,0:T(8,128)(2,1)}, bf16[...) custom-call(s32[40,6]{1,0:T(8,128)S(1)} %copy.388.table, ...), custom_call_target="tpu_custom_call", output_to_operand_aliasing={{0}: (8, {}), {1}: (9, {}), {2}: (10, {}), {3}: (11, {}), {... | custom-call | flops 150000000 | bytes 9000000 | tf_op jit(solution)/shard_map/section_forward/pallas_call | solution.py:258
  86.0 3.5 collective-permute-start.19
  89.5 6.4 %section_forward.29 = (bf16[192,9216]{1,0:T(8,128)(2,1)}, bf16[192,9216]{1,0:T(8,128)(2,1)}, f32[192,256]{1,0:T(8,128)}, bf16[192,256]{1,0:T(8,128)(2,1)}, bf16[...) custom-call(s32[40,6]{1,0:T(8,128)S(1)} %copy.388.table, ...), custom_call_target="tpu_custom_call", output_to_operand_aliasing={{0}: (8, {}), {1}: (9, {}), {2}: (10, {}), {3}: (11, {}), {... | custom-call | flops 150000000 | bytes 9000000 | tf_op jit(solution)/shard_map/section_forward/pallas_call | solution.py:258
  97.8 6.4 %section_forward.30 = (bf16[192,9216]{1,0:T(8,128)(2,1)}, bf16[192,9216]{1,0:T(8,128)(2,1)}, f32[192,256]{1,0:T(8,128)}, bf16[192,256]{1,0:T(8,128)(2,1)}, bf16[...) custom-call(s32[40,6]{1,0:T(8,128)S(1)} %copy.388.table, ...), custom_call_target="tpu_custom_call", output_to_operand_aliasing={{0}: (8, {}), {1}: (9, {}), {2}: (10, {}), {3}: (11, {}), {... | custom-call | flops 150000000 | bytes 9000000 | tf_op jit(solution)/shard_map/section_forward/pallas_call | solution.py:258
  106.3 6.4 %section_forward.31 = (bf16[192,9216]{1,0:T(8,128)(2,1)}, bf16[192,9216]{1,0:T(8,128)(2,1)}, f32[192,256]{1,0:T(8,128)}, bf16[192,256]{1,0:T(8,128)(2,1)}, bf16[...) custom-call(s32[40,6]{1,0:T(8,128)S(1)} %copy.388.table, ...), custom_call_target="tpu_custom_call", output_to_operand_aliasing={{0}: (8, {}), {1}: (9, {}), {2}: (10, {}), {3}: (11, {}), {... | custom-call | flops 150000000 | bytes 9000000 | tf_op jit(solution)/shard_map/section_forward/pallas_call | solution.py:258
  114.9 6.4 %section_forward.32 = (bf16[192,9216]{1,0:T(8,128)(2,1)}, bf16[192,9216]{1,0:T(8,128)(2,1)}, f32[192,256]{1,0:T(8,128)}, bf16[192,256]{1,0:T(8,128)(2,1)}, bf16[...) custom-call(s32[40,6]{1,0:T(8,128)S(1)} %copy.388.table, ...), custom_call_target="tpu_custom_call", output_to_operand_aliasing={{0}: (8, {}), {1}: (9, {}), {2}: (10, {}), {3}: (11, {}), {... | custom-call | flops 150000000 | bytes 9000000 | tf_op jit(solution)/shard_map/section_forward/pallas_call | solution.py:258
  123.2 6.5 %section_forward.33 = (bf16[192,9216]{1,0:T(8,128)(2,1)}, bf16[192,9216]{1,0:T(8,128)(2,1)}, f32[192,256]{1,0:T(8,128)}, bf16[192,256]{1,0:T(8,128)(2,1)}, bf16[...) custom-call(s32[40,6]{1,0:T(8,128)S(1)} %copy.388.table, ...), custom_call_target="tpu_custom_call", output_to_operand_aliasing={{0}: (8, {}), {1}: (9, {}), {2}: (10, {}), {3}: (11, {}), {... | custom-call | flops 150000000 | bytes 9000000 | tf_op jit(solution)/shard_map/section_forward/pallas_call | solution.py:258
  131.6 6.4 %section_forward.34 = (bf16[192,9216]{1,0:T(8,128)(2,1)}, bf16[192,9216]{1,0:T(8,128)(2,1)}, f32[192,256]{1,0:T(8,128)}, bf16[192,256]{1,0:T(8,128)(2,1)}, bf16[...) custom-call(s32[40,6]{1,0:T(8,128)S(1)} %copy.388.table, ...), custom_call_target="tpu_custom_call", output_to_operand_aliasing={{0}: (8, {}), {1}: (9, {}), {2}: (10, {}), {3}: (11, {}), {... | custom-call | flops 150000000 | bytes 9000000 | tf_op jit(solution)/shard_map/section_forward/pallas_call | solution.py:258
  139.9 6.4 %section_forward.35 = (bf16[192,9216]{1,0:T(8,128)(2,1)}, bf16[192,9216]{1,0:T(8,128)(2,1)}, f32[192,256]{1,0:T(8,128)}, bf16[192,256]{1,0:T(8,128)(2,1)}, bf16[...) custom-call(s32[40,6]{1,0:T(8,128)S(1)} %copy.388.table, ...), custom_call_target="tpu_custom_call", output_to_operand_aliasing={{0}: (8, {}), {1}: (9, {}), {2}: (10, {}), {3}: (11, {}), {... | custom-call | flops 150000000 | bytes 9000000 | tf_op jit(solution)/shard_map/section_forward/pallas_call | solution.py:258
  148.2 6.4 %section_forward.36 = (bf16[192,9216]{1,0:T(8,128)(2,1)}, bf16[192,9216]{1,0:T(8,128)(2,1)}, f32[192,256]{1,0:T(8,128)}, bf16[192,256]{1,0:T(8,128)(2,1)}, bf16[...) custom-call(s32[40,6]{1,0:T(8,128)S(1)} %copy.388.table, ...), custom_call_target="tpu_custom_call", output_to_operand_aliasing={{0}: (8, {}), {1}: (9, {}), {2}: (10, {}), {3}: (11, {}), {... | custom-call | flops 150000000 | bytes 9000000 | tf_op jit(solution)/shard_map/section_forward/pallas_call | solution.py:258
  156.5 6.4 %section_forward.37 = (bf16[192,9216]{1,0:T(8,128)(2,1)}, bf16[192,9216]{1,0:T(8,128)(2,1)}, f32[192,256]{1,0:T(8,128)}, bf16[192,256]{1,0:T(8,128)(2,1)}, bf16[...) custom-call(s32[40,6]{1,0:T(8,128)S(1)} %copy.388.table, ...), custom_call_target="tpu_custom_call", output_to_operand_aliasing={{0}: (8, {}), {1}: (9, {}), {2}: (10, {}), {3}: (11, {}), {... | custom-call | flops 150000000 | bytes 9000000 | tf_op jit(solution)/shard_map/section_forward/pallas_call | solution.py:258
  162.9 3.0 collective-permute-start.26
  167.1 7.5 %collective-permute-start.29 = (bf16[16,9216]{1,0:T(8,128)(2,1)S(1)}, bf16[16,9216]{1,0:T(8,128)(2,1)S(1)}, u32[]{:S(2)}, u32[]{:S(2)}) collective-permute-start(bf16[16,9216]{1,0:T(8,128)(2,1)S(1)} %get-tuple-element.520), channel_id=1, source_target_pairs={{0,16},{16,32},{32,48},{48,64},{64,80},{80,96},{96,112},{1,17},{17... | collective-permute-start | bytes 884744 | tf_op jit(solution)/shard_map/ppermute | solution.py:566
  175.6 7.6 %collective-permute-start.28 = (bf16[16,9216]{1,0:T(8,128)(2,1)S(1)}, bf16[16,9216]{1,0:T(8,128)(2,1)S(1)}, u32[]{:S(2)}, u32[]{:S(2)}) collective-permute-start(bf16[16,9216]{1,0:T(8,128)(2,1)S(1)} %get-tuple-element.518), channel_id=1, source_target_pairs={{0,16},{16,32},{32,48},{48,64},{64,80},{80,96},{96,112},{1,17},{17... | collective-permute-start | bytes 884744 | tf_op jit(solution)/shard_map/ppermute | solution.py:566
  191.3 6.5 %collective-permute-start.30 = (bf16[16,9216]{1,0:T(8,128)(2,1)S(1)}, bf16[16,9216]{1,0:T(8,128)(2,1)S(1)}, u32[]{:S(2)}, u32[]{:S(2)}) collective-permute-start(bf16[16,9216]{1,0:T(8,128)(2,1)S(1)} %get-tuple-element.539), channel_id=1, source_target_pairs={{0,16},{16,32},{32,48},{48,64},{64,80},{80,96},{96,112},{1,17},{17... | collective-permute-start | bytes 884744 | tf_op jit(solution)/shard_map/ppermute | solution.py:566
  201.6 9.9 %collective-permute-start.35 = (bf16[16,9216]{1,0:T(8,128)(2,1)S(1)}, bf16[16,9216]{1,0:T(8,128)(2,1)S(1)}, u32[]{:S(2)}, u32[]{:S(2)}) collective-permute-start(bf16[16,9216]{1,0:T(8,128)(2,1)S(1)} %get-tuple-element.570), channel_id=1, source_target_pairs={{0,16},{16,32},{32,48},{48,64},{64,80},{80,96},{96,112},{1,17},{17... | collective-permute-start | bytes 884744 | tf_op jit(solution)/shard_map/ppermute | solution.py:566
  214.9 4.6 collective-permute-start.33
  222.8 8.5 %collective-permute-start.39 = (bf16[16,9216]{1,0:T(8,128)(2,1)S(1)}, bf16[16,9216]{1,0:T(8,128)(2,1)S(1)}, u32[]{:S(2)}, u32[]{:S(2)}) collective-permute-start(bf16[16,9216]{1,0:T(8,128)(2,1)S(1)} %get-tuple-element.600), channel_id=1, source_target_pairs={{0,16},{16,32},{32,48},{48,64},{64,80},{80,96},{96,112},{1,17},{17... | collective-permute-start | bytes 884744 | tf_op jit(solution)/shard_map/ppermute | solution.py:566
  234.7 12.0 %collective-permute-start.37 = (bf16[16,9216]{1,0:T(8,128)(2,1)S(1)}, bf16[16,9216]{1,0:T(8,128)(2,1)S(1)}, u32[]{:S(2)}, u32[]{:S(2)}) collective-permute-start(bf16[16,9216]{1,0:T(8,128)(2,1)S(1)} %get-tuple-element.598), channel_id=1, source_target_pairs={{0,16},{16,32},{32,48},{48,64},{64,80},{80,96},{96,112},{1,17},{17... | collective-permute-start | bytes 884744 | tf_op jit(solution)/shard_map/ppermute | solution.py:566
  250.1 6.7 %collective-permute-start.43 = (bf16[16,9216]{1,0:T(8,128)(2,1)S(1)}, bf16[16,9216]{1,0:T(8,128)(2,1)S(1)}, u32[]{:S(2)}, u32[]{:S(2)}) collective-permute-start(bf16[16,9216]{1,0:T(8,128)(2,1)S(1)} %get-tuple-element.630), channel_id=1, source_target_pairs={{0,16},{16,32},{32,48},{48,64},{64,80},{80,96},{96,112},{1,17},{17... | collective-permute-start | bytes 884744 | tf_op jit(solution)/shard_map/ppermute | solution.py:566
  260.1 12.0 %collective-permute-start.41 = (bf16[16,9216]{1,0:T(8,128)(2,1)S(1)}, bf16[16,9216]{1,0:T(8,128)(2,1)S(1)}, u32[]{:S(2)}, u32[]{:S(2)}) collective-permute-start(bf16[16,9216]{1,0:T(8,128)(2,1)S(1)} %get-tuple-element.628), channel_id=1, source_target_pairs={{0,16},{16,32},{32,48},{48,64},{64,80},{80,96},{96,112},{1,17},{17... | collective-permute-start | bytes 884744 | tf_op jit(solution)/shard_map/ppermute | solution.py:566
  275.9 12.0 %collective-permute-start.47 = (bf16[16,9216]{1,0:T(8,128)(2,1)S(1)}, bf16[16,9216]{1,0:T(8,128)(2,1)S(1)}, u32[]{:S(2)}, u32[]{:S(2)}) collective-permute-start(bf16[16,9216]{1,0:T(8,128)(2,1)S(1)} %get-tuple-element.660), channel_id=1, source_target_pairs={{0,16},{16,32},{32,48},{48,64},{64,80},{80,96},{96,112},{1,17},{17... | collective-permute-start | bytes 884744 | tf_op jit(solution)/shard_map/ppermute | solution.py:566
  291.2 6.7 %collective-permute-start.45 = (bf16[16,9216]{1,0:T(8,128)(2,1)S(1)}, bf16[16,9216]{1,0:T(8,128)(2,1)S(1)}, u32[]{:S(2)}, u32[]{:S(2)}) collective-permute-start(bf16[16,9216]{1,0:T(8,128)(2,1)S(1)} %get-tuple-element.658), channel_id=1, source_target_pairs={{0,16},{16,32},{32,48},{48,64},{64,80},{80,96},{96,112},{1,17},{17... | collective-permute-start | bytes 884744 | tf_op jit(solution)/shard_map/ppermute | solution.py:566
  306.1 11.1 %collective-permute-done.49.incoming = bf16[16,9216]{1,0:T(8,128)(2,1)S(1)} collective-permute-done((bf16[16,9216]{1,0:T(8,128)(2,1)S(1)}, bf16[16,9216]{1,0:T(8,128)(2,1)S(1)}, u32[]{:S(2)}, u32[]{:S(2)}) %collective-permute-start.49) | collective-permute-done | bytes 294944 | tf_op jit(solution)/shard_map/ppermute | solution.py:580
  323.6 18.1 %collective-permute-done.50.incoming = bf16[16,9216]{1,0:T(8,128)(2,1)S(1)} collective-permute-done((bf16[16,9216]{1,0:T(8,128)(2,1)S(1)}, bf16[16,9216]{1,0:T(8,128)(2,1)S(1)}, u32[]{:S(2)}, u32[]{:S(2)}) %collective-permute-start.50) | collective-permute-done | bytes 294944 | tf_op jit(solution)/shard_map/ppermute | solution.py:580
  344.0 11.7 %collective-permute-done.53.incoming = bf16[16,9216]{1,0:T(8,128)(2,1)S(1)} collective-permute-done((bf16[16,9216]{1,0:T(8,128)(2,1)S(1)}, bf16[16,9216]{1,0:T(8,128)(2,1)S(1)}, u32[]{:S(2)}, u32[]{:S(2)}) %collective-permute-start.53) | collective-permute-done | bytes 294944 | tf_op jit(solution)/shard_map/ppermute | solution.py:580
  355.7 5.4 %section_backward.40 = (bf16[192,9216]{1,0:T(8,128)(2,1)}, f32[192,256]{1,0:T(8,128)}, f32[192,256]{1,0:T(8,128)}, bf16[192,9216]{1,0:T(8,128)(2,1)}, bf16[192,9...) custom-call(s32[40,6]{1,0:T(8,128)S(1)} %copy.388.table, ...), custom_call_target="tpu_custom_call", output_to_operand_aliasing={{0}: (7, {}), {1}: (8, {}), {2}: (9, {}), {3}: (10, {}), {4... | custom-call | flops 150000000 | bytes 9000000 | tf_op jit(solution)/shard_map/section_backward/pallas_call | solution.py:287
  362.4 10.1 %collective-permute-done.52.incoming = bf16[16,9216]{1,0:T(8,128)(2,1)S(1)} collective-permute-done((bf16[16,9216]{1,0:T(8,128)(2,1)S(1)}, bf16[16,9216]{1,0:T(8,128)(2,1)S(1)}, u32[]{:S(2)}, u32[]{:S(2)}) %collective-permute-start.52) | collective-permute-done | bytes 294944 | tf_op jit(solution)/shard_map/ppermute | solution.py:580
  372.6 5.8 %section_backward.41 = (bf16[192,9216]{1,0:T(8,128)(2,1)}, f32[192,256]{1,0:T(8,128)}, f32[192,256]{1,0:T(8,128)}, bf16[192,9216]{1,0:T(8,128)(2,1)}, bf16[192,9...) custom-call(s32[40,6]{1,0:T(8,128)S(1)} %copy.388.table, ...), custom_call_target="tpu_custom_call", output_to_operand_aliasing={{0}: (7, {}), {1}: (8, {}), {2}: (9, {}), {3}: (10, {}), {4... | custom-call | flops 150000000 | bytes 9000000 | tf_op jit(solution)/shard_map/section_backward/pallas_call | solution.py:287
  379.7 2.7 collective-permute-done.55.incoming
  382.4 5.4 %section_backward.42 = (bf16[192,9216]{1,0:T(8,128)(2,1)}, f32[192,256]{1,0:T(8,128)}, f32[192,256]{1,0:T(8,128)}, bf16[192,9216]{1,0:T(8,128)(2,1)}, bf16[192,9...) custom-call(s32[40,6]{1,0:T(8,128)S(1)} %copy.388.table, ...), custom_call_target="tpu_custom_call", output_to_operand_aliasing={{0}: (7, {}), {1}: (8, {}), {2}: (9, {}), {3}: (10, {}), {4... | custom-call | flops 150000000 | bytes 9000000 | tf_op jit(solution)/shard_map/section_backward/pallas_call | solution.py:287
  389.1 3.2 collective-permute-done.54.incoming
  392.3 5.4 %section_backward.43 = (bf16[192,9216]{1,0:T(8,128)(2,1)}, f32[192,256]{1,0:T(8,128)}, f32[192,256]{1,0:T(8,128)}, bf16[192,9216]{1,0:T(8,128)(2,1)}, bf16[192,9...) custom-call(s32[40,6]{1,0:T(8,128)S(1)} %copy.388.table, ...), custom_call_target="tpu_custom_call", output_to_operand_aliasing={{0}: (7, {}), {1}: (8, {}), {2}: (9, {}), {3}: (10, {}), {4... | custom-call | flops 150000000 | bytes 9000000 | tf_op jit(solution)/shard_map/section_backward/pallas_call | solution.py:287
  399.1 3.5 collective-permute-done.57.incoming
  402.6 5.4 %section_backward.44 = (bf16[192,9216]{1,0:T(8,128)(2,1)}, f32[192,256]{1,0:T(8,128)}, f32[192,256]{1,0:T(8,128)}, bf16[192,9216]{1,0:T(8,128)(2,1)}, bf16[192,9...) custom-call(s32[40,6]{1,0:T(8,128)S(1)} %copy.388.table, ...), custom_call_target="tpu_custom_call", output_to_operand_aliasing={{0}: (7, {}), {1}: (8, {}), {2}: (9, {}), {3}: (10, {}), {4... | custom-call | flops 150000000 | bytes 9000000 | tf_op jit(solution)/shard_map/section_backward/pallas_call | solution.py:287
  409.3 4.1 collective-permute-done.56.incoming
  413.4 5.4 %section_backward.45 = (bf16[192,9216]{1,0:T(8,128)(2,1)}, f32[192,256]{1,0:T(8,128)}, f32[192,256]{1,0:T(8,128)}, bf16[192,9216]{1,0:T(8,128)(2,1)}, bf16[192,9...) custom-call(s32[40,6]{1,0:T(8,128)S(1)} %copy.388.table, ...), custom_call_target="tpu_custom_call", output_to_operand_aliasing={{0}: (7, {}), {1}: (8, {}), {2}: (9, {}), {3}: (10, {}), {4... | custom-call | flops 150000000 | bytes 9000000 | tf_op jit(solution)/shard_map/section_backward/pallas_call | solution.py:287
  420.2 3.7 collective-permute-done.59.incoming
  423.8 5.4 %section_backward.46 = (bf16[192,9216]{1,0:T(8,128)(2,1)}, f32[192,256]{1,0:T(8,128)}, f32[192,256]{1,0:T(8,128)}, bf16[192,9216]{1,0:T(8,128)(2,1)}, bf16[192,9...) custom-call(s32[40,6]{1,0:T(8,128)S(1)} %copy.388.table, ...), custom_call_target="tpu_custom_call", output_to_operand_aliasing={{0}: (7, {}), {1}: (8, {}), {2}: (9, {}), {3}: (10, {}), {4... | custom-call | flops 150000000 | bytes 9000000 | tf_op jit(solution)/shard_map/section_backward/pallas_call | solution.py:287
  431.2 5.6 %section_backward.47 = (bf16[192,9216]{1,0:T(8,128)(2,1)}, f32[192,256]{1,0:T(8,128)}, f32[192,256]{1,0:T(8,128)}, bf16[192,9216]{1,0:T(8,128)(2,1)}, bf16[192,9...) custom-call(s32[40,6]{1,0:T(8,128)S(1)} %copy.388.table, ...), custom_call_target="tpu_custom_call", output_to_operand_aliasing={{0}: (7, {}), {1}: (8, {}), {2}: (9, {}), {3}: (10, {}), {4... | custom-call | flops 150000000 | bytes 9000000 | tf_op jit(solution)/shard_map/section_backward/pallas_call | solution.py:287
  439.9 5.4 %section_backward.48 = (bf16[192,9216]{1,0:T(8,128)(2,1)}, f32[192,256]{1,0:T(8,128)}, f32[192,256]{1,0:T(8,128)}, bf16[192,9216]{1,0:T(8,128)(2,1)}, bf16[192,9...) custom-call(s32[40,6]{1,0:T(8,128)S(1)} %copy.388.table, ...), custom_call_target="tpu_custom_call", output_to_operand_aliasing={{0}: (7, {}), {1}: (8, {}), {2}: (9, {}), {3}: (10, {}), {4... | custom-call | flops 150000000 | bytes 9000000 | tf_op jit(solution)/shard_map/section_backward/pallas_call | solution.py:287
  447.3 5.4 %section_backward.49 = (bf16[192,9216]{1,0:T(8,128)(2,1)}, f32[192,256]{1,0:T(8,128)}, f32[192,256]{1,0:T(8,128)}, bf16[192,9216]{1,0:T(8,128)(2,1)}, bf16[192,9...) custom-call(s32[40,6]{1,0:T(8,128)S(1)} %copy.388.table, ...), custom_call_target="tpu_custom_call", output_to_operand_aliasing={{0}: (7, {}), {1}: (8, {}), {2}: (9, {}), {3}: (10, {}), {4... | custom-call | flops 150000000 | bytes 9000000 | tf_op jit(solution)/shard_map/section_backward/pallas_call | solution.py:287
  455.7 2.3 copy-done.1
  458.0 2.3 copy-done.3
  460.3 6.1 %section_backward.50 = (bf16[192,9216]{1,0:T(8,128)(2,1)}, f32[192,256]{1,0:T(8,128)}, f32[192,256]{1,0:T(8,128)}, bf16[192,9216]{1,0:T(8,128)(2,1)}, bf16[192,9...) custom-call(s32[40,6]{1,0:T(8,128)S(1)} %copy.388.table, ...), custom_call_target="tpu_custom_call", output_to_operand_aliasing={{0}: (7, {}), {1}: (8, {}), {2}: (9, {}), {3}: (10, {}), {4... | custom-call | flops 150000000 | bytes 9000000 | tf_op jit(solution)/shard_map/section_backward/pallas_call | solution.py:287
  466.5 6.2 %section_backward.51 = (bf16[192,9216]{1,0:T(8,128)(2,1)}, f32[192,256]{1,0:T(8,128)}, f32[192,256]{1,0:T(8,128)}, bf16[192,9216]{1,0:T(8,128)(2,1)}, bf16[192,9...) custom-call(s32[40,6]{1,0:T(8,128)S(1)} %copy.388.table, ...), custom_call_target="tpu_custom_call", output_to_operand_aliasing={{0}: (7, {}), {1}: (8, {}), {2}: (9, {}), {3}: (10, {}), {4... | custom-call | flops 150000000 | bytes 9000000 | tf_op jit(solution)/shard_map/section_backward/pallas_call | solution.py:287
  473.6 4.9 gradient_blocks.3
  478.6 4.9 gradient_blocks.2
  489.4 2.5 collective-permute-start.67
  491.8 9.3 %collective-permute-done.71 = bf16[1168,256]{1,0:T(8,128)(2,1)S(1)} collective-permute-done((bf16[1168,256]{1,0:T(8,128)(2,1)S(1)}, bf16[1168,256]{1,0:T(8,128)(2,1)S(1)}, u32[]{:S(2)}, u32[]{:S(2)}) %collective-permute-start.71) | collective-permute-done | bytes 598048 | tf_op jit(solution)/shard_map/ppermute | solution.py:372
  501.1 3.4 collective-permute-done.70
  507.2 21.8 %collective-permute-done.66 = bf16[1168,256]{1,0:T(8,128)(2,1)} collective-permute-done((bf16[1168,256]{1,0:T(8,128)(2,1)S(1)}, bf16[1168,256]{1,0:T(8,128)(2,1)}, u32[]{:S(2)}, u32[]{:S(2)}) %collective-permute-start.66) | collective-permute-done | bytes 598048 | tf_op jit(solution)/shard_map/ppermute | solution.py:372
  (182 shorter events, 121.6 us)
Async XLA Ops:
  4.0 17.9 %collective-permute-start.1 = (bf16[1168,256]{1,0:T(8,128)(2,1)S(1)}, bf16[1168,256]{1,0:T(8,128)(2,1)S(1)}, u32[]{:S(2)}, u32[]{:S(2)}) collective-permute-start(bf16[1168,256]{1,0:T(8,128)(2,1)S(1)} %fusion.7.refs_0_), channel_id=1, source_target_pairs={{0,2},{1,3},{2,0},{3,1},{4,6},{5,7},{6,4},{7,5},{8,10},{9,11},{10,... | collective-permute-start | bytes 1794056 | tf_op jit(solution)/shard_map/ppermute | solution.py:368
  8.1 18.9 %collective-permute-start.8 = (bf16[1168,256]{1,0:T(8,128)(2,1)S(1)}, bf16[1168,256]{1,0:T(8,128)(2,1)S(1)}, u32[]{:S(2)}, u32[]{:S(2)}) collective-permute-start(bf16[1168,256]{1,0:T(8,128)(2,1)S(1)} %fusion.7.refs_0_), channel_id=1, source_target_pairs={{0,8},{1,9},{2,10},{3,11},{4,12},{5,13},{6,14},{7,15},{8,0},{9,1},... | collective-permute-start | bytes 1794056 | tf_op jit(solution)/shard_map/ppermute | solution.py:372
  11.3 26.4 %collective-permute-start.6 = (bf16[1168,256]{1,0:T(8,128)(2,1)S(1)}, bf16[1168,256]{1,0:T(8,128)(2,1)S(1)}, u32[]{:S(2)}, u32[]{:S(2)}) collective-permute-start(bf16[1168,256]{1,0:T(8,128)(2,1)S(1)} %fusion.7.refs_0_), channel_id=1, source_target_pairs={{0,4},{1,5},{2,6},{3,7},{4,8},{5,9},{6,10},{7,11},{8,12},{9,13},{1... | collective-permute-start | bytes 1794056 | tf_op jit(solution)/shard_map/ppermute | solution.py:372
  11.9 26.1 %collective-permute-start.4 = (bf16[1168,256]{1,0:T(8,128)(2,1)S(1)}, bf16[1168,256]{1,0:T(8,128)(2,1)S(1)}, u32[]{:S(2)}, u32[]{:S(2)}) collective-permute-start(bf16[1168,256]{1,0:T(8,128)(2,1)S(1)} %fusion.7.refs_0_), channel_id=1, source_target_pairs={{0,12},{1,13},{2,14},{3,15},{4,0},{5,1},{6,2},{7,3},{8,4},{9,5},{1... | collective-permute-start | bytes 1794056 | tf_op jit(solution)/shard_map/ppermute | solution.py:372
  14.5 24.9 %collective-permute-start.2 = (bf16[1168,256]{1,0:T(8,128)(2,1)S(1)}, bf16[1168,256]{1,0:T(8,128)(2,1)}, u32[]{:S(2)}, u32[]{:S(2)}) collective-permute-start(bf16[1168,256]{1,0:T(8,128)(2,1)S(1)} %fusion.7.refs_0_), channel_id=1, source_target_pairs={{0,1},{1,0},{2,3},{3,2},{4,5},{5,4},{6,7},{7,6},{8,9},{9,8},{10,11... | collective-permute-start | bytes 1794056 | tf_op jit(solution)/shard_map/ppermute | solution.py:364
  27.0 16.8 %collective-permute-start.10 = (bf16[1168,256]{1,0:T(8,128)(2,1)S(1)}, bf16[1168,256]{1,0:T(8,128)(2,1)}, u32[]{:S(2)}, u32[]{:S(2)}) collective-permute-start(bf16[1168,256]{1,0:T(8,128)(2,1)S(1)} %collective-permute-done.8.refs_8_), channel_id=1, source_target_pairs={{0,2},{1,3},{2,0},{3,1},{4,6},{5,7},{6,4},{7,5},{8,10},{9,11},{10,... | collective-permute-start | bytes 1794056 | tf_op jit(solution)/shard_map/ppermute | solution.py:368
  30.3 13.4 %collective-permute-start.9 = (bf16[1168,256]{1,0:T(8,128)(2,1)S(1)}, bf16[1168,256]{1,0:T(8,128)(2,1)S(1)}, u32[]{:S(2)}, u32[]{:S(2)}) collective-permute-start(bf16[1168,256]{1,0:T(8,128)(2,1)S(1)} %collective-permute-done.8.refs_8_), channel_id=1, source_target_pairs={{0,1},{1,0},{2,3},{3,2},{4,5},{5,4},{6,7},{7,6},{8,9},{9,8},{10,11... | collective-permute-start | bytes 1794056 | tf_op jit(solution)/shard_map/ppermute | solution.py:364
  38.1 16.9 %collective-permute-start.14 = (bf16[1168,256]{1,0:T(8,128)(2,1)S(1)}, bf16[1168,256]{1,0:T(8,128)(2,1)}, u32[]{:S(2)}, u32[]{:S(2)}) collective-permute-start(bf16[1168,256]{1,0:T(8,128)(2,1)S(1)} %collective-permute-done.1.refs_2_), channel_id=1, source_target_pairs={{0,4},{1,5},{2,6},{3,7},{4,8},{5,9},{6,10},{7,11},{8,12},{9,13},{1... | collective-permute-start | bytes 1794056 | tf_op jit(solution)/shard_map/ppermute | solution.py:372
  39.4 15.7 %collective-permute-start.12 = (bf16[1168,256]{1,0:T(8,128)(2,1)S(1)}, bf16[1168,256]{1,0:T(8,128)(2,1)}, u32[]{:S(2)}, u32[]{:S(2)}) collective-permute-start(bf16[1168,256]{1,0:T(8,128)(2,1)S(1)} %collective-permute-done.1.refs_2_), channel_id=1, source_target_pairs={{0,12},{1,13},{2,14},{3,15},{4,0},{5,1},{6,2},{7,3},{8,4},{9,5},{1... | collective-permute-start | bytes 1794056 | tf_op jit(solution)/shard_map/ppermute | solution.py:372
  43.8 11.9 %collective-permute-start.3 = (bf16[1168,256]{1,0:T(8,128)(2,1)S(1)}, bf16[1168,256]{1,0:T(8,128)(2,1)}, u32[]{:S(2)}, u32[]{:S(2)}) collective-permute-start(bf16[1168,256]{1,0:T(8,128)(2,1)S(1)} %collective-permute-done.1.refs_2_), channel_id=1, source_target_pairs={{0,1},{1,0},{2,3},{3,2},{4,5},{5,4},{6,7},{7,6},{8,9},{9,8},{10,11... | collective-permute-start | bytes 1794056 | tf_op jit(solution)/shard_map/ppermute | solution.py:364
  44.6 11.0 %collective-permute-start.5 = (bf16[1168,256]{1,0:T(8,128)(2,1)S(1)}, bf16[1168,256]{1,0:T(8,128)(2,1)}, u32[]{:S(2)}, u32[]{:S(2)}) collective-permute-start(bf16[1168,256]{1,0:T(8,128)(2,1)S(1)} %collective-permute-done.4.refs_4_), channel_id=1, source_target_pairs={{0,1},{1,0},{2,3},{3,2},{4,5},{5,4},{6,7},{7,6},{8,9},{9,8},{10,11... | collective-permute-start | bytes 1794056 | tf_op jit(solution)/shard_map/ppermute | solution.py:364
  77.7 11.7 %collective-permute-start.16 = (bf16[16,9216]{1,0:T(8,128)(2,1)S(1)}, bf16[16,9216]{1,0:T(8,128)(2,1)S(1)}, u32[]{:S(2)}, u32[]{:S(2)}) collective-permute-start(bf16[16,9216]{1,0:T(8,128)(2,1)S(1)} %get-tuple-element.434), channel_id=1, source_target_pairs={{0,16},{16,32},{32,48},{48,64},{64,80},{80,96},{96,112},{1,17},{17... | collective-permute-start | bytes 884744 | tf_op jit(solution)/shard_map/ppermute | solution.py:566
  86.0 11.8 %collective-permute-start.19 = (bf16[16,9216]{1,0:T(8,128)(2,1)S(1)}, bf16[16,9216]{1,0:T(8,128)(2,1)S(1)}, u32[]{:S(2)}, u32[]{:S(2)}) collective-permute-start(bf16[16,9216]{1,0:T(8,128)(2,1)S(1)} %get-tuple-element.449), channel_id=1, source_target_pairs={{0,16},{16,32},{32,48},{48,64},{64,80},{80,96},{96,112},{1,17},{17... | collective-permute-start | bytes 884744 | tf_op jit(solution)/shard_map/ppermute | solution.py:566
  95.9 10.4 %collective-permute-start.18 = (bf16[16,9216]{1,0:T(8,128)(2,1)S(1)}, bf16[16,9216]{1,0:T(8,128)(2,1)S(1)}, u32[]{:S(2)}, u32[]{:S(2)}) collective-permute-start(bf16[16,9216]{1,0:T(8,128)(2,1)S(1)} %get-tuple-element.448), channel_id=1, source_target_pairs={{0,16},{16,32},{32,48},{48,64},{64,80},{80,96},{96,112},{1,17},{17... | collective-permute-start | bytes 884744 | tf_op jit(solution)/shard_map/ppermute | solution.py:566
  104.2 10.7 %collective-permute-start.21 = (bf16[16,9216]{1,0:T(8,128)(2,1)S(1)}, bf16[16,9216]{1,0:T(8,128)(2,1)S(1)}, u32[]{:S(2)}, u32[]{:S(2)}) collective-permute-start(bf16[16,9216]{1,0:T(8,128)(2,1)S(1)} %get-tuple-element.463), channel_id=1, source_target_pairs={{0,16},{16,32},{32,48},{48,64},{64,80},{80,96},{96,112},{1,17},{17... | collective-permute-start | bytes 884744 | tf_op jit(solution)/shard_map/ppermute | solution.py:566
  112.6 10.5 %collective-permute-start.20 = (bf16[16,9216]{1,0:T(8,128)(2,1)S(1)}, bf16[16,9216]{1,0:T(8,128)(2,1)S(1)}, u32[]{:S(2)}, u32[]{:S(2)}) collective-permute-start(bf16[16,9216]{1,0:T(8,128)(2,1)S(1)} %get-tuple-element.462), channel_id=1, source_target_pairs={{0,16},{16,32},{32,48},{48,64},{64,80},{80,96},{96,112},{1,17},{17... | collective-permute-start | bytes 884744 | tf_op jit(solution)/shard_map/ppermute | solution.py:566
  121.2 10.4 %collective-permute-start.23 = (bf16[16,9216]{1,0:T(8,128)(2,1)S(1)}, bf16[16,9216]{1,0:T(8,128)(2,1)S(1)}, u32[]{:S(2)}, u32[]{:S(2)}) collective-permute-start(bf16[16,9216]{1,0:T(8,128)(2,1)S(1)} %get-tuple-element.477), channel_id=1, source_target_pairs={{0,16},{16,32},{32,48},{48,64},{64,80},{80,96},{96,112},{1,17},{17... | collective-permute-start | bytes 884744 | tf_op jit(solution)/shard_map/ppermute | solution.py:566
  129.7 10.2 %collective-permute-start.22 = (bf16[16,9216]{1,0:T(8,128)(2,1)S(1)}, bf16[16,9216]{1,0:T(8,128)(2,1)S(1)}, u32[]{:S(2)}, u32[]{:S(2)}) collective-permute-start(bf16[16,9216]{1,0:T(8,128)(2,1)S(1)} %get-tuple-element.476), channel_id=1, source_target_pairs={{0,16},{16,32},{32,48},{48,64},{64,80},{80,96},{96,112},{1,17},{17... | collective-permute-start | bytes 884744 | tf_op jit(solution)/shard_map/ppermute | solution.py:566
  138.0 10.2 %collective-permute-start.25 = (bf16[16,9216]{1,0:T(8,128)(2,1)S(1)}, bf16[16,9216]{1,0:T(8,128)(2,1)S(1)}, u32[]{:S(2)}, u32[]{:S(2)}) collective-permute-start(bf16[16,9216]{1,0:T(8,128)(2,1)S(1)} %get-tuple-element.491), channel_id=1, source_target_pairs={{0,16},{16,32},{32,48},{48,64},{64,80},{80,96},{96,112},{1,17},{17... | collective-permute-start | bytes 884744 | tf_op jit(solution)/shard_map/ppermute | solution.py:566
  154.6 11.3 %collective-permute-start.27 = (bf16[16,9216]{1,0:T(8,128)(2,1)S(1)}, bf16[16,9216]{1,0:T(8,128)(2,1)S(1)}, u32[]{:S(2)}, u32[]{:S(2)}) collective-permute-start(bf16[16,9216]{1,0:T(8,128)(2,1)S(1)} %get-tuple-element.505), channel_id=1, source_target_pairs={{0,16},{16,32},{32,48},{48,64},{64,80},{80,96},{96,112},{1,17},{17... | collective-permute-start | bytes 884744 | tf_op jit(solution)/shard_map/ppermute | solution.py:566
  162.9 11.7 %collective-permute-start.26 = (bf16[16,9216]{1,0:T(8,128)(2,1)S(1)}, bf16[16,9216]{1,0:T(8,128)(2,1)S(1)}, u32[]{:S(2)}, u32[]{:S(2)}) collective-permute-start(bf16[16,9216]{1,0:T(8,128)(2,1)S(1)} %get-tuple-element.504), channel_id=1, source_target_pairs={{0,16},{16,32},{32,48},{48,64},{64,80},{80,96},{96,112},{1,17},{17... | collective-permute-start | bytes 884744 | tf_op jit(solution)/shard_map/ppermute | solution.py:566
  167.1 16.1 %collective-permute-start.29 = (bf16[16,9216]{1,0:T(8,128)(2,1)S(1)}, bf16[16,9216]{1,0:T(8,128)(2,1)S(1)}, u32[]{:S(2)}, u32[]{:S(2)}) collective-permute-start(bf16[16,9216]{1,0:T(8,128)(2,1)S(1)} %get-tuple-element.520), channel_id=1, source_target_pairs={{0,16},{16,32},{32,48},{48,64},{64,80},{80,96},{96,112},{1,17},{17... | collective-permute-start | bytes 884744 | tf_op jit(solution)/shard_map/ppermute | solution.py:566
  175.6 14.8 %collective-permute-start.28 = (bf16[16,9216]{1,0:T(8,128)(2,1)S(1)}, bf16[16,9216]{1,0:T(8,128)(2,1)S(1)}, u32[]{:S(2)}, u32[]{:S(2)}) collective-permute-start(bf16[16,9216]{1,0:T(8,128)(2,1)S(1)} %get-tuple-element.518), channel_id=1, source_target_pairs={{0,16},{16,32},{32,48},{48,64},{64,80},{80,96},{96,112},{1,17},{17... | collective-permute-start | bytes 884744 | tf_op jit(solution)/shard_map/ppermute | solution.py:566
  184.2 16.5 %collective-permute-start.32 = (bf16[16,9216]{1,0:T(8,128)(2,1)S(1)}, bf16[16,9216]{1,0:T(8,128)(2,1)S(1)}, u32[]{:S(2)}, u32[]{:S(2)}) collective-permute-start(bf16[16,9216]{1,0:T(8,128)(2,1)S(1)} %get-tuple-element.541), channel_id=1, source_target_pairs={{0,16},{16,32},{32,48},{48,64},{64,80},{80,96},{96,112},{1,17},{17... | collective-permute-start | bytes 884744 | tf_op jit(solution)/shard_map/ppermute | solution.py:566
  187.3 24.2 %collective-permute-start.31 = (bf16[16,9216]{1,0:T(8,128)(2,1)S(1)}, bf16[16,9216]{1,0:T(8,128)(2,1)S(1)}, u32[]{:S(2)}, u32[]{:S(2)}) collective-permute-start(bf16[16,9216]{1,0:T(8,128)(2,1)S(1)} %get-tuple-element.540), channel_id=1, source_target_pairs={{16,0},{32,16},{48,32},{64,48},{80,64},{96,80},{112,96},{17,1},{33... | collective-permute-start | bytes 884744 | tf_op jit(solution)/shard_map/ppermute | solution.py:580
  191.3 22.5 %collective-permute-start.30 = (bf16[16,9216]{1,0:T(8,128)(2,1)S(1)}, bf16[16,9216]{1,0:T(8,128)(2,1)S(1)}, u32[]{:S(2)}, u32[]{:S(2)}) collective-permute-start(bf16[16,9216]{1,0:T(8,128)(2,1)S(1)} %get-tuple-element.539), channel_id=1, source_target_pairs={{0,16},{16,32},{32,48},{48,64},{64,80},{80,96},{96,112},{1,17},{17... | collective-permute-start | bytes 884744 | tf_op jit(solution)/shard_map/ppermute | solution.py:566
  199.3 20.1 %collective-permute-start.36 = (bf16[16,9216]{1,0:T(8,128)(2,1)S(1)}, bf16[16,9216]{1,0:T(8,128)(2,1)S(1)}, u32[]{:S(2)}, u32[]{:S(2)}) collective-permute-start(bf16[16,9216]{1,0:T(8,128)(2,1)S(1)} %get-tuple-element.571), channel_id=1, source_target_pairs={{16,0},{32,16},{48,32},{64,48},{80,64},{96,80},{112,96},{17,1},{33... | collective-permute-start | bytes 884744 | tf_op jit(solution)/shard_map/ppermute | solution.py:580
  201.6 20.2 %collective-permute-start.35 = (bf16[16,9216]{1,0:T(8,128)(2,1)S(1)}, bf16[16,9216]{1,0:T(8,128)(2,1)S(1)}, u32[]{:S(2)}, u32[]{:S(2)}) collective-permute-start(bf16[16,9216]{1,0:T(8,128)(2,1)S(1)} %get-tuple-element.570), channel_id=1, source_target_pairs={{0,16},{16,32},{32,48},{48,64},{64,80},{80,96},{96,112},{1,17},{17... | collective-permute-start | bytes 884744 | tf_op jit(solution)/shard_map/ppermute | solution.py:566
  212.6 18.7 %collective-permute-start.34 = (bf16[16,9216]{1,0:T(8,128)(2,1)S(1)}, bf16[16,9216]{1,0:T(8,128)(2,1)S(1)}, u32[]{:S(2)}, u32[]{:S(2)}) collective-permute-start(bf16[16,9216]{1,0:T(8,128)(2,1)S(1)} %get-tuple-element.569), channel_id=1, source_target_pairs={{16,0},{32,16},{48,32},{64,48},{80,64},{96,80},{112,96},{17,1},{33... | collective-permute-start | bytes 884744 | tf_op jit(solution)/shard_map/ppermute | solution.py:580
  214.9 18.9 %collective-permute-start.33 = (bf16[16,9216]{1,0:T(8,128)(2,1)S(1)}, bf16[16,9216]{1,0:T(8,128)(2,1)S(1)}, u32[]{:S(2)}, u32[]{:S(2)}) collective-permute-start(bf16[16,9216]{1,0:T(8,128)(2,1)S(1)} %get-tuple-element.568), channel_id=1, source_target_pairs={{0,16},{16,32},{32,48},{48,64},{64,80},{80,96},{96,112},{1,17},{17... | collective-permute-start | bytes 884744 | tf_op jit(solution)/shard_map/ppermute | solution.py:566
  220.5 26.3 %collective-permute-start.40 = (bf16[16,9216]{1,0:T(8,128)(2,1)S(1)}, bf16[16,9216]{1,0:T(8,128)(2,1)S(1)}, u32[]{:S(2)}, u32[]{:S(2)}) collective-permute-start(bf16[16,9216]{1,0:T(8,128)(2,1)S(1)} %get-tuple-element.601), channel_id=1, source_target_pairs={{16,0},{32,16},{48,32},{64,48},{80,64},{96,80},{112,96},{17,1},{33... | collective-permute-start | bytes 884744 | tf_op jit(solution)/shard_map/ppermute | solution.py:580
  222.8 26.4 %collective-permute-start.39 = (bf16[16,9216]{1,0:T(8,128)(2,1)S(1)}, bf16[16,9216]{1,0:T(8,128)(2,1)S(1)}, u32[]{:S(2)}, u32[]{:S(2)}) collective-permute-start(bf16[16,9216]{1,0:T(8,128)(2,1)S(1)} %get-tuple-element.600), channel_id=1, source_target_pairs={{0,16},{16,32},{32,48},{48,64},{64,80},{80,96},{96,112},{1,17},{17... | collective-permute-start | bytes 884744 | tf_op jit(solution)/shard_map/ppermute | solution.py:566
  232.5 24.3 %collective-permute-start.38 = (bf16[16,9216]{1,0:T(8,128)(2,1)S(1)}, bf16[16,9216]{1,0:T(8,128)(2,1)S(1)}, u32[]{:S(2)}, u32[]{:S(2)}) collective-permute-start(bf16[16,9216]{1,0:T(8,128)(2,1)S(1)} %get-tuple-element.599), channel_id=1, source_target_pairs={{16,0},{32,16},{48,32},{64,48},{80,64},{96,80},{112,96},{17,1},{33... | collective-permute-start | bytes 884744 | tf_op jit(solution)/shard_map/ppermute | solution.py:580
  234.7 24.4 %collective-permute-start.37 = (bf16[16,9216]{1,0:T(8,128)(2,1)S(1)}, bf16[16,9216]{1,0:T(8,128)(2,1)S(1)}, u32[]{:S(2)}, u32[]{:S(2)}) collective-permute-start(bf16[16,9216]{1,0:T(8,128)(2,1)S(1)} %get-tuple-element.598), channel_id=1, source_target_pairs={{0,16},{16,32},{32,48},{48,64},{64,80},{80,96},{96,112},{1,17},{17... | collective-permute-start | bytes 884744 | tf_op jit(solution)/shard_map/ppermute | solution.py:566
  247.8 24.3 %collective-permute-start.44 = (bf16[16,9216]{1,0:T(8,128)(2,1)S(1)}, bf16[16,9216]{1,0:T(8,128)(2,1)S(1)}, u32[]{:S(2)}, u32[]{:S(2)}) collective-permute-start(bf16[16,9216]{1,0:T(8,128)(2,1)S(1)} %get-tuple-element.631), channel_id=1, source_target_pairs={{16,0},{32,16},{48,32},{64,48},{80,64},{96,80},{112,96},{17,1},{33... | collective-permute-start | bytes 884744 | tf_op jit(solution)/shard_map/ppermute | solution.py:580
  250.1 24.8 %collective-permute-start.43 = (bf16[16,9216]{1,0:T(8,128)(2,1)S(1)}, bf16[16,9216]{1,0:T(8,128)(2,1)S(1)}, u32[]{:S(2)}, u32[]{:S(2)}) collective-permute-start(bf16[16,9216]{1,0:T(8,128)(2,1)S(1)} %get-tuple-element.630), channel_id=1, source_target_pairs={{0,16},{16,32},{32,48},{48,64},{64,80},{80,96},{96,112},{1,17},{17... | collective-permute-start | bytes 884744 | tf_op jit(solution)/shard_map/ppermute | solution.py:566
  257.8 30.1 %collective-permute-start.42 = (bf16[16,9216]{1,0:T(8,128)(2,1)S(1)}, bf16[16,9216]{1,0:T(8,128)(2,1)S(1)}, u32[]{:S(2)}, u32[]{:S(2)}) collective-permute-start(bf16[16,9216]{1,0:T(8,128)(2,1)S(1)} %get-tuple-element.629), channel_id=1, source_target_pairs={{16,0},{32,16},{48,32},{64,48},{80,64},{96,80},{112,96},{17,1},{33... | collective-permute-start | bytes 884744 | tf_op jit(solution)/shard_map/ppermute | solution.py:580
  260.1 30.2 %collective-permute-start.41 = (bf16[16,9216]{1,0:T(8,128)(2,1)S(1)}, bf16[16,9216]{1,0:T(8,128)(2,1)S(1)}, u32[]{:S(2)}, u32[]{:S(2)}) collective-permute-start(bf16[16,9216]{1,0:T(8,128)(2,1)S(1)} %get-tuple-element.628), channel_id=1, source_target_pairs={{0,16},{16,32},{32,48},{48,64},{64,80},{80,96},{96,112},{1,17},{17... | collective-permute-start | bytes 884744 | tf_op jit(solution)/shard_map/ppermute | solution.py:566
  273.6 24.3 %collective-permute-start.48 = (bf16[16,9216]{1,0:T(8,128)(2,1)S(1)}, bf16[16,9216]{1,0:T(8,128)(2,1)S(1)}, u32[]{:S(2)}, u32[]{:S(2)}) collective-permute-start(bf16[16,9216]{1,0:T(8,128)(2,1)S(1)} %get-tuple-element.661), channel_id=1, source_target_pairs={{16,0},{32,16},{48,32},{64,48},{80,64},{96,80},{112,96},{17,1},{33... | collective-permute-start | bytes 884744 | tf_op jit(solution)/shard_map/ppermute | solution.py:580
  275.9 24.4 %collective-permute-start.47 = (bf16[16,9216]{1,0:T(8,128)(2,1)S(1)}, bf16[16,9216]{1,0:T(8,128)(2,1)S(1)}, u32[]{:S(2)}, u32[]{:S(2)}) collective-permute-start(bf16[16,9216]{1,0:T(8,128)(2,1)S(1)} %get-tuple-element.660), channel_id=1, source_target_pairs={{0,16},{16,32},{32,48},{48,64},{64,80},{80,96},{96,112},{1,17},{17... | collective-permute-start | bytes 884744 | tf_op jit(solution)/shard_map/ppermute | solution.py:566
  288.9 13.0 %collective-permute-start.46 = (bf16[16,9216]{1,0:T(8,128)(2,1)S(1)}, bf16[16,9216]{1,0:T(8,128)(2,1)S(1)}, u32[]{:S(2)}, u32[]{:S(2)}) collective-permute-start(bf16[16,9216]{1,0:T(8,128)(2,1)S(1)} %get-tuple-element.659), channel_id=1, source_target_pairs={{16,0},{32,16},{48,32},{64,48},{80,64},{96,80},{112,96},{17,1},{33... | collective-permute-start | bytes 884744 | tf_op jit(solution)/shard_map/ppermute | solution.py:580
  291.2 13.2 %collective-permute-start.45 = (bf16[16,9216]{1,0:T(8,128)(2,1)S(1)}, bf16[16,9216]{1,0:T(8,128)(2,1)S(1)}, u32[]{:S(2)}, u32[]{:S(2)}) collective-permute-start(bf16[16,9216]{1,0:T(8,128)(2,1)S(1)} %get-tuple-element.658), channel_id=1, source_target_pairs={{0,16},{16,32},{32,48},{48,64},{64,80},{80,96},{96,112},{1,17},{17... | collective-permute-start | bytes 884744 | tf_op jit(solution)/shard_map/ppermute | solution.py:566
  298.9 18.3 %collective-permute-start.49 = (bf16[16,9216]{1,0:T(8,128)(2,1)S(1)}, bf16[16,9216]{1,0:T(8,128)(2,1)S(1)}, u32[]{:S(2)}, u32[]{:S(2)}) collective-permute-start(bf16[16,9216]{1,0:T(8,128)(2,1)S(1)} %get-tuple-element.689), channel_id=1, source_target_pairs={{16,0},{32,16},{48,32},{64,48},{80,64},{96,80},{112,96},{17,1},{33... | collective-permute-start | bytes 884744 | tf_op jit(solution)/shard_map/ppermute | solution.py:580
  303.1 18.2 %collective-permute-start.51 = (bf16[16,9216]{1,0:T(8,128)(2,1)S(1)}, bf16[16,9216]{1,0:T(8,128)(2,1)S(1)}, u32[]{:S(2)}, u32[]{:S(2)}) collective-permute-start(bf16[16,9216]{1,0:T(8,128)(2,1)S(1)} %get-tuple-element.698), channel_id=1, source_target_pairs={{16,0},{32,16},{48,32},{64,48},{80,64},{96,80},{112,96},{17,1},{33... | collective-permute-start | bytes 884744 | tf_op jit(solution)/shard_map/ppermute | solution.py:580
  318.2 23.5 %collective-permute-start.50 = (bf16[16,9216]{1,0:T(8,128)(2,1)S(1)}, bf16[16,9216]{1,0:T(8,128)(2,1)S(1)}, u32[]{:S(2)}, u32[]{:S(2)}) collective-permute-start(bf16[16,9216]{1,0:T(8,128)(2,1)S(1)} %get-tuple-element.697), channel_id=1, source_target_pairs={{16,0},{32,16},{48,32},{64,48},{80,64},{96,80},{112,96},{17,1},{33... | collective-permute-start | bytes 884744 | tf_op jit(solution)/shard_map/ppermute | solution.py:580
  322.3 33.4 %collective-permute-start.53 = (bf16[16,9216]{1,0:T(8,128)(2,1)S(1)}, bf16[16,9216]{1,0:T(8,128)(2,1)S(1)}, u32[]{:S(2)}, u32[]{:S(2)}) collective-permute-start(bf16[16,9216]{1,0:T(8,128)(2,1)S(1)} %get-tuple-element.714), channel_id=1, source_target_pairs={{16,0},{32,16},{48,32},{64,48},{80,64},{96,80},{112,96},{17,1},{33... | collective-permute-start | bytes 884744 | tf_op jit(solution)/shard_map/ppermute | solution.py:580
  342.7 29.8 %collective-permute-start.52 = (bf16[16,9216]{1,0:T(8,128)(2,1)S(1)}, bf16[16,9216]{1,0:T(8,128)(2,1)S(1)}, u32[]{:S(2)}, u32[]{:S(2)}) collective-permute-start(bf16[16,9216]{1,0:T(8,128)(2,1)S(1)} %get-tuple-element.713), channel_id=1, source_target_pairs={{16,0},{32,16},{48,32},{64,48},{80,64},{96,80},{112,96},{17,1},{33... | collective-permute-start | bytes 884744 | tf_op jit(solution)/shard_map/ppermute | solution.py:580
  361.1 21.2 %collective-permute-start.55 = (bf16[16,9216]{1,0:T(8,128)(2,1)S(1)}, bf16[16,9216]{1,0:T(8,128)(2,1)S(1)}, u32[]{:S(2)}, u32[]{:S(2)}) collective-permute-start(bf16[16,9216]{1,0:T(8,128)(2,1)S(1)} %get-tuple-element.730), channel_id=1, source_target_pairs={{16,0},{32,16},{48,32},{64,48},{80,64},{96,80},{112,96},{17,1},{33... | collective-permute-start | bytes 884744 | tf_op jit(solution)/shard_map/ppermute | solution.py:580
  378.4 14.0 %collective-permute-start.54 = (bf16[16,9216]{1,0:T(8,128)(2,1)S(1)}, bf16[16,9216]{1,0:T(8,128)(2,1)S(1)}, u32[]{:S(2)}, u32[]{:S(2)}) collective-permute-start(bf16[16,9216]{1,0:T(8,128)(2,1)S(1)} %get-tuple-element.729), channel_id=1, source_target_pairs={{16,0},{32,16},{48,32},{64,48},{80,64},{96,80},{112,96},{17,1},{33... | collective-permute-start | bytes 884744 | tf_op jit(solution)/shard_map/ppermute | solution.py:580
  387.8 14.8 %collective-permute-start.57 = (bf16[16,9216]{1,0:T(8,128)(2,1)S(1)}, bf16[16,9216]{1,0:T(8,128)(2,1)S(1)}, u32[]{:S(2)}, u32[]{:S(2)}) collective-permute-start(bf16[16,9216]{1,0:T(8,128)(2,1)S(1)} %get-tuple-element.746), channel_id=1, source_target_pairs={{16,0},{32,16},{48,32},{64,48},{80,64},{96,80},{112,96},{17,1},{33... | collective-permute-start | bytes 884744 | tf_op jit(solution)/shard_map/ppermute | solution.py:580
  397.8 15.6 %collective-permute-start.56 = (bf16[16,9216]{1,0:T(8,128)(2,1)S(1)}, bf16[16,9216]{1,0:T(8,128)(2,1)S(1)}, u32[]{:S(2)}, u32[]{:S(2)}) collective-permute-start(bf16[16,9216]{1,0:T(8,128)(2,1)S(1)} %get-tuple-element.745), channel_id=1, source_target_pairs={{16,0},{32,16},{48,32},{64,48},{80,64},{96,80},{112,96},{17,1},{33... | collective-permute-start | bytes 884744 | tf_op jit(solution)/shard_map/ppermute | solution.py:580
  408.0 15.8 %collective-permute-start.59 = (bf16[16,9216]{1,0:T(8,128)(2,1)S(1)}, bf16[16,9216]{1,0:T(8,128)(2,1)S(1)}, u32[]{:S(2)}, u32[]{:S(2)}) collective-permute-start(bf16[16,9216]{1,0:T(8,128)(2,1)S(1)} %get-tuple-element.762), channel_id=1, source_target_pairs={{16,0},{32,16},{48,32},{64,48},{80,64},{96,80},{112,96},{17,1},{33... | collective-permute-start | bytes 884744 | tf_op jit(solution)/shard_map/ppermute | solution.py:580
  418.9 12.4 %collective-permute-start.58 = (bf16[16,9216]{1,0:T(8,128)(2,1)S(1)}, bf16[16,9216]{1,0:T(8,128)(2,1)S(1)}, u32[]{:S(2)}, u32[]{:S(2)}) collective-permute-start(bf16[16,9216]{1,0:T(8,128)(2,1)S(1)} %get-tuple-element.761), channel_id=1, source_target_pairs={{16,0},{32,16},{48,32},{64,48},{80,64},{96,80},{112,96},{17,1},{33... | collective-permute-start | bytes 884744 | tf_op jit(solution)/shard_map/ppermute | solution.py:580
  429.3 10.6 %collective-permute-start.61 = (bf16[16,9216]{1,0:T(8,128)(2,1)S(1)}, bf16[16,9216]{1,0:T(8,128)(2,1)S(1)}, u32[]{:S(2)}, u32[]{:S(2)}) collective-permute-start(bf16[16,9216]{1,0:T(8,128)(2,1)S(1)} %get-tuple-element.778), channel_id=1, source_target_pairs={{16,0},{32,16},{48,32},{64,48},{80,64},{96,80},{112,96},{17,1},{33... | collective-permute-start | bytes 884744 | tf_op jit(solution)/shard_map/ppermute | solution.py:580
  436.8 10.5 %collective-permute-start.60 = (bf16[16,9216]{1,0:T(8,128)(2,1)S(1)}, bf16[16,9216]{1,0:T(8,128)(2,1)S(1)}, u32[]{:S(2)}, u32[]{:S(2)}) collective-permute-start(bf16[16,9216]{1,0:T(8,128)(2,1)S(1)} %get-tuple-element.777), channel_id=1, source_target_pairs={{16,0},{32,16},{48,32},{64,48},{80,64},{96,80},{112,96},{17,1},{33... | collective-permute-start | bytes 884744 | tf_op jit(solution)/shard_map/ppermute | solution.py:580
  445.4 10.3 %collective-permute-start.63 = (bf16[16,9216]{1,0:T(8,128)(2,1)S(1)}, bf16[16,9216]{1,0:T(8,128)(2,1)S(1)}, u32[]{:S(2)}, u32[]{:S(2)}) collective-permute-start(bf16[16,9216]{1,0:T(8,128)(2,1)S(1)} %get-tuple-element.794), channel_id=1, source_target_pairs={{16,0},{32,16},{48,32},{64,48},{80,64},{96,80},{112,96},{17,1},{33... | collective-permute-start | bytes 884744 | tf_op jit(solution)/shard_map/ppermute | solution.py:580
  452.8 13.7 %collective-permute-start.62 = (bf16[16,9216]{1,0:T(8,128)(2,1)S(1)}, bf16[16,9216]{1,0:T(8,128)(2,1)S(1)}, u32[]{:S(2)}, u32[]{:S(2)}) collective-permute-start(bf16[16,9216]{1,0:T(8,128)(2,1)S(1)} %get-tuple-element.793), channel_id=1, source_target_pairs={{16,0},{32,16},{48,32},{64,48},{80,64},{96,80},{112,96},{17,1},{33... | collective-permute-start | bytes 884744 | tf_op jit(solution)/shard_map/ppermute | solution.py:580
  484.7 16.4 %collective-permute-start.71 = (bf16[1168,256]{1,0:T(8,128)(2,1)S(1)}, bf16[1168,256]{1,0:T(8,128)(2,1)S(1)}, u32[]{:S(2)}, u32[]{:S(2)}) collective-permute-start(bf16[1168,256]{1,0:T(8,128)(2,1)S(1)} %get-tuple-element.820), channel_id=1, source_target_pairs={{0,12},{1,13},{2,14},{3,15},{4,0},{5,1},{6,2},{7,3},{8,4},{9,5},{1... | collective-permute-start | bytes 1794056 | tf_op jit(solution)/shard_map/ppermute | solution.py:372
  486.9 17.6 %collective-permute-start.70 = (bf16[1168,256]{1,0:T(8,128)(2,1)S(1)}, bf16[1168,256]{1,0:T(8,128)(2,1)S(1)}, u32[]{:S(2)}, u32[]{:S(2)}) collective-permute-start(bf16[1168,256]{1,0:T(8,128)(2,1)S(1)} %get-tuple-element.821), channel_id=1, source_target_pairs={{0,4},{1,5},{2,6},{3,7},{4,8},{5,9},{6,10},{7,11},{8,12},{9,13},{1... | collective-permute-start | bytes 1794056 | tf_op jit(solution)/shard_map/ppermute | solution.py:372
  486.9 17.6 %collective-permute-start.68 = (bf16[1168,256]{1,0:T(8,128)(2,1)S(1)}, bf16[1168,256]{1,0:T(8,128)(2,1)S(1)}, u32[]{:S(2)}, u32[]{:S(2)}) collective-permute-start(bf16[1168,256]{1,0:T(8,128)(2,1)S(1)} %get-tuple-element.822), channel_id=1, source_target_pairs={{0,2},{1,3},{2,0},{3,1},{4,6},{5,7},{6,4},{7,5},{8,10},{9,11},{10,... | collective-permute-start | bytes 1794056 | tf_op jit(solution)/shard_map/ppermute | solution.py:368
  487.3 41.7 %collective-permute-start.66 = (bf16[1168,256]{1,0:T(8,128)(2,1)S(1)}, bf16[1168,256]{1,0:T(8,128)(2,1)}, u32[]{:S(2)}, u32[]{:S(2)}) collective-permute-start(bf16[1168,256]{1,0:T(8,128)(2,1)S(1)} %get-tuple-element.819), channel_id=1, source_target_pairs={{0,4},{1,5},{2,6},{3,7},{4,8},{5,9},{6,10},{7,11},{8,12},{9,13},{1... | collective-permute-start | bytes 1794056 | tf_op jit(solution)/shard_map/ppermute | solution.py:372
  489.4 39.6 %collective-permute-start.67 = (bf16[1168,256]{1,0:T(8,128)(2,1)}, bf16[1168,256]{1,0:T(8,128)(2,1)}, u32[]{:S(2)}, u32[]{:S(2)}) collective-permute-start(bf16[1168,256]{1,0:T(8,128)(2,1)} %fusion.9), channel_id=1, source_target_pairs={{0,12},{1,13},{2,14},{3,15},{4,0},{5,1},{6,2},{7,3},{8,4},{9,5},{1... | collective-permute-start | bytes 1794056 | tf_op jit(solution)/shard_map/ppermute | solution.py:372
  506.2 22.8 %collective-permute-start.69 = (bf16[1168,256]{1,0:T(8,128)(2,1)}, bf16[1168,256]{1,0:T(8,128)(2,1)}, u32[]{:S(2)}, u32[]{:S(2)}) collective-permute-start(bf16[1168,256]{1,0:T(8,128)(2,1)} %get-tuple-element.823), channel_id=1, source_target_pairs={{0,8},{1,9},{2,10},{3,11},{4,12},{5,13},{6,14},{7,15},{8,0},{9,1},... | collective-permute-start | bytes 1794056 | tf_op jit(solution)/shard_map/ppermute | solution.py:372
  506.8 22.2 %collective-permute-start.72 = (bf16[1168,256]{1,0:T(8,128)(2,1)}, bf16[1168,256]{1,0:T(8,128)(2,1)}, u32[]{:S(2)}, u32[]{:S(2)}) collective-permute-start(bf16[1168,256]{1,0:T(8,128)(2,1)} %get-tuple-element.824), channel_id=1, source_target_pairs={{0,2},{1,3},{2,0},{3,1},{4,6},{5,7},{6,4},{7,5},{8,10},{9,11},{10,... | collective-permute-start | bytes 1794056 | tf_op jit(solution)/shard_map/ppermute | solution.py:368
  (20 other events, 853.1 us)

commit v4 on v3

--- a/solution.py
+++ b/solution.py
@@ -255,6 +255,7 @@
 def forward_call(tick, table, incoming, gain, down, up, base_in, base_out, limits, state):
     shape = jax.ShapeDtypeStruct
     outs = [shape(item.shape, item.dtype) for item in state] + [shape((ROWS, WIDTH), BF16)]
+    held = [item if number == 1 else in_hbm(item) for number, item in enumerate(state)]
     got = pl.pallas_call(
         functools.partial(forward_kernel, tick),
         out_shape=outs,
@@ -276,7 +277,7 @@
         compiler_params=call_params(8),
         cost_estimate=pl.CostEstimate(flops=150_000_000, bytes_accessed=9_000_000, transcendentals=0),
         name="section_forward",
-    )(table, incoming, gain, down, up, in_hbm(base_in), in_hbm(base_out), limits, *map(in_hbm, state))
+    )(table, incoming, gain, down, up, base_in, base_out, limits, *held)
     return got[:6], got[6]
 
 

time: 543 us -> 536 us (0.987)
  Pallas kernels: 188 us -> 178 us
  starting transfers between devices: 177 us -> 184 us
    pallas_call x26, Pallas kernels: 92.4 us -> 82.2 us  [forward_call(): pl.pallas_call(functools.partial(forward_kernel, tick), out_shape=outs, i...]
  transfers between devices with their start and end apart: 73 -> 73, of which waited for: 28 -> 27; matrix products, arithmetic and copies ran while one was open for 2% -> 2% of each run, Pallas kernels for 31% -> 30%
where the time goes in v4:
time: 536 us; the launch traced here: 527 us
  starting transfers between devices  184 us (34%)
  Pallas kernels  178 us (33%)
  waiting for transfers between devices  139 us (26%)
  local copies, waits for them, and re-layouts  12.9 us (2%)
  other arithmetic  11.3 us (2%)
    ppermute x24, starting transfers between devices, shards(): arriving.append(lax.ppermute(delivered, 'section', onward))  123 us
    pallas_call x26, Pallas kernels, backward_call(): pl.pallas_call(functools.partial(backward_kernel, tick), out_shape=outs,...  82.5 us
    pallas_call x26, Pallas kernels, forward_call(): pl.pallas_call(functools.partial(forward_kernel, tick), out_shape=outs, i...  82.2 us
    ppermute x24, waiting for transfers between devices, shards(): returning.append(lax.ppermute(sent, 'section', inverse))  73.2 us
    ppermute x10, waiting for transfers between devices, along_y(): lax.ppermute(value, 'fsdp', fsdp_pairs(lambda y, z, core: ((y + by) % 4,...  51.4 us
    ppermute x24, starting transfers between devices, shards(): returning.append(lax.ppermute(sent, 'section', inverse))  31 us
    ppermute x10, starting transfers between devices, along_y(): lax.ppermute(value, 'fsdp', fsdp_pairs(lambda y, z, core: ((y + by) % 4,...  20.1 us
  transfers between devices with their start and end apart: 73, of which 27 were waited for; matrix products, arithmetic and copies ran while one was open for 2% of the time, Pallas kernels for 30%

profile of v4, /device:TPU:0, one launch (start us, length us, event | category | flops | bytes accessed | tf_op | source)
XLA Modules:
  0.0 526.6 jit_solution(12797171127899678362)
XLA Ops:
  4.0 4.0 collective-permute-start.1
  8.1 3.2 collective-permute-start.8
  11.9 2.6 collective-permute-start.4
  14.5 7.4 %collective-permute-done.1.refs_2_ = bf16[1168,256]{1,0:T(8,128)(2,1)S(1)} collective-permute-done((bf16[1168,256]{1,0:T(8,128)(2,1)S(1)}, bf16[1168,256]{1,0:T(8,128)(2,1)S(1)}, u32[]{:S(2)}, u32[]{:S(2)}) %collective-permute-start.1) | collective-permute-done | bytes 598048 | tf_op jit(solution)/shard_map/ppermute | solution.py:369
  23.3 2.6 fusion.15
  27.0 3.3 collective-permute-start.10
  30.3 7.4 %collective-permute-done.6.refs_6_ = bf16[1168,256]{1,0:T(8,128)(2,1)S(1)} collective-permute-done((bf16[1168,256]{1,0:T(8,128)(2,1)S(1)}, bf16[1168,256]{1,0:T(8,128)(2,1)S(1)}, u32[]{:S(2)}, u32[]{:S(2)}) %collective-permute-start.6) | collective-permute-done | bytes 598048 | tf_op jit(solution)/shard_map/ppermute | solution.py:373
  46.0 9.0 %collective-permute-done.14.refs_14_ = bf16[1168,256]{1,0:T(8,128)(2,1)} collective-permute-done((bf16[1168,256]{1,0:T(8,128)(2,1)S(1)}, bf16[1168,256]{1,0:T(8,128)(2,1)}, u32[]{:S(2)}, u32[]{:S(2)}) %collective-permute-start.14) | collective-permute-done | bytes 598048 | tf_op jit(solution)/shard_map/ppermute | solution.py:373
  60.3 3.3 assemble_weights.1
  63.7 5.5 %section_forward.26 = (bf16[192,9216]{1,0:T(8,128)(2,1)}, bf16[192,9216]{1,0:T(8,128)(2,1)}, f32[192,256]{1,0:T(8,128)}, bf16[192,256]{1,0:T(8,128)(2,1)}, bf16[...) custom-call(s32[40,6]{1,0:T(8,128)S(1)} %copy.388.table, ...), custom_call_target="tpu_custom_call", output_to_operand_aliasing={{0}: (8, {}), {1}: (9, {}), {2}: (10, {}), {3}: (11, {}), {... | custom-call | flops 150000000 | bytes 9000000 | tf_op jit(solution)/shard_map/section_forward/pallas_call | solution.py:259
  70.6 5.5 %section_forward.27 = (bf16[192,9216]{1,0:T(8,128)(2,1)}, bf16[192,9216]{1,0:T(8,128)(2,1)}, f32[192,256]{1,0:T(8,128)}, bf16[192,256]{1,0:T(8,128)(2,1)}, bf16[...) custom-call(s32[40,6]{1,0:T(8,128)S(1)} %copy.388.table, ...), custom_call_target="tpu_custom_call", output_to_operand_aliasing={{0}: (8, {}), {1}: (9, {}), {2}: (10, {}), {3}: (11, {}), {... | custom-call | flops 150000000 | bytes 9000000 | tf_op jit(solution)/shard_map/section_forward/pallas_call | solution.py:259
  77.5 6.0 %section_forward.28 = (bf16[192,9216]{1,0:T(8,128)(2,1)}, bf16[192,9216]{1,0:T(8,128)(2,1)}, f32[192,256]{1,0:T(8,128)}, bf16[192,256]{1,0:T(8,128)(2,1)}, bf16[...) custom-call(s32[40,6]{1,0:T(8,128)S(1)} %copy.388.table, ...), custom_call_target="tpu_custom_call", output_to_operand_aliasing={{0}: (8, {}), {1}: (9, {}), {2}: (10, {}), {3}: (11, {}), {... | custom-call | flops 150000000 | bytes 9000000 | tf_op jit(solution)/shard_map/section_forward/pallas_call | solution.py:259
  83.5 4.4 collective-permute-start.19
  88.0 5.5 %section_forward.29 = (bf16[192,9216]{1,0:T(8,128)(2,1)}, bf16[192,9216]{1,0:T(8,128)(2,1)}, f32[192,256]{1,0:T(8,128)}, bf16[192,256]{1,0:T(8,128)(2,1)}, bf16[...) custom-call(s32[40,6]{1,0:T(8,128)S(1)} %copy.388.table, ...), custom_call_target="tpu_custom_call", output_to_operand_aliasing={{0}: (8, {}), {1}: (9, {}), {2}: (10, {}), {3}: (11, {}), {... | custom-call | flops 150000000 | bytes 9000000 | tf_op jit(solution)/shard_map/section_forward/pallas_call | solution.py:259
  95.4 5.5 %section_forward.30 = (bf16[192,9216]{1,0:T(8,128)(2,1)}, bf16[192,9216]{1,0:T(8,128)(2,1)}, f32[192,256]{1,0:T(8,128)}, bf16[192,256]{1,0:T(8,128)(2,1)}, bf16[...) custom-call(s32[40,6]{1,0:T(8,128)S(1)} %copy.388.table, ...), custom_call_target="tpu_custom_call", output_to_operand_aliasing={{0}: (8, {}), {1}: (9, {}), {2}: (10, {}), {3}: (11, {}), {... | custom-call | flops 150000000 | bytes 9000000 | tf_op jit(solution)/shard_map/section_forward/pallas_call | solution.py:259
  101.0 3.0 collective-permute-start.21
  104.0 5.5 %section_forward.31 = (bf16[192,9216]{1,0:T(8,128)(2,1)}, bf16[192,9216]{1,0:T(8,128)(2,1)}, f32[192,256]{1,0:T(8,128)}, bf16[192,256]{1,0:T(8,128)(2,1)}, bf16[...) custom-call(s32[40,6]{1,0:T(8,128)S(1)} %copy.388.table, ...), custom_call_target="tpu_custom_call", output_to_operand_aliasing={{0}: (8, {}), {1}: (9, {}), {2}: (10, {}), {3}: (11, {}), {... | custom-call | flops 150000000 | bytes 9000000 | tf_op jit(solution)/shard_map/section_forward/pallas_call | solution.py:259
  111.8 5.5 %section_forward.32 = (bf16[192,9216]{1,0:T(8,128)(2,1)}, bf16[192,9216]{1,0:T(8,128)(2,1)}, f32[192,256]{1,0:T(8,128)}, bf16[192,256]{1,0:T(8,128)(2,1)}, bf16[...) custom-call(s32[40,6]{1,0:T(8,128)S(1)} %copy.388.table, ...), custom_call_target="tpu_custom_call", output_to_operand_aliasing={{0}: (8, {}), {1}: (9, {}), {2}: (10, {}), {3}: (11, {}), {... | custom-call | flops 150000000 | bytes 9000000 | tf_op jit(solution)/shard_map/section_forward/pallas_call | solution.py:259
  119.3 5.7 %section_forward.33 = (bf16[192,9216]{1,0:T(8,128)(2,1)}, bf16[192,9216]{1,0:T(8,128)(2,1)}, f32[192,256]{1,0:T(8,128)}, bf16[192,256]{1,0:T(8,128)(2,1)}, bf16[...) custom-call(s32[40,6]{1,0:T(8,128)S(1)} %copy.388.table, ...), custom_call_target="tpu_custom_call", output_to_operand_aliasing={{0}: (8, {}), {1}: (9, {}), {2}: (10, {}), {3}: (11, {}), {... | custom-call | flops 150000000 | bytes 9000000 | tf_op jit(solution)/shard_map/section_forward/pallas_call | solution.py:259
  125.0 2.5 collective-permute-start.22
  127.5 5.5 %section_forward.34 = (bf16[192,9216]{1,0:T(8,128)(2,1)}, bf16[192,9216]{1,0:T(8,128)(2,1)}, f32[192,256]{1,0:T(8,128)}, bf16[192,256]{1,0:T(8,128)(2,1)}, bf16[...) custom-call(s32[40,6]{1,0:T(8,128)S(1)} %copy.388.table, ...), custom_call_target="tpu_custom_call", output_to_operand_aliasing={{0}: (8, {}), {1}: (9, {}), {2}: (10, {}), {3}: (11, {}), {... | custom-call | flops 150000000 | bytes 9000000 | tf_op jit(solution)/shard_map/section_forward/pallas_call | solution.py:259
  135.2 5.5 %section_forward.35 = (bf16[192,9216]{1,0:T(8,128)(2,1)}, bf16[192,9216]{1,0:T(8,128)(2,1)}, f32[192,256]{1,0:T(8,128)}, bf16[192,256]{1,0:T(8,128)(2,1)}, bf16[...) custom-call(s32[40,6]{1,0:T(8,128)S(1)} %copy.388.table, ...), custom_call_target="tpu_custom_call", output_to_operand_aliasing={{0}: (8, {}), {1}: (9, {}), {2}: (10, {}), {3}: (11, {}), {... | custom-call | flops 150000000 | bytes 9000000 | tf_op jit(solution)/shard_map/section_forward/pallas_call | solution.py:259
  142.7 5.5 %section_forward.36 = (bf16[192,9216]{1,0:T(8,128)(2,1)}, bf16[192,9216]{1,0:T(8,128)(2,1)}, f32[192,256]{1,0:T(8,128)}, bf16[192,256]{1,0:T(8,128)(2,1)}, bf16[...) custom-call(s32[40,6]{1,0:T(8,128)S(1)} %copy.388.table, ...), custom_call_target="tpu_custom_call", output_to_operand_aliasing={{0}: (8, {}), {1}: (9, {}), {2}: (10, {}), {3}: (11, {}), {... | custom-call | flops 150000000 | bytes 9000000 | tf_op jit(solution)/shard_map/section_forward/pallas_call | solution.py:259
  150.2 5.5 %section_forward.37 = (bf16[192,9216]{1,0:T(8,128)(2,1)}, bf16[192,9216]{1,0:T(8,128)(2,1)}, f32[192,256]{1,0:T(8,128)}, bf16[192,256]{1,0:T(8,128)(2,1)}, bf16[...) custom-call(s32[40,6]{1,0:T(8,128)S(1)} %copy.388.table, ...), custom_call_target="tpu_custom_call", output_to_operand_aliasing={{0}: (8, {}), {1}: (9, {}), {2}: (10, {}), {3}: (11, {}), {... | custom-call | flops 150000000 | bytes 9000000 | tf_op jit(solution)/shard_map/section_forward/pallas_call | solution.py:259
  155.7 4.1 collective-permute-start.26
  161.0 6.6 %collective-permute-start.29 = (bf16[16,9216]{1,0:T(8,128)(2,1)S(1)}, bf16[16,9216]{1,0:T(8,128)(2,1)S(1)}, u32[]{:S(2)}, u32[]{:S(2)}) collective-permute-start(bf16[16,9216]{1,0:T(8,128)(2,1)S(1)} %get-tuple-element.520), channel_id=1, source_target_pairs={{0,16},{16,32},{32,48},{48,64},{64,80},{80,96},{96,112},{1,17},{17... | collective-permute-start | bytes 884744 | tf_op jit(solution)/shard_map/ppermute | solution.py:567
  168.6 7.7 %collective-permute-start.28 = (bf16[16,9216]{1,0:T(8,128)(2,1)S(1)}, bf16[16,9216]{1,0:T(8,128)(2,1)S(1)}, u32[]{:S(2)}, u32[]{:S(2)}) collective-permute-start(bf16[16,9216]{1,0:T(8,128)(2,1)S(1)} %get-tuple-element.518), channel_id=1, source_target_pairs={{0,16},{16,32},{32,48},{48,64},{64,80},{80,96},{96,112},{1,17},{17... | collective-permute-start | bytes 884744 | tf_op jit(solution)/shard_map/ppermute | solution.py:567
  182.9 8.0 %collective-permute-start.30 = (bf16[16,9216]{1,0:T(8,128)(2,1)S(1)}, bf16[16,9216]{1,0:T(8,128)(2,1)S(1)}, u32[]{:S(2)}, u32[]{:S(2)}) collective-permute-start(bf16[16,9216]{1,0:T(8,128)(2,1)S(1)} %get-tuple-element.539), channel_id=1, source_target_pairs={{0,16},{16,32},{32,48},{48,64},{64,80},{80,96},{96,112},{1,17},{17... | collective-permute-start | bytes 884744 | tf_op jit(solution)/shard_map/ppermute | solution.py:567
  194.7 9.1 %collective-permute-start.35 = (bf16[16,9216]{1,0:T(8,128)(2,1)S(1)}, bf16[16,9216]{1,0:T(8,128)(2,1)S(1)}, u32[]{:S(2)}, u32[]{:S(2)}) collective-permute-start(bf16[16,9216]{1,0:T(8,128)(2,1)S(1)} %get-tuple-element.570), channel_id=1, source_target_pairs={{0,16},{16,32},{32,48},{48,64},{64,80},{80,96},{96,112},{1,17},{17... | collective-permute-start | bytes 884744 | tf_op jit(solution)/shard_map/ppermute | solution.py:567
  207.2 4.6 collective-permute-start.33
  215.0 9.3 %collective-permute-start.39 = (bf16[16,9216]{1,0:T(8,128)(2,1)S(1)}, bf16[16,9216]{1,0:T(8,128)(2,1)S(1)}, u32[]{:S(2)}, u32[]{:S(2)}) collective-permute-start(bf16[16,9216]{1,0:T(8,128)(2,1)S(1)} %get-tuple-element.600), channel_id=1, source_target_pairs={{0,16},{16,32},{32,48},{48,64},{64,80},{80,96},{96,112},{1,17},{17... | collective-permute-start | bytes 884744 | tf_op jit(solution)/shard_map/ppermute | solution.py:567
  227.8 11.2 %collective-permute-start.37 = (bf16[16,9216]{1,0:T(8,128)(2,1)S(1)}, bf16[16,9216]{1,0:T(8,128)(2,1)S(1)}, u32[]{:S(2)}, u32[]{:S(2)}) collective-permute-start(bf16[16,9216]{1,0:T(8,128)(2,1)S(1)} %get-tuple-element.598), channel_id=1, source_target_pairs={{0,16},{16,32},{32,48},{48,64},{64,80},{80,96},{96,112},{1,17},{17... | collective-permute-start | bytes 884744 | tf_op jit(solution)/shard_map/ppermute | solution.py:567
  242.4 6.7 %collective-permute-start.43 = (bf16[16,9216]{1,0:T(8,128)(2,1)S(1)}, bf16[16,9216]{1,0:T(8,128)(2,1)S(1)}, u32[]{:S(2)}, u32[]{:S(2)}) collective-permute-start(bf16[16,9216]{1,0:T(8,128)(2,1)S(1)} %get-tuple-element.630), channel_id=1, source_target_pairs={{0,16},{16,32},{32,48},{48,64},{64,80},{80,96},{96,112},{1,17},{17... | collective-permute-start | bytes 884744 | tf_op jit(solution)/shard_map/ppermute | solution.py:567
  252.3 11.2 %collective-permute-start.41 = (bf16[16,9216]{1,0:T(8,128)(2,1)S(1)}, bf16[16,9216]{1,0:T(8,128)(2,1)S(1)}, u32[]{:S(2)}, u32[]{:S(2)}) collective-permute-start(bf16[16,9216]{1,0:T(8,128)(2,1)S(1)} %get-tuple-element.628), channel_id=1, source_target_pairs={{0,16},{16,32},{32,48},{48,64},{64,80},{80,96},{96,112},{1,17},{17... | collective-permute-start | bytes 884744 | tf_op jit(solution)/shard_map/ppermute | solution.py:567
  267.3 11.2 %collective-permute-start.47 = (bf16[16,9216]{1,0:T(8,128)(2,1)S(1)}, bf16[16,9216]{1,0:T(8,128)(2,1)S(1)}, u32[]{:S(2)}, u32[]{:S(2)}) collective-permute-start(bf16[16,9216]{1,0:T(8,128)(2,1)S(1)} %get-tuple-element.660), channel_id=1, source_target_pairs={{0,16},{16,32},{32,48},{48,64},{64,80},{80,96},{96,112},{1,17},{17... | collective-permute-start | bytes 884744 | tf_op jit(solution)/shard_map/ppermute | solution.py:567
  281.8 6.6 %collective-permute-start.45 = (bf16[16,9216]{1,0:T(8,128)(2,1)S(1)}, bf16[16,9216]{1,0:T(8,128)(2,1)S(1)}, u32[]{:S(2)}, u32[]{:S(2)}) collective-permute-start(bf16[16,9216]{1,0:T(8,128)(2,1)S(1)} %get-tuple-element.658), channel_id=1, source_target_pairs={{0,16},{16,32},{32,48},{48,64},{64,80},{80,96},{96,112},{1,17},{17... | collective-permute-start | bytes 884744 | tf_op jit(solution)/shard_map/ppermute | solution.py:567
  296.7 9.5 %collective-permute-done.49.incoming = bf16[16,9216]{1,0:T(8,128)(2,1)S(1)} collective-permute-done((bf16[16,9216]{1,0:T(8,128)(2,1)S(1)}, bf16[16,9216]{1,0:T(8,128)(2,1)S(1)}, u32[]{:S(2)}, u32[]{:S(2)}) %collective-permute-start.49) | collective-permute-done | bytes 294944 | tf_op jit(solution)/shard_map/ppermute | solution.py:581
  308.6 2.5 collective-permute-done.51.incoming
  313.4 18.3 %collective-permute-done.50.incoming = bf16[16,9216]{1,0:T(8,128)(2,1)S(1)} collective-permute-done((bf16[16,9216]{1,0:T(8,128)(2,1)S(1)}, bf16[16,9216]{1,0:T(8,128)(2,1)S(1)}, u32[]{:S(2)}, u32[]{:S(2)}) %collective-permute-start.50) | collective-permute-done | bytes 294944 | tf_op jit(solution)/shard_map/ppermute | solution.py:581
  334.0 14.7 %collective-permute-done.53.incoming = bf16[16,9216]{1,0:T(8,128)(2,1)S(1)} collective-permute-done((bf16[16,9216]{1,0:T(8,128)(2,1)S(1)}, bf16[16,9216]{1,0:T(8,128)(2,1)S(1)}, u32[]{:S(2)}, u32[]{:S(2)}) %collective-permute-start.53) | collective-permute-done | bytes 294944 | tf_op jit(solution)/shard_map/ppermute | solution.py:581
  348.7 5.4 %section_backward.40 = (bf16[192,9216]{1,0:T(8,128)(2,1)}, f32[192,256]{1,0:T(8,128)}, f32[192,256]{1,0:T(8,128)}, bf16[192,9216]{1,0:T(8,128)(2,1)}, bf16[192,9...) custom-call(s32[40,6]{1,0:T(8,128)S(1)} %copy.388.table, ...), custom_call_target="tpu_custom_call", output_to_operand_aliasing={{0}: (7, {}), {1}: (8, {}), {2}: (9, {}), {3}: (10, {}), {4... | custom-call | flops 150000000 | bytes 9000000 | tf_op jit(solution)/shard_map/section_backward/pallas_call | solution.py:288
  355.4 3.1 collective-permute-done.52.incoming
  358.5 5.8 %section_backward.41 = (bf16[192,9216]{1,0:T(8,128)(2,1)}, f32[192,256]{1,0:T(8,128)}, f32[192,256]{1,0:T(8,128)}, bf16[192,9216]{1,0:T(8,128)(2,1)}, bf16[192,9...) custom-call(s32[40,6]{1,0:T(8,128)S(1)} %copy.388.table, ...), custom_call_target="tpu_custom_call", output_to_operand_aliasing={{0}: (7, {}), {1}: (8, {}), {2}: (9, {}), {3}: (10, {}), {4... | custom-call | flops 150000000 | bytes 9000000 | tf_op jit(solution)/shard_map/section_backward/pallas_call | solution.py:288
  367.6 5.4 %section_backward.42 = (bf16[192,9216]{1,0:T(8,128)(2,1)}, f32[192,256]{1,0:T(8,128)}, f32[192,256]{1,0:T(8,128)}, bf16[192,9216]{1,0:T(8,128)(2,1)}, bf16[192,9...) custom-call(s32[40,6]{1,0:T(8,128)S(1)} %copy.388.table, ...), custom_call_target="tpu_custom_call", output_to_operand_aliasing={{0}: (7, {}), {1}: (8, {}), {2}: (9, {}), {3}: (10, {}), {4... | custom-call | flops 150000000 | bytes 9000000 | tf_op jit(solution)/shard_map/section_backward/pallas_call | solution.py:288
  375.0 5.4 %section_backward.43 = (bf16[192,9216]{1,0:T(8,128)(2,1)}, f32[192,256]{1,0:T(8,128)}, f32[192,256]{1,0:T(8,128)}, bf16[192,9216]{1,0:T(8,128)(2,1)}, bf16[192,9...) custom-call(s32[40,6]{1,0:T(8,128)S(1)} %copy.388.table, ...), custom_call_target="tpu_custom_call", output_to_operand_aliasing={{0}: (7, {}), {1}: (8, {}), {2}: (9, {}), {3}: (10, {}), {4... | custom-call | flops 150000000 | bytes 9000000 | tf_op jit(solution)/shard_map/section_backward/pallas_call | solution.py:288
  383.3 5.4 %section_backward.44 = (bf16[192,9216]{1,0:T(8,128)(2,1)}, f32[192,256]{1,0:T(8,128)}, f32[192,256]{1,0:T(8,128)}, bf16[192,9216]{1,0:T(8,128)(2,1)}, bf16[192,9...) custom-call(s32[40,6]{1,0:T(8,128)S(1)} %copy.388.table, ...), custom_call_target="tpu_custom_call", output_to_operand_aliasing={{0}: (7, {}), {1}: (8, {}), {2}: (9, {}), {3}: (10, {}), {4... | custom-call | flops 150000000 | bytes 9000000 | tf_op jit(solution)/shard_map/section_backward/pallas_call | solution.py:288
  392.3 5.4 %section_backward.45 = (bf16[192,9216]{1,0:T(8,128)(2,1)}, f32[192,256]{1,0:T(8,128)}, f32[192,256]{1,0:T(8,128)}, bf16[192,9216]{1,0:T(8,128)(2,1)}, bf16[192,9...) custom-call(s32[40,6]{1,0:T(8,128)S(1)} %copy.388.table, ...), custom_call_target="tpu_custom_call", output_to_operand_aliasing={{0}: (7, {}), {1}: (8, {}), {2}: (9, {}), {3}: (10, {}), {4... | custom-call | flops 150000000 | bytes 9000000 | tf_op jit(solution)/shard_map/section_backward/pallas_call | solution.py:288
  401.1 5.4 %section_backward.46 = (bf16[192,9216]{1,0:T(8,128)(2,1)}, f32[192,256]{1,0:T(8,128)}, f32[192,256]{1,0:T(8,128)}, bf16[192,9216]{1,0:T(8,128)(2,1)}, bf16[192,9...) custom-call(s32[40,6]{1,0:T(8,128)S(1)} %copy.388.table, ...), custom_call_target="tpu_custom_call", output_to_operand_aliasing={{0}: (7, {}), {1}: (8, {}), {2}: (9, {}), {3}: (10, {}), {4... | custom-call | flops 150000000 | bytes 9000000 | tf_op jit(solution)/shard_map/section_backward/pallas_call | solution.py:288
  408.5 5.6 %section_backward.47 = (bf16[192,9216]{1,0:T(8,128)(2,1)}, f32[192,256]{1,0:T(8,128)}, f32[192,256]{1,0:T(8,128)}, bf16[192,9216]{1,0:T(8,128)(2,1)}, bf16[192,9...) custom-call(s32[40,6]{1,0:T(8,128)S(1)} %copy.388.table, ...), custom_call_target="tpu_custom_call", output_to_operand_aliasing={{0}: (7, {}), {1}: (8, {}), {2}: (9, {}), {3}: (10, {}), {4... | custom-call | flops 150000000 | bytes 9000000 | tf_op jit(solution)/shard_map/section_backward/pallas_call | solution.py:288
  415.4 2.8 collective-permute-done.61.incoming
  418.2 5.4 %section_backward.48 = (bf16[192,9216]{1,0:T(8,128)(2,1)}, f32[192,256]{1,0:T(8,128)}, f32[192,256]{1,0:T(8,128)}, bf16[192,9216]{1,0:T(8,128)(2,1)}, bf16[192,9...) custom-call(s32[40,6]{1,0:T(8,128)S(1)} %copy.388.table, ...), custom_call_target="tpu_custom_call", output_to_operand_aliasing={{0}: (7, {}), {1}: (8, {}), {2}: (9, {}), {3}: (10, {}), {4... | custom-call | flops 150000000 | bytes 9000000 | tf_op jit(solution)/shard_map/section_backward/pallas_call | solution.py:288
  425.0 5.5 %section_backward.49 = (bf16[192,9216]{1,0:T(8,128)(2,1)}, f32[192,256]{1,0:T(8,128)}, f32[192,256]{1,0:T(8,128)}, bf16[192,9216]{1,0:T(8,128)(2,1)}, bf16[192,9...) custom-call(s32[40,6]{1,0:T(8,128)S(1)} %copy.388.table, ...), custom_call_target="tpu_custom_call", output_to_operand_aliasing={{0}: (7, {}), {1}: (8, {}), {2}: (9, {}), {3}: (10, {}), {4... | custom-call | flops 150000000 | bytes 9000000 | tf_op jit(solution)/shard_map/section_backward/pallas_call | solution.py:288
  431.9 13.0 %collective-permute-done.63.incoming = bf16[16,9216]{1,0:T(8,128)(2,1)S(1)} collective-permute-done((bf16[16,9216]{1,0:T(8,128)(2,1)S(1)}, bf16[16,9216]{1,0:T(8,128)(2,1)S(1)}, u32[]{:S(2)}, u32[]{:S(2)}) %collective-permute-start.63) | collective-permute-done | bytes 294944 | tf_op jit(solution)/shard_map/ppermute | solution.py:581
  444.9 2.3 copy-done.1
  447.2 2.3 copy-done.3
  449.6 6.1 %section_backward.50 = (bf16[192,9216]{1,0:T(8,128)(2,1)}, f32[192,256]{1,0:T(8,128)}, f32[192,256]{1,0:T(8,128)}, bf16[192,9216]{1,0:T(8,128)(2,1)}, bf16[192,9...) custom-call(s32[40,6]{1,0:T(8,128)S(1)} %copy.388.table, ...), custom_call_target="tpu_custom_call", output_to_operand_aliasing={{0}: (7, {}), {1}: (8, {}), {2}: (9, {}), {3}: (10, {}), {4... | custom-call | flops 150000000 | bytes 9000000 | tf_op jit(solution)/shard_map/section_backward/pallas_call | solution.py:288
  455.8 6.2 %section_backward.51 = (bf16[192,9216]{1,0:T(8,128)(2,1)}, f32[192,256]{1,0:T(8,128)}, f32[192,256]{1,0:T(8,128)}, bf16[192,9216]{1,0:T(8,128)(2,1)}, bf16[192,9...) custom-call(s32[40,6]{1,0:T(8,128)S(1)} %copy.388.table, ...), custom_call_target="tpu_custom_call", output_to_operand_aliasing={{0}: (7, {}), {1}: (8, {}), {2}: (9, {}), {3}: (10, {}), {4... | custom-call | flops 150000000 | bytes 9000000 | tf_op jit(solution)/shard_map/section_backward/pallas_call | solution.py:288
  462.8 4.9 gradient_blocks.3
  467.8 4.9 gradient_blocks.2
  474.0 6.4 %collective-permute-start.71 = (bf16[1168,256]{1,0:T(8,128)(2,1)S(1)}, bf16[1168,256]{1,0:T(8,128)(2,1)S(1)}, u32[]{:S(2)}, u32[]{:S(2)}) collective-permute-start(bf16[1168,256]{1,0:T(8,128)(2,1)S(1)} %get-tuple-element.820), channel_id=1, source_target_pairs={{0,12},{1,13},{2,14},{3,15},{4,0},{5,1},{6,2},{7,3},{8,4},{9,5},{1... | collective-permute-start | bytes 1794056 | tf_op jit(solution)/shard_map/ppermute | solution.py:373
  482.1 3.2 collective-permute-start.67
  485.3 8.9 %collective-permute-done.71 = bf16[1168,256]{1,0:T(8,128)(2,1)S(1)} collective-permute-done((bf16[1168,256]{1,0:T(8,128)(2,1)S(1)}, bf16[1168,256]{1,0:T(8,128)(2,1)S(1)}, u32[]{:S(2)}, u32[]{:S(2)}) %collective-permute-start.71) | collective-permute-done | bytes 598048 | tf_op jit(solution)/shard_map/ppermute | solution.py:373
  494.2 3.7 collective-permute-done.70
  500.6 21.8 %collective-permute-done.66 = bf16[1168,256]{1,0:T(8,128)(2,1)} collective-permute-done((bf16[1168,256]{1,0:T(8,128)(2,1)S(1)}, bf16[1168,256]{1,0:T(8,128)(2,1)}, u32[]{:S(2)}, u32[]{:S(2)}) %collective-permute-start.66) | collective-permute-done | bytes 598048 | tf_op jit(solution)/shard_map/ppermute | solution.py:373
  (189 shorter events, 118.6 us)
Async XLA Ops:
  4.0 17.9 %collective-permute-start.1 = (bf16[1168,256]{1,0:T(8,128)(2,1)S(1)}, bf16[1168,256]{1,0:T(8,128)(2,1)S(1)}, u32[]{:S(2)}, u32[]{:S(2)}) collective-permute-start(bf16[1168,256]{1,0:T(8,128)(2,1)S(1)} %fusion.7.refs_0_), channel_id=1, source_target_pairs={{0,2},{1,3},{2,0},{3,1},{4,6},{5,7},{6,4},{7,5},{8,10},{9,11},{10,... | collective-permute-start | bytes 1794056 | tf_op jit(solution)/shard_map/ppermute | solution.py:369
  8.1 18.9 %collective-permute-start.8 = (bf16[1168,256]{1,0:T(8,128)(2,1)S(1)}, bf16[1168,256]{1,0:T(8,128)(2,1)S(1)}, u32[]{:S(2)}, u32[]{:S(2)}) collective-permute-start(bf16[1168,256]{1,0:T(8,128)(2,1)S(1)} %fusion.7.refs_0_), channel_id=1, source_target_pairs={{0,8},{1,9},{2,10},{3,11},{4,12},{5,13},{6,14},{7,15},{8,0},{9,1},... | collective-permute-start | bytes 1794056 | tf_op jit(solution)/shard_map/ppermute | solution.py:373
  11.3 26.4 %collective-permute-start.6 = (bf16[1168,256]{1,0:T(8,128)(2,1)S(1)}, bf16[1168,256]{1,0:T(8,128)(2,1)S(1)}, u32[]{:S(2)}, u32[]{:S(2)}) collective-permute-start(bf16[1168,256]{1,0:T(8,128)(2,1)S(1)} %fusion.7.refs_0_), channel_id=1, source_target_pairs={{0,4},{1,5},{2,6},{3,7},{4,8},{5,9},{6,10},{7,11},{8,12},{9,13},{1... | collective-permute-start | bytes 1794056 | tf_op jit(solution)/shard_map/ppermute | solution.py:373
  11.9 26.2 %collective-permute-start.4 = (bf16[1168,256]{1,0:T(8,128)(2,1)S(1)}, bf16[1168,256]{1,0:T(8,128)(2,1)}, u32[]{:S(2)}, u32[]{:S(2)}) collective-permute-start(bf16[1168,256]{1,0:T(8,128)(2,1)S(1)} %fusion.7.refs_0_), channel_id=1, source_target_pairs={{0,12},{1,13},{2,14},{3,15},{4,0},{5,1},{6,2},{7,3},{8,4},{9,5},{1... | collective-permute-start | bytes 1794056 | tf_op jit(solution)/shard_map/ppermute | solution.py:373
  14.5 24.9 %collective-permute-start.2 = (bf16[1168,256]{1,0:T(8,128)(2,1)S(1)}, bf16[1168,256]{1,0:T(8,128)(2,1)}, u32[]{:S(2)}, u32[]{:S(2)}) collective-permute-start(bf16[1168,256]{1,0:T(8,128)(2,1)S(1)} %fusion.7.refs_0_), channel_id=1, source_target_pairs={{0,1},{1,0},{2,3},{3,2},{4,5},{5,4},{6,7},{7,6},{8,9},{9,8},{10,11... | collective-permute-start | bytes 1794056 | tf_op jit(solution)/shard_map/ppermute | solution.py:365
  27.0 16.8 %collective-permute-start.10 = (bf16[1168,256]{1,0:T(8,128)(2,1)S(1)}, bf16[1168,256]{1,0:T(8,128)(2,1)}, u32[]{:S(2)}, u32[]{:S(2)}) collective-permute-start(bf16[1168,256]{1,0:T(8,128)(2,1)S(1)} %collective-permute-done.8.refs_8_), channel_id=1, source_target_pairs={{0,2},{1,3},{2,0},{3,1},{4,6},{5,7},{6,4},{7,5},{8,10},{9,11},{10,... | collective-permute-start | bytes 1794056 | tf_op jit(solution)/shard_map/ppermute | solution.py:369
  30.3 13.4 %collective-permute-start.9 = (bf16[1168,256]{1,0:T(8,128)(2,1)S(1)}, bf16[1168,256]{1,0:T(8,128)(2,1)S(1)}, u32[]{:S(2)}, u32[]{:S(2)}) collective-permute-start(bf16[1168,256]{1,0:T(8,128)(2,1)S(1)} %collective-permute-done.8.refs_8_), channel_id=1, source_target_pairs={{0,1},{1,0},{2,3},{3,2},{4,5},{5,4},{6,7},{7,6},{8,9},{9,8},{10,11... | collective-permute-start | bytes 1794056 | tf_op jit(solution)/shard_map/ppermute | solution.py:365
  38.2 16.7 %collective-permute-start.14 = (bf16[1168,256]{1,0:T(8,128)(2,1)S(1)}, bf16[1168,256]{1,0:T(8,128)(2,1)}, u32[]{:S(2)}, u32[]{:S(2)}) collective-permute-start(bf16[1168,256]{1,0:T(8,128)(2,1)S(1)} %collective-permute-done.1.refs_2_), channel_id=1, source_target_pairs={{0,4},{1,5},{2,6},{3,7},{4,8},{5,9},{6,10},{7,11},{8,12},{9,13},{1... | collective-permute-start | bytes 1794056 | tf_op jit(solution)/shard_map/ppermute | solution.py:373
  39.4 15.7 %collective-permute-start.12 = (bf16[1168,256]{1,0:T(8,128)(2,1)S(1)}, bf16[1168,256]{1,0:T(8,128)(2,1)}, u32[]{:S(2)}, u32[]{:S(2)}) collective-permute-start(bf16[1168,256]{1,0:T(8,128)(2,1)S(1)} %collective-permute-done.1.refs_2_), channel_id=1, source_target_pairs={{0,12},{1,13},{2,14},{3,15},{4,0},{5,1},{6,2},{7,3},{8,4},{9,5},{1... | collective-permute-start | bytes 1794056 | tf_op jit(solution)/shard_map/ppermute | solution.py:373
  43.8 11.9 %collective-permute-start.3 = (bf16[1168,256]{1,0:T(8,128)(2,1)S(1)}, bf16[1168,256]{1,0:T(8,128)(2,1)}, u32[]{:S(2)}, u32[]{:S(2)}) collective-permute-start(bf16[1168,256]{1,0:T(8,128)(2,1)S(1)} %collective-permute-done.1.refs_2_), channel_id=1, source_target_pairs={{0,1},{1,0},{2,3},{3,2},{4,5},{5,4},{6,7},{7,6},{8,9},{9,8},{10,11... | collective-permute-start | bytes 1794056 | tf_op jit(solution)/shard_map/ppermute | solution.py:365
  44.6 11.0 %collective-permute-start.5 = (bf16[1168,256]{1,0:T(8,128)(2,1)}, bf16[1168,256]{1,0:T(8,128)(2,1)}, u32[]{:S(2)}, u32[]{:S(2)}) collective-permute-start(bf16[1168,256]{1,0:T(8,128)(2,1)} %collective-permute-done.4.refs_4_), channel_id=1, source_target_pairs={{0,1},{1,0},{2,3},{3,2},{4,5},{5,4},{6,7},{7,6},{8,9},{9,8},{10,11... | collective-permute-start | bytes 1794056 | tf_op jit(solution)/shard_map/ppermute | solution.py:365
  46.0 9.7 %collective-permute-start.11 = (bf16[1168,256]{1,0:T(8,128)(2,1)}, bf16[1168,256]{1,0:T(8,128)(2,1)}, u32[]{:S(2)}, u32[]{:S(2)}) collective-permute-start(bf16[1168,256]{1,0:T(8,128)(2,1)} %collective-permute-done.10.refs_10_), channel_id=1, source_target_pairs={{0,1},{1,0},{2,3},{3,2},{4,5},{5,4},{6,7},{7,6},{8,9},{9,8},{10,11... | collective-permute-start | bytes 1794056 | tf_op jit(solution)/shard_map/ppermute | solution.py:365
  76.1 11.8 %collective-permute-start.16 = (bf16[16,9216]{1,0:T(8,128)(2,1)S(1)}, bf16[16,9216]{1,0:T(8,128)(2,1)S(1)}, u32[]{:S(2)}, u32[]{:S(2)}) collective-permute-start(bf16[16,9216]{1,0:T(8,128)(2,1)S(1)} %get-tuple-element.434), channel_id=1, source_target_pairs={{0,16},{16,32},{32,48},{48,64},{64,80},{80,96},{96,112},{1,17},{17... | collective-permute-start | bytes 884744 | tf_op jit(solution)/shard_map/ppermute | solution.py:567
  83.5 11.9 %collective-permute-start.19 = (bf16[16,9216]{1,0:T(8,128)(2,1)S(1)}, bf16[16,9216]{1,0:T(8,128)(2,1)S(1)}, u32[]{:S(2)}, u32[]{:S(2)}) collective-permute-start(bf16[16,9216]{1,0:T(8,128)(2,1)S(1)} %get-tuple-element.449), channel_id=1, source_target_pairs={{0,16},{16,32},{32,48},{48,64},{64,80},{80,96},{96,112},{1,17},{17... | collective-permute-start | bytes 884744 | tf_op jit(solution)/shard_map/ppermute | solution.py:567
  93.5 10.5 %collective-permute-start.18 = (bf16[16,9216]{1,0:T(8,128)(2,1)S(1)}, bf16[16,9216]{1,0:T(8,128)(2,1)S(1)}, u32[]{:S(2)}, u32[]{:S(2)}) collective-permute-start(bf16[16,9216]{1,0:T(8,128)(2,1)S(1)} %get-tuple-element.448), channel_id=1, source_target_pairs={{0,16},{16,32},{32,48},{48,64},{64,80},{80,96},{96,112},{1,17},{17... | collective-permute-start | bytes 884744 | tf_op jit(solution)/shard_map/ppermute | solution.py:567
  101.0 10.8 %collective-permute-start.21 = (bf16[16,9216]{1,0:T(8,128)(2,1)S(1)}, bf16[16,9216]{1,0:T(8,128)(2,1)S(1)}, u32[]{:S(2)}, u32[]{:S(2)}) collective-permute-start(bf16[16,9216]{1,0:T(8,128)(2,1)S(1)} %get-tuple-element.463), channel_id=1, source_target_pairs={{0,16},{16,32},{32,48},{48,64},{64,80},{80,96},{96,112},{1,17},{17... | collective-permute-start | bytes 884744 | tf_op jit(solution)/shard_map/ppermute | solution.py:567
  109.6 9.7 %collective-permute-start.20 = (bf16[16,9216]{1,0:T(8,128)(2,1)S(1)}, bf16[16,9216]{1,0:T(8,128)(2,1)S(1)}, u32[]{:S(2)}, u32[]{:S(2)}) collective-permute-start(bf16[16,9216]{1,0:T(8,128)(2,1)S(1)} %get-tuple-element.462), channel_id=1, source_target_pairs={{0,16},{16,32},{32,48},{48,64},{64,80},{80,96},{96,112},{1,17},{17... | collective-permute-start | bytes 884744 | tf_op jit(solution)/shard_map/ppermute | solution.py:567
  117.3 10.1 %collective-permute-start.23 = (bf16[16,9216]{1,0:T(8,128)(2,1)S(1)}, bf16[16,9216]{1,0:T(8,128)(2,1)S(1)}, u32[]{:S(2)}, u32[]{:S(2)}) collective-permute-start(bf16[16,9216]{1,0:T(8,128)(2,1)S(1)} %get-tuple-element.477), channel_id=1, source_target_pairs={{0,16},{16,32},{32,48},{48,64},{64,80},{80,96},{96,112},{1,17},{17... | collective-permute-start | bytes 884744 | tf_op jit(solution)/shard_map/ppermute | solution.py:567
  125.0 10.2 %collective-permute-start.22 = (bf16[16,9216]{1,0:T(8,128)(2,1)S(1)}, bf16[16,9216]{1,0:T(8,128)(2,1)S(1)}, u32[]{:S(2)}, u32[]{:S(2)}) collective-permute-start(bf16[16,9216]{1,0:T(8,128)(2,1)S(1)} %get-tuple-element.476), channel_id=1, source_target_pairs={{0,16},{16,32},{32,48},{48,64},{64,80},{80,96},{96,112},{1,17},{17... | collective-permute-start | bytes 884744 | tf_op jit(solution)/shard_map/ppermute | solution.py:567
  148.2 11.5 %collective-permute-start.27 = (bf16[16,9216]{1,0:T(8,128)(2,1)S(1)}, bf16[16,9216]{1,0:T(8,128)(2,1)S(1)}, u32[]{:S(2)}, u32[]{:S(2)}) collective-permute-start(bf16[16,9216]{1,0:T(8,128)(2,1)S(1)} %get-tuple-element.505), channel_id=1, source_target_pairs={{0,16},{16,32},{32,48},{48,64},{64,80},{80,96},{96,112},{1,17},{17... | collective-permute-start | bytes 884744 | tf_op jit(solution)/shard_map/ppermute | solution.py:567
  155.7 11.9 %collective-permute-start.26 = (bf16[16,9216]{1,0:T(8,128)(2,1)S(1)}, bf16[16,9216]{1,0:T(8,128)(2,1)S(1)}, u32[]{:S(2)}, u32[]{:S(2)}) collective-permute-start(bf16[16,9216]{1,0:T(8,128)(2,1)S(1)} %get-tuple-element.504), channel_id=1, source_target_pairs={{0,16},{16,32},{32,48},{48,64},{64,80},{80,96},{96,112},{1,17},{17... | collective-permute-start | bytes 884744 | tf_op jit(solution)/shard_map/ppermute | solution.py:567
  161.0 15.3 %collective-permute-start.29 = (bf16[16,9216]{1,0:T(8,128)(2,1)S(1)}, bf16[16,9216]{1,0:T(8,128)(2,1)S(1)}, u32[]{:S(2)}, u32[]{:S(2)}) collective-permute-start(bf16[16,9216]{1,0:T(8,128)(2,1)S(1)} %get-tuple-element.520), channel_id=1, source_target_pairs={{0,16},{16,32},{32,48},{48,64},{64,80},{80,96},{96,112},{1,17},{17... | collective-permute-start | bytes 884744 | tf_op jit(solution)/shard_map/ppermute | solution.py:567
  168.6 13.4 %collective-permute-start.28 = (bf16[16,9216]{1,0:T(8,128)(2,1)S(1)}, bf16[16,9216]{1,0:T(8,128)(2,1)S(1)}, u32[]{:S(2)}, u32[]{:S(2)}) collective-permute-start(bf16[16,9216]{1,0:T(8,128)(2,1)S(1)} %get-tuple-element.518), channel_id=1, source_target_pairs={{0,16},{16,32},{32,48},{48,64},{64,80},{80,96},{96,112},{1,17},{17... | collective-permute-start | bytes 884744 | tf_op jit(solution)/shard_map/ppermute | solution.py:567
  177.3 16.5 %collective-permute-start.32 = (bf16[16,9216]{1,0:T(8,128)(2,1)S(1)}, bf16[16,9216]{1,0:T(8,128)(2,1)S(1)}, u32[]{:S(2)}, u32[]{:S(2)}) collective-permute-start(bf16[16,9216]{1,0:T(8,128)(2,1)S(1)} %get-tuple-element.541), channel_id=1, source_target_pairs={{0,16},{16,32},{32,48},{48,64},{64,80},{80,96},{96,112},{1,17},{17... | collective-permute-start | bytes 884744 | tf_op jit(solution)/shard_map/ppermute | solution.py:567
  180.4 23.4 %collective-permute-start.31 = (bf16[16,9216]{1,0:T(8,128)(2,1)S(1)}, bf16[16,9216]{1,0:T(8,128)(2,1)S(1)}, u32[]{:S(2)}, u32[]{:S(2)}) collective-permute-start(bf16[16,9216]{1,0:T(8,128)(2,1)S(1)} %get-tuple-element.540), channel_id=1, source_target_pairs={{16,0},{32,16},{48,32},{64,48},{80,64},{96,80},{112,96},{17,1},{33... | collective-permute-start | bytes 884744 | tf_op jit(solution)/shard_map/ppermute | solution.py:581
  182.9 23.2 %collective-permute-start.30 = (bf16[16,9216]{1,0:T(8,128)(2,1)S(1)}, bf16[16,9216]{1,0:T(8,128)(2,1)S(1)}, u32[]{:S(2)}, u32[]{:S(2)}) collective-permute-start(bf16[16,9216]{1,0:T(8,128)(2,1)S(1)} %get-tuple-element.539), channel_id=1, source_target_pairs={{0,16},{16,32},{32,48},{48,64},{64,80},{80,96},{96,112},{1,17},{17... | collective-permute-start | bytes 884744 | tf_op jit(solution)/shard_map/ppermute | solution.py:567
  192.4 19.3 %collective-permute-start.36 = (bf16[16,9216]{1,0:T(8,128)(2,1)S(1)}, bf16[16,9216]{1,0:T(8,128)(2,1)S(1)}, u32[]{:S(2)}, u32[]{:S(2)}) collective-permute-start(bf16[16,9216]{1,0:T(8,128)(2,1)S(1)} %get-tuple-element.571), channel_id=1, source_target_pairs={{16,0},{32,16},{48,32},{64,48},{80,64},{96,80},{112,96},{17,1},{33... | collective-permute-start | bytes 884744 | tf_op jit(solution)/shard_map/ppermute | solution.py:581
  194.7 19.3 %collective-permute-start.35 = (bf16[16,9216]{1,0:T(8,128)(2,1)S(1)}, bf16[16,9216]{1,0:T(8,128)(2,1)S(1)}, u32[]{:S(2)}, u32[]{:S(2)}) collective-permute-start(bf16[16,9216]{1,0:T(8,128)(2,1)S(1)} %get-tuple-element.570), channel_id=1, source_target_pairs={{0,16},{16,32},{32,48},{48,64},{64,80},{80,96},{96,112},{1,17},{17... | collective-permute-start | bytes 884744 | tf_op jit(solution)/shard_map/ppermute | solution.py:567
  204.9 19.5 %collective-permute-start.34 = (bf16[16,9216]{1,0:T(8,128)(2,1)S(1)}, bf16[16,9216]{1,0:T(8,128)(2,1)S(1)}, u32[]{:S(2)}, u32[]{:S(2)}) collective-permute-start(bf16[16,9216]{1,0:T(8,128)(2,1)S(1)} %get-tuple-element.569), channel_id=1, source_target_pairs={{16,0},{32,16},{48,32},{64,48},{80,64},{96,80},{112,96},{17,1},{33... | collective-permute-start | bytes 884744 | tf_op jit(solution)/shard_map/ppermute | solution.py:581
  207.2 19.7 %collective-permute-start.33 = (bf16[16,9216]{1,0:T(8,128)(2,1)S(1)}, bf16[16,9216]{1,0:T(8,128)(2,1)S(1)}, u32[]{:S(2)}, u32[]{:S(2)}) collective-permute-start(bf16[16,9216]{1,0:T(8,128)(2,1)S(1)} %get-tuple-element.568), channel_id=1, source_target_pairs={{0,16},{16,32},{32,48},{48,64},{64,80},{80,96},{96,112},{1,17},{17... | collective-permute-start | bytes 884744 | tf_op jit(solution)/shard_map/ppermute | solution.py:567
  212.8 26.3 %collective-permute-start.40 = (bf16[16,9216]{1,0:T(8,128)(2,1)S(1)}, bf16[16,9216]{1,0:T(8,128)(2,1)S(1)}, u32[]{:S(2)}, u32[]{:S(2)}) collective-permute-start(bf16[16,9216]{1,0:T(8,128)(2,1)S(1)} %get-tuple-element.601), channel_id=1, source_target_pairs={{16,0},{32,16},{48,32},{64,48},{80,64},{96,80},{112,96},{17,1},{33... | collective-permute-start | bytes 884744 | tf_op jit(solution)/shard_map/ppermute | solution.py:581
  215.0 26.3 %collective-permute-start.39 = (bf16[16,9216]{1,0:T(8,128)(2,1)S(1)}, bf16[16,9216]{1,0:T(8,128)(2,1)S(1)}, u32[]{:S(2)}, u32[]{:S(2)}) collective-permute-start(bf16[16,9216]{1,0:T(8,128)(2,1)S(1)} %get-tuple-element.600), channel_id=1, source_target_pairs={{0,16},{16,32},{32,48},{48,64},{64,80},{80,96},{96,112},{1,17},{17... | collective-permute-start | bytes 884744 | tf_op jit(solution)/shard_map/ppermute | solution.py:567
  225.5 23.5 %collective-permute-start.38 = (bf16[16,9216]{1,0:T(8,128)(2,1)S(1)}, bf16[16,9216]{1,0:T(8,128)(2,1)S(1)}, u32[]{:S(2)}, u32[]{:S(2)}) collective-permute-start(bf16[16,9216]{1,0:T(8,128)(2,1)S(1)} %get-tuple-element.599), channel_id=1, source_target_pairs={{16,0},{32,16},{48,32},{64,48},{80,64},{96,80},{112,96},{17,1},{33... | collective-permute-start | bytes 884744 | tf_op jit(solution)/shard_map/ppermute | solution.py:581
  227.8 23.5 %collective-permute-start.37 = (bf16[16,9216]{1,0:T(8,128)(2,1)S(1)}, bf16[16,9216]{1,0:T(8,128)(2,1)S(1)}, u32[]{:S(2)}, u32[]{:S(2)}) collective-permute-start(bf16[16,9216]{1,0:T(8,128)(2,1)S(1)} %get-tuple-element.598), channel_id=1, source_target_pairs={{0,16},{16,32},{32,48},{48,64},{64,80},{80,96},{96,112},{1,17},{17... | collective-permute-start | bytes 884744 | tf_op jit(solution)/shard_map/ppermute | solution.py:567
  240.1 23.5 %collective-permute-start.44 = (bf16[16,9216]{1,0:T(8,128)(2,1)S(1)}, bf16[16,9216]{1,0:T(8,128)(2,1)S(1)}, u32[]{:S(2)}, u32[]{:S(2)}) collective-permute-start(bf16[16,9216]{1,0:T(8,128)(2,1)S(1)} %get-tuple-element.631), channel_id=1, source_target_pairs={{16,0},{32,16},{48,32},{64,48},{80,64},{96,80},{112,96},{17,1},{33... | collective-permute-start | bytes 884744 | tf_op jit(solution)/shard_map/ppermute | solution.py:581
  242.4 23.9 %collective-permute-start.43 = (bf16[16,9216]{1,0:T(8,128)(2,1)S(1)}, bf16[16,9216]{1,0:T(8,128)(2,1)S(1)}, u32[]{:S(2)}, u32[]{:S(2)}) collective-permute-start(bf16[16,9216]{1,0:T(8,128)(2,1)S(1)} %get-tuple-element.630), channel_id=1, source_target_pairs={{0,16},{16,32},{32,48},{48,64},{64,80},{80,96},{96,112},{1,17},{17... | collective-permute-start | bytes 884744 | tf_op jit(solution)/shard_map/ppermute | solution.py:567
  250.0 28.5 %collective-permute-start.42 = (bf16[16,9216]{1,0:T(8,128)(2,1)S(1)}, bf16[16,9216]{1,0:T(8,128)(2,1)S(1)}, u32[]{:S(2)}, u32[]{:S(2)}) collective-permute-start(bf16[16,9216]{1,0:T(8,128)(2,1)S(1)} %get-tuple-element.629), channel_id=1, source_target_pairs={{16,0},{32,16},{48,32},{64,48},{80,64},{96,80},{112,96},{17,1},{33... | collective-permute-start | bytes 884744 | tf_op jit(solution)/shard_map/ppermute | solution.py:581
  252.3 28.5 %collective-permute-start.41 = (bf16[16,9216]{1,0:T(8,128)(2,1)S(1)}, bf16[16,9216]{1,0:T(8,128)(2,1)S(1)}, u32[]{:S(2)}, u32[]{:S(2)}) collective-permute-start(bf16[16,9216]{1,0:T(8,128)(2,1)S(1)} %get-tuple-element.628), channel_id=1, source_target_pairs={{0,16},{16,32},{32,48},{48,64},{64,80},{80,96},{96,112},{1,17},{17... | collective-permute-start | bytes 884744 | tf_op jit(solution)/shard_map/ppermute | solution.py:567
  265.0 23.5 %collective-permute-start.48 = (bf16[16,9216]{1,0:T(8,128)(2,1)S(1)}, bf16[16,9216]{1,0:T(8,128)(2,1)S(1)}, u32[]{:S(2)}, u32[]{:S(2)}) collective-permute-start(bf16[16,9216]{1,0:T(8,128)(2,1)S(1)} %get-tuple-element.661), channel_id=1, source_target_pairs={{16,0},{32,16},{48,32},{64,48},{80,64},{96,80},{112,96},{17,1},{33... | collective-permute-start | bytes 884744 | tf_op jit(solution)/shard_map/ppermute | solution.py:581
  267.3 23.5 %collective-permute-start.47 = (bf16[16,9216]{1,0:T(8,128)(2,1)S(1)}, bf16[16,9216]{1,0:T(8,128)(2,1)S(1)}, u32[]{:S(2)}, u32[]{:S(2)}) collective-permute-start(bf16[16,9216]{1,0:T(8,128)(2,1)S(1)} %get-tuple-element.660), channel_id=1, source_target_pairs={{0,16},{16,32},{32,48},{48,64},{64,80},{80,96},{96,112},{1,17},{17... | collective-permute-start | bytes 884744 | tf_op jit(solution)/shard_map/ppermute | solution.py:567
  279.5 13.0 %collective-permute-start.46 = (bf16[16,9216]{1,0:T(8,128)(2,1)S(1)}, bf16[16,9216]{1,0:T(8,128)(2,1)S(1)}, u32[]{:S(2)}, u32[]{:S(2)}) collective-permute-start(bf16[16,9216]{1,0:T(8,128)(2,1)S(1)} %get-tuple-element.659), channel_id=1, source_target_pairs={{16,0},{32,16},{48,32},{64,48},{80,64},{96,80},{112,96},{17,1},{33... | collective-permute-start | bytes 884744 | tf_op jit(solution)/shard_map/ppermute | solution.py:581
  281.8 13.2 %collective-permute-start.45 = (bf16[16,9216]{1,0:T(8,128)(2,1)S(1)}, bf16[16,9216]{1,0:T(8,128)(2,1)S(1)}, u32[]{:S(2)}, u32[]{:S(2)}) collective-permute-start(bf16[16,9216]{1,0:T(8,128)(2,1)S(1)} %get-tuple-element.658), channel_id=1, source_target_pairs={{0,16},{16,32},{32,48},{48,64},{64,80},{80,96},{96,112},{1,17},{17... | collective-permute-start | bytes 884744 | tf_op jit(solution)/shard_map/ppermute | solution.py:567
  289.5 16.7 %collective-permute-start.49 = (bf16[16,9216]{1,0:T(8,128)(2,1)S(1)}, bf16[16,9216]{1,0:T(8,128)(2,1)S(1)}, u32[]{:S(2)}, u32[]{:S(2)}) collective-permute-start(bf16[16,9216]{1,0:T(8,128)(2,1)S(1)} %get-tuple-element.689), channel_id=1, source_target_pairs={{16,0},{32,16},{48,32},{64,48},{80,64},{96,80},{112,96},{17,1},{33... | collective-permute-start | bytes 884744 | tf_op jit(solution)/shard_map/ppermute | solution.py:581
  293.7 17.4 %collective-permute-start.51 = (bf16[16,9216]{1,0:T(8,128)(2,1)S(1)}, bf16[16,9216]{1,0:T(8,128)(2,1)S(1)}, u32[]{:S(2)}, u32[]{:S(2)}) collective-permute-start(bf16[16,9216]{1,0:T(8,128)(2,1)S(1)} %get-tuple-element.698), channel_id=1, source_target_pairs={{16,0},{32,16},{48,32},{64,48},{80,64},{96,80},{112,96},{17,1},{33... | collective-permute-start | bytes 884744 | tf_op jit(solution)/shard_map/ppermute | solution.py:581
  307.3 24.4 %collective-permute-start.50 = (bf16[16,9216]{1,0:T(8,128)(2,1)S(1)}, bf16[16,9216]{1,0:T(8,128)(2,1)S(1)}, u32[]{:S(2)}, u32[]{:S(2)}) collective-permute-start(bf16[16,9216]{1,0:T(8,128)(2,1)S(1)} %get-tuple-element.697), channel_id=1, source_target_pairs={{16,0},{32,16},{48,32},{64,48},{80,64},{96,80},{112,96},{17,1},{33... | collective-permute-start | bytes 884744 | tf_op jit(solution)/shard_map/ppermute | solution.py:581
  312.1 36.6 %collective-permute-start.53 = (bf16[16,9216]{1,0:T(8,128)(2,1)S(1)}, bf16[16,9216]{1,0:T(8,128)(2,1)S(1)}, u32[]{:S(2)}, u32[]{:S(2)}) collective-permute-start(bf16[16,9216]{1,0:T(8,128)(2,1)S(1)} %get-tuple-element.714), channel_id=1, source_target_pairs={{16,0},{32,16},{48,32},{64,48},{80,64},{96,80},{112,96},{17,1},{33... | collective-permute-start | bytes 884744 | tf_op jit(solution)/shard_map/ppermute | solution.py:581
  332.7 25.8 %collective-permute-start.52 = (bf16[16,9216]{1,0:T(8,128)(2,1)S(1)}, bf16[16,9216]{1,0:T(8,128)(2,1)S(1)}, u32[]{:S(2)}, u32[]{:S(2)}) collective-permute-start(bf16[16,9216]{1,0:T(8,128)(2,1)S(1)} %get-tuple-element.713), channel_id=1, source_target_pairs={{16,0},{32,16},{48,32},{64,48},{80,64},{96,80},{112,96},{17,1},{33... | collective-permute-start | bytes 884744 | tf_op jit(solution)/shard_map/ppermute | solution.py:581
  354.1 13.5 %collective-permute-start.55 = (bf16[16,9216]{1,0:T(8,128)(2,1)S(1)}, bf16[16,9216]{1,0:T(8,128)(2,1)S(1)}, u32[]{:S(2)}, u32[]{:S(2)}) collective-permute-start(bf16[16,9216]{1,0:T(8,128)(2,1)S(1)} %get-tuple-element.730), channel_id=1, source_target_pairs={{16,0},{32,16},{48,32},{64,48},{80,64},{96,80},{112,96},{17,1},{33... | collective-permute-start | bytes 884744 | tf_op jit(solution)/shard_map/ppermute | solution.py:581
  364.3 10.7 %collective-permute-start.54 = (bf16[16,9216]{1,0:T(8,128)(2,1)S(1)}, bf16[16,9216]{1,0:T(8,128)(2,1)S(1)}, u32[]{:S(2)}, u32[]{:S(2)}) collective-permute-start(bf16[16,9216]{1,0:T(8,128)(2,1)S(1)} %get-tuple-element.729), channel_id=1, source_target_pairs={{16,0},{32,16},{48,32},{64,48},{80,64},{96,80},{112,96},{17,1},{33... | collective-permute-start | bytes 884744 | tf_op jit(solution)/shard_map/ppermute | solution.py:581
  373.1 10.2 %collective-permute-start.57 = (bf16[16,9216]{1,0:T(8,128)(2,1)S(1)}, bf16[16,9216]{1,0:T(8,128)(2,1)S(1)}, u32[]{:S(2)}, u32[]{:S(2)}) collective-permute-start(bf16[16,9216]{1,0:T(8,128)(2,1)S(1)} %get-tuple-element.746), channel_id=1, source_target_pairs={{16,0},{32,16},{48,32},{64,48},{80,64},{96,80},{112,96},{17,1},{33... | collective-permute-start | bytes 884744 | tf_op jit(solution)/shard_map/ppermute | solution.py:581
  380.5 11.8 %collective-permute-start.56 = (bf16[16,9216]{1,0:T(8,128)(2,1)S(1)}, bf16[16,9216]{1,0:T(8,128)(2,1)S(1)}, u32[]{:S(2)}, u32[]{:S(2)}) collective-permute-start(bf16[16,9216]{1,0:T(8,128)(2,1)S(1)} %get-tuple-element.745), channel_id=1, source_target_pairs={{16,0},{32,16},{48,32},{64,48},{80,64},{96,80},{112,96},{17,1},{33... | collective-permute-start | bytes 884744 | tf_op jit(solution)/shard_map/ppermute | solution.py:581
  388.8 12.3 %collective-permute-start.59 = (bf16[16,9216]{1,0:T(8,128)(2,1)S(1)}, bf16[16,9216]{1,0:T(8,128)(2,1)S(1)}, u32[]{:S(2)}, u32[]{:S(2)}) collective-permute-start(bf16[16,9216]{1,0:T(8,128)(2,1)S(1)} %get-tuple-element.762), channel_id=1, source_target_pairs={{16,0},{32,16},{48,32},{64,48},{80,64},{96,80},{112,96},{17,1},{33... | collective-permute-start | bytes 884744 | tf_op jit(solution)/shard_map/ppermute | solution.py:581
  397.7 10.8 %collective-permute-start.58 = (bf16[16,9216]{1,0:T(8,128)(2,1)S(1)}, bf16[16,9216]{1,0:T(8,128)(2,1)S(1)}, u32[]{:S(2)}, u32[]{:S(2)}) collective-permute-start(bf16[16,9216]{1,0:T(8,128)(2,1)S(1)} %get-tuple-element.761), channel_id=1, source_target_pairs={{16,0},{32,16},{48,32},{64,48},{80,64},{96,80},{112,96},{17,1},{33... | collective-permute-start | bytes 884744 | tf_op jit(solution)/shard_map/ppermute | solution.py:581
  406.5 11.7 %collective-permute-start.61 = (bf16[16,9216]{1,0:T(8,128)(2,1)S(1)}, bf16[16,9216]{1,0:T(8,128)(2,1)S(1)}, u32[]{:S(2)}, u32[]{:S(2)}) collective-permute-start(bf16[16,9216]{1,0:T(8,128)(2,1)S(1)} %get-tuple-element.778), channel_id=1, source_target_pairs={{16,0},{32,16},{48,32},{64,48},{80,64},{96,80},{112,96},{17,1},{33... | collective-permute-start | bytes 884744 | tf_op jit(solution)/shard_map/ppermute | solution.py:581
  414.1 10.9 %collective-permute-start.60 = (bf16[16,9216]{1,0:T(8,128)(2,1)S(1)}, bf16[16,9216]{1,0:T(8,128)(2,1)S(1)}, u32[]{:S(2)}, u32[]{:S(2)}) collective-permute-start(bf16[16,9216]{1,0:T(8,128)(2,1)S(1)} %get-tuple-element.777), channel_id=1, source_target_pairs={{16,0},{32,16},{48,32},{64,48},{80,64},{96,80},{112,96},{17,1},{33... | collective-permute-start | bytes 884744 | tf_op jit(solution)/shard_map/ppermute | solution.py:581
  423.7 21.2 %collective-permute-start.63 = (bf16[16,9216]{1,0:T(8,128)(2,1)S(1)}, bf16[16,9216]{1,0:T(8,128)(2,1)S(1)}, u32[]{:S(2)}, u32[]{:S(2)}) collective-permute-start(bf16[16,9216]{1,0:T(8,128)(2,1)S(1)} %get-tuple-element.794), channel_id=1, source_target_pairs={{16,0},{32,16},{48,32},{64,48},{80,64},{96,80},{112,96},{17,1},{33... | collective-permute-start | bytes 884744 | tf_op jit(solution)/shard_map/ppermute | solution.py:581
  430.5 25.3 %collective-permute-start.62 = (bf16[16,9216]{1,0:T(8,128)(2,1)S(1)}, bf16[16,9216]{1,0:T(8,128)(2,1)S(1)}, u32[]{:S(2)}, u32[]{:S(2)}) collective-permute-start(bf16[16,9216]{1,0:T(8,128)(2,1)S(1)} %get-tuple-element.793), channel_id=1, source_target_pairs={{16,0},{32,16},{48,32},{64,48},{80,64},{96,80},{112,96},{17,1},{33... | collective-permute-start | bytes 884744 | tf_op jit(solution)/shard_map/ppermute | solution.py:581
  474.0 20.2 %collective-permute-start.71 = (bf16[1168,256]{1,0:T(8,128)(2,1)S(1)}, bf16[1168,256]{1,0:T(8,128)(2,1)S(1)}, u32[]{:S(2)}, u32[]{:S(2)}) collective-permute-start(bf16[1168,256]{1,0:T(8,128)(2,1)S(1)} %get-tuple-element.820), channel_id=1, source_target_pairs={{0,12},{1,13},{2,14},{3,15},{4,0},{5,1},{6,2},{7,3},{8,4},{9,5},{1... | collective-permute-start | bytes 1794056 | tf_op jit(solution)/shard_map/ppermute | solution.py:373
  480.3 17.6 %collective-permute-start.70 = (bf16[1168,256]{1,0:T(8,128)(2,1)S(1)}, bf16[1168,256]{1,0:T(8,128)(2,1)S(1)}, u32[]{:S(2)}, u32[]{:S(2)}) collective-permute-start(bf16[1168,256]{1,0:T(8,128)(2,1)S(1)} %get-tuple-element.821), channel_id=1, source_target_pairs={{0,4},{1,5},{2,6},{3,7},{4,8},{5,9},{6,10},{7,11},{8,12},{9,13},{1... | collective-permute-start | bytes 1794056 | tf_op jit(solution)/shard_map/ppermute | solution.py:373
  480.3 17.6 %collective-permute-start.68 = (bf16[1168,256]{1,0:T(8,128)(2,1)S(1)}, bf16[1168,256]{1,0:T(8,128)(2,1)S(1)}, u32[]{:S(2)}, u32[]{:S(2)}) collective-permute-start(bf16[1168,256]{1,0:T(8,128)(2,1)S(1)} %get-tuple-element.822), channel_id=1, source_target_pairs={{0,2},{1,3},{2,0},{3,1},{4,6},{5,7},{6,4},{7,5},{8,10},{9,11},{10,... | collective-permute-start | bytes 1794056 | tf_op jit(solution)/shard_map/ppermute | solution.py:369
  480.7 41.7 %collective-permute-start.66 = (bf16[1168,256]{1,0:T(8,128)(2,1)S(1)}, bf16[1168,256]{1,0:T(8,128)(2,1)}, u32[]{:S(2)}, u32[]{:S(2)}) collective-permute-start(bf16[1168,256]{1,0:T(8,128)(2,1)S(1)} %get-tuple-element.819), channel_id=1, source_target_pairs={{0,4},{1,5},{2,6},{3,7},{4,8},{5,9},{6,10},{7,11},{8,12},{9,13},{1... | collective-permute-start | bytes 1794056 | tf_op jit(solution)/shard_map/ppermute | solution.py:373
  482.1 40.4 %collective-permute-start.67 = (bf16[1168,256]{1,0:T(8,128)(2,1)}, bf16[1168,256]{1,0:T(8,128)(2,1)}, u32[]{:S(2)}, u32[]{:S(2)}) collective-permute-start(bf16[1168,256]{1,0:T(8,128)(2,1)} %fusion.9), channel_id=1, source_target_pairs={{0,12},{1,13},{2,14},{3,15},{4,0},{5,1},{6,2},{7,3},{8,4},{9,5},{1... | collective-permute-start | bytes 1794056 | tf_op jit(solution)/shard_map/ppermute | solution.py:373
  499.7 22.8 %collective-permute-start.69 = (bf16[1168,256]{1,0:T(8,128)(2,1)}, bf16[1168,256]{1,0:T(8,128)(2,1)}, u32[]{:S(2)}, u32[]{:S(2)}) collective-permute-start(bf16[1168,256]{1,0:T(8,128)(2,1)} %get-tuple-element.823), channel_id=1, source_target_pairs={{0,8},{1,9},{2,10},{3,11},{4,12},{5,13},{6,14},{7,15},{8,0},{9,1},... | collective-permute-start | bytes 1794056 | tf_op jit(solution)/shard_map/ppermute | solution.py:373
  500.2 22.2 %collective-permute-start.72 = (bf16[1168,256]{1,0:T(8,128)(2,1)}, bf16[1168,256]{1,0:T(8,128)(2,1)}, u32[]{:S(2)}, u32[]{:S(2)}) collective-permute-start(bf16[1168,256]{1,0:T(8,128)(2,1)} %get-tuple-element.824), channel_id=1, source_target_pairs={{0,2},{1,3},{2,0},{3,1},{4,6},{5,7},{6,4},{7,5},{8,10},{9,11},{10,... | collective-permute-start | bytes 1794056 | tf_op jit(solution)/shard_map/ppermute | solution.py:369
  (23 other events, 834.9 us)
